TPU v7x, 32 devices: a whole 2x2x4 slice. The times are simulated.
32 devices in a mesh: seq: 4 (over z), fsdp: 8 (over y, x, core).
Axes of the slice: x: 2, y: 2, z: 4, core: 2. Of those that a mesh axis runs over, the one named last changes fastest.
Arguments:
- frames: bfloat16 [8, 1024, 1536], P('fsdp', 'seq'), may hold values from -6 to 6
- conv_kernel: float32 [31, 1536], replicated, may hold values from -1 to 1
- pw_weight: bfloat16 [1536, 1536], P('fsdp'), may hold values from -0.15625 to 0.15625
- head_weight: bfloat16 [1536, 8192], P(None, 'fsdp'), may hold values from -4.5 to 4.5
- targets: int32 [8, 1024], P('fsdp', 'seq'), may hold values from 0 to 8191
- frame_weight: bfloat16 [8, 1024], P('fsdp', 'seq'), may hold values from 0.19921875 to 1
Outputs:
- frames_grad: bfloat16 [8, 1024, 1536], P('fsdp', 'seq')
- kernel_grad: float32 [31, 1536], replicated
- pw_grad: float32 [1536, 1536], P(('seq', 'fsdp'))
- head_grad: float32 [1536, 8192], P('seq', 'fsdp')
All inputs are finite; a program needn't handle non-finite values.
Results may differ from a plain program's by a relative error of at most 0.014.
The roundings to bfloat16 on the way count: a program that leaves them out, or rounds other values in their place, can miss the bound.
Values may be sent and summed in bfloat16 or wider, within the bound.
No kernel may reach another device: no remote copies, remote signals or barrier semaphores. Data moves between devices by JAX's collectives and lax.ppermute only.
A program may use at most 128 MiB of HBM per device.

v0:
```python
import jax
import jax.numpy as jnp
from jax import lax
from jax.sharding import PartitionSpec as P


def with_halo(block, sides, width):
    for axis, dim in sides:
        count = lax.axis_size(axis)
        forward = [(i, i + 1) for i in range(count - 1)]
        backward = [(target, source) for source, target in forward]
        low = lax.ppermute(
            lax.slice_in_dim(block, block.shape[dim] - width, None, axis=dim), axis, forward
        )
        high = lax.ppermute(lax.slice_in_dim(block, 0, width, axis=dim), axis, backward)
        block = jnp.concatenate([low, block, high], axis=dim)
    return block


def joined(value, axis, join):
    pieces = jax.tree.map(lambda part: lax.all_gather(part, axis), value)
    head = jax.tree.map(lambda part: part[0], pieces)
    tail = jax.tree.map(lambda part: part[1:], pieces)
    total, _ = lax.scan(lambda total, section: (join(total, section), None), head, tail)
    return total


def body(frames, conv_kernel, pw_weight, head_weight, targets, frame_weight):
    rows = frames.shape[1]
    width = frames.shape[2]
    taps = conv_kernel.shape[0]
    reach = (taps - 1) // 2
    padded = with_halo(frames, (("seq", 1),), reach)[0]
    conv = jnp.zeros((rows, width), jnp.float32)
    for tap in range(taps):
        conv = conv + conv_kernel[tap] * padded[tap : tap + rows].astype(jnp.float32)
    gated = jax.nn.silu(conv).astype(jnp.bfloat16)
    pw_full = lax.all_gather(pw_weight, "fsdp", axis=0, tiled=True)
    proj = jnp.dot(gated, pw_full, preferred_element_type=jnp.float32)
    mixed = (frames[0].astype(jnp.float32) + proj).astype(jnp.bfloat16)
    all_mixed, all_targets, all_weights = (
        lax.all_gather(mixed, "fsdp", axis=0, tiled=True),
        lax.all_gather(targets[0], "fsdp", axis=0, tiled=True),
        lax.all_gather(frame_weight[0], "fsdp", axis=0, tiled=True),
    )
    logits = jnp.dot(all_mixed, head_weight, preferred_element_type=jnp.float32)
    vocab_local = head_weight.shape[1]
    offset = lax.axis_index("fsdp") * vocab_local
    local_top = jnp.max(logits, axis=1)
    local_total = jnp.sum(jnp.exp(logits - local_top[:, None]), axis=1)

    def combine(first, second):
        upper = jnp.maximum(first[0], second[0])
        return (
            upper,
            first[1] * jnp.exp(first[0] - upper) + second[1] * jnp.exp(second[0] - upper),
        )

    top, total = joined((local_top, local_total), "fsdp", combine)
    probs = jnp.exp(logits - top[:, None]) / total[:, None]
    entries = lax.broadcasted_iota(jnp.int32, (1, vocab_local), 1)
    hit = (all_targets[:, None] - offset == entries).astype(jnp.float32)
    dlogits = (all_weights.astype(jnp.float32)[:, None] * (probs - hit)).astype(jnp.bfloat16)
    head_term = lax.dot_general(
        all_mixed, dlogits, (((0,), (0,)), ((), ())), preferred_element_type=jnp.float32
    )
    head_grad = lax.psum_scatter(
        head_term.astype(jnp.bfloat16), "seq", scatter_dimension=0, tiled=True
    ).astype(jnp.float32)
    dmixed = lax.psum_scatter(
        lax.dot_general(
            dlogits, head_weight, (((1,), (1,)), ((), ())), preferred_element_type=jnp.float32
        ).astype(jnp.bfloat16),
        "fsdp",
        scatter_dimension=0,
        tiled=True,
    )
    pw_grad = lax.psum_scatter(
        lax.dot_general(
            gated, dmixed, (((0,), (0,)), ((), ())), preferred_element_type=jnp.float32
        ),
        ("seq", "fsdp"),
        scatter_dimension=0,
        tiled=True,
    )
    dgated = lax.dot_general(
        dmixed, pw_full, (((1,), (1,)), ((), ())), preferred_element_type=jnp.float32
    )
    sig = jax.nn.sigmoid(conv)
    dconv = (dgated * sig * (1.0 + conv * (1.0 - sig))).astype(jnp.bfloat16)
    dpad = with_halo(dconv[None], (("seq", 1),), reach)[0]
    dconv_f = dconv.astype(jnp.float32)
    back = dmixed.astype(jnp.float32)
    kernel_rows = []
    for tap in range(taps):
        kernel_rows.append(jnp.sum(dconv_f * padded[tap : tap + rows].astype(jnp.float32), axis=0))
        back = back + conv_kernel[tap] * dpad[2 * reach - tap : 2 * reach - tap + rows].astype(
            jnp.float32
        )
    kernel_term = jnp.stack(kernel_rows, axis=0)
    kernel_grad = lax.psum(kernel_term, ("seq", "fsdp"))
    return (back.astype(jnp.bfloat16)[None], kernel_grad, pw_grad, head_grad)


def solution(mesh):
    return jax.shard_map(
        body,
        mesh=mesh,
        in_specs=(
            P("fsdp", "seq", None),
            P(),
            P("fsdp", None),
            P(None, "fsdp"),
            P("fsdp", "seq"),
            P("fsdp", "seq"),
        ),
        out_specs=(P("fsdp", "seq", None), P(), P(("seq", "fsdp"), None), P("seq", "fsdp")),
        check_vma=False,
    )
```

profile of v0, /device:TPU:0, one launch (start us, length us, event | category | flops | bytes accessed | tf_op | source)
XLA Modules:
  0.0 554.9 jit_solution(13179139525917075057)
XLA Ops:
  8.0 1.0 fusion.186
  9.0 4.9 collective-permute-start
  13.9 1.3 collective-permute-start.1
  15.2 1.8 slice_reduce_fusion.30
  17.1 1.2 constant_dynamic-update-slice_fusion.1
  18.3 1.6 slice_reduce_fusion.29
  20.9 7.2 %fusion.32 = f32[256,1536]{1,0:T(8,128)} fusion(bf16[1,256,1536]{2,1,0:T(8,128)(2,1)S(1)} %copy-done.6, f32[1536]{0:T(1024)S(1)} %get-tuple-element.94, f32[1536]{0:T(1024)S(1)} %get-tuple-element.95, f32[1536]{0:T(1024)S(1)} %get-tuple-element.66, f32[1536]{0:T(1024)S(1)} %get-tuple-element.67, f32[1536]{0:T(1024)S(1)} %get-tuple-element.68, ...), kind=kLoop, calls=%fused_computation.147 | loop fusion | flops 59768832 | bytes 14392320 | tf_op jit(solution)/shard_map/add | solution.py:36
  28.3 23.3 %all-gather.7.cloned.1.call-done = bf16[1536,1536]{1,0:T(8,128)(2,1)} async-done(((bf16[192,1536]{1,0:T(8,128)(2,1)}), bf16[1536,1536]{1,0:T(8,128)(2,1)}) %all-gather.7.cloned.1.call-update) | async-done | bytes 4718608 | tf_op jit(solution)/shard_map/all_gather | solution.py:38
  51.6 5.3 fusion.2
  56.9 8.9 %all-gather = bf16[1,2048]{1,0:T(2,128)(2,1)S(1)} all-gather(bf16[1,256]{1,0:T(2,128)(2,1)S(1)} %copy-done.49), channel_id=2, replica_groups=mesh['seq'=4,'fsdp'=8] {'fsdp'}, dimensions={1}, use_global_device_ids=true | all-gather | bytes 4608 | tf_op jit(solution)/shard_map/all_gather | solution.py:44
  66.4 7.9 %all-gather.3 = s32[1,2048]{1,0:T(1,128)S(1)} all-gather(s32[1,256]{1,0:T(1,128)S(1)} %copy-done.50), channel_id=5, replica_groups=mesh['seq'=4,'fsdp'=8] {'fsdp'}, dimensions={1}, use_global_device_ids=true | all-gather | bytes 9216 | tf_op jit(solution)/shard_map/all_gather | solution.py:43
  74.9 27.6 %all-gather.9.cloned.1.call-done = bf16[2048,1536]{1,0:T(8,128)(2,1)} async-done(((bf16[256,1536]{1,0:T(8,128)(2,1)}), bf16[2048,1536]{1,0:T(8,128)(2,1)}) %all-gather.9.cloned.1.call-update) | async-done | bytes 6291472 | tf_op jit(solution)/shard_map/all_gather | solution.py:42
  102.6 8.9 %fusion.187 = (f32[2048]{0:T(1024)S(1)}, f32[2048,1024]{0,1:T(8,128)S(1)}) fusion(bf16[2048,1536]{1,0:T(8,128)(2,1)} %all-gather.9.cloned.1.call-done, bf16[1536,1024]{1,0:T(8,128)(2,1)S(1)} %copy-done), kind=kOutput, calls=%fused_computation.403 | convolution fusion | flops 6444546048 | bytes 17833984 | tf_op jit(solution)/shard_map/dot_general | solution.py:46
  111.5 9.2 %all-gather.1 = f32[16384]{0:T(1024)S(1)} all-gather(f32[2048]{0:T(1024)S(1)} %get-tuple-element.114), channel_id=3, replica_groups=mesh['seq'=4,'fsdp'=8] {'fsdp'}, dimensions={0}, use_global_device_ids=true | all-gather | bytes 73728 | tf_op jit(solution)/shard_map/all_gather | solution.py:21
  120.7 1.2 exponential_reduce_fusion
  121.8 8.5 %all-gather.2 = f32[16384]{0:T(1024)S(1)} all-gather(f32[2048]{0:T(1024)S(1)} %exponential_reduce_fusion), channel_id=4, replica_groups=mesh['seq'=4,'fsdp'=8] {'fsdp'}, dimensions={0}, use_global_device_ids=true | all-gather | bytes 73728 | tf_op jit(solution)/shard_map/all_gather | solution.py:21
  130.8 16.5 %convolution_convert_fusion = bf16[2048,1536]{1,0:T(8,128)(2,1)} fusion(bf16[1536,1024]{1,0:T(8,128)(2,1)S(1)} %copy-done, f32[2048,1024]{0,1:T(8,128)} %copy-done.5, s32[2048]{0:T(1024)} %bitcast.450, f32[2048]{0:T(1024)S(1)} %get-tuple-element.33, f32[2048]{0:T(1024)S(1)} %get-tuple-element.32, f32[2048]{0:T(1024)} %bitcast.448), kind=kOutput, calls=%fused_computation.38 | convolution fusion | flops 6460276736 | bytes 17858560 | tf_op jit(solution)/shard_map/dot_general | solution.py:71
  148.0 12.6 %convolution_convert_fusion.1 = bf16[1536,1024]{1,0:T(8,128)(2,1)} fusion(bf16[2048,1536]{1,0:T(8,128)(2,1)} %all-gather.9.cloned.1.call-done, f32[2048,1024]{0,1:T(8,128)} %copy-done.5, s32[2048]{0:T(1024)S(1)} %bitcast.451, f32[2048]{0:T(1024)S(1)} %get-tuple-element.33, f32[2048]{0:T(1024)S(1)} %get-tuple-element.32, f32[2048]{0:T(1024)S(1)} %bitcast.449), kind=kOutput, calls=%fused_computation.81 | convolution fusion | flops 6458703872 | bytes 17858560 | tf_op jit(solution)/shard_map/dot_general | solution.py:64
  160.8 48.4 %reduce-scatter.4.cloned.1.call-done = bf16[256,1536]{1,0:T(8,128)(2,1)} async-done(((bf16[2048,1536]{1,0:T(8,128)(2,1)}), bf16[256,1536]{1,0:T(8,128)(2,1)}) %reduce-scatter.4.cloned.1.call-update) | async-done | bytes 786448 | tf_op jit(solution)/shard_map/reduce_scatter | solution.py:70
  209.2 8.4 %fusion.63 = (f32[1536]{0:T(1024)S(1)}, f32[1536]{0:T(1024)S(1)}, f32[1536]{0:T(1024)S(1)}, f32[1536]{0:T(1024)S(1)}, f32[1536]{0:T(1024)S(1)}, /*index=5*/f32[1...) fusion(bf16[1,256,1536]{2,1,0:T(8,128)(2,1)} %param.8, ...), kind=kOutput, calls=%fused_computation.178 | convolution fusion | flops 1236650496 | bytes 8752128 | tf_op jit(solution)/shard_map/dot_general | solution.py:86
  217.7 3.3 fusion.79
  221.3 1.6 fusion.62
  223.1 2.8 stack.127
  225.9 6.7 %fusion.184 = f32[1536,1536]{1,0:T(8,128)} fusion(bf16[256,1536]{1,0:T(8,128)(2,1)} %reduce-scatter.4.cloned.1.call-done, f32[256,1536]{1,0:T(8,128)} %fusion.32), kind=kOutput, calls=%fused_computation.400 | convolution fusion | flops 1209925632 | bytes 11796480 | tf_op jit(solution)/shard_map/dot_general | solution.py:79
  233.8 1.3 collective-permute-start.2
  235.1 5.2 collective-permute-start.3
  240.3 32.5 %reduce-scatter.8.cloned.1.call-done = bf16[384,1024]{1,0:T(8,128)(2,1)} async-done(((bf16[1536,1024]{1,0:T(8,128)(2,1)}), bf16[384,1024]{1,0:T(8,128)(2,1)}) %reduce-scatter.8.cloned.1.call-update) | async-done | bytes 786448 | tf_op jit(solution)/shard_map/reduce_scatter | solution.py:67
  272.8 2.6 convert_element_type.568
  275.6 9.5 %fusion.183 = bf16[1,256,1536]{2,1,0:T(8,128)(2,1)} fusion(bf16[1,256,1536]{2,1,0:T(8,128)(2,1)S(1)} %bitcast.445, bf16[1,15,1536]{2,1,0:T(8,128)(2,1)} %collective-permute-done.3, f32[1536]{0:T(1024)S(1)} %copy-done.44, f32[1536]{0:T(1024)S(1)} %copy-done.46, f32[1536]{0:T(1024)S(1)} %get-tuple-element.66, f32[1536]{0:T(1024)S(1)} %get-tuple-element.67, ...), kind=kLoop, calls=%fused_computation.365 | loop fusion | flops 84541440 | bytes 3428352 | tf_op jit(solution)/shard_map/broadcast_in_dim | solution.py:102
  285.1 117.6 %all-reduce.2.cloned.1.call-done = f32[31,1536]{1,0:T(8,128)} async-done(((f32[31,1536]{1,0:T(8,128)}), f32[31,1536]{1,0:T(8,128)}) %all-reduce.2.cloned.1.call-update) | async-done | bytes 190480 | tf_op jit(solution)/shard_map/psum | solution.py:101
  402.7 143.7 %reduce-scatter.6.cloned.1.call-done = f32[48,1536]{1,0:T(8,128)} async-done(((f32[1536,1536]{1,0:T(8,128)}), f32[48,1536]{1,0:T(8,128)}) %reduce-scatter.6.cloned.1.call-update) | async-done | bytes 294928 | tf_op jit(solution)/shard_map/reduce_scatter | solution.py:78
  546.4 1.6 copy.23
  (174 shorter events, 6.0 us)
Async XLA Ops:
  7.2 95.4 %copy-start = (bf16[1536,1024]{1,0:T(8,128)(2,1)S(1)}, bf16[1536,1024]{1,0:T(8,128)(2,1)}, u32[]{:S(2)}) copy-start(bf16[1536,1024]{1,0:T(8,128)(2,1)} %param.11) | copy-start | bytes 9437188
  7.2 44.4 %all-gather.7.cloned.1.call-start = ((), (), s32[]{:S(2)}) async-start(), calls=%async_computation.3 | async-start | bytes 5308416 | tf_op jit(solution)/shard_map/all_gather | solution.py:38
  7.9 94.7 %all-gather.9.cloned.1.call-start = ((), (), s32[]{:S(2)}) async-start(), calls=%async_computation.4 | async-start | bytes 7077888 | tf_op jit(solution)/shard_map/all_gather | solution.py:42
  9.0 11.1 %collective-permute-start = (bf16[1,15,1536]{2,1,0:T(8,128)(2,1)S(1)}, bf16[1,15,1536]{2,1,0:T(8,128)(2,1)S(1)}, u32[]{:S(2)}, u32[]{:S(2)}) collective-permute-start(bf16[1,15,1536]{2,1,0:T(8,128)(2,1)S(1)} %get-tuple-element.112), channel_id=1, source_target_pairs={{0,8},{8,16},{16,24},{1,9},{9,17},{17,25},{2,10},{10,18},{18,26},{... | collective-permute-start | bytes 138248 | tf_op jit(solution)/shard_map/ppermute | solution.py:12
  13.9 6.1 %collective-permute-start.1 = (bf16[1,15,1536]{2,1,0:T(8,128)(2,1)S(1)}, bf16[1,15,1536]{2,1,0:T(8,128)(2,1)S(1)}, u32[]{:S(2)}, u32[]{:S(2)}) collective-permute-start(bf16[1,15,1536]{2,1,0:T(8,128)(2,1)S(1)} %get-tuple-element.113), channel_id=1, source_target_pairs={{8,0},{16,8},{24,16},{9,1},{17,9},{25,17},{10,2},{18,10},{26,18},{... | collective-permute-start | bytes 138248 | tf_op jit(solution)/shard_map/ppermute | solution.py:15
  28.2 28.7 %copy-start.49 = (bf16[1,256]{1,0:T(2,128)(2,1)S(1)}, bf16[1,256]{1,0:T(2,128)(2,1)}, u32[]{:S(2)}) copy-start(bf16[1,256]{1,0:T(2,128)(2,1)} %param.13) | copy-start | bytes 1540
  28.3 38.2 %copy-start.50 = (s32[1,256]{1,0:T(1,128)S(1)}, s32[1,256]{1,0:T(1,128)}, u32[]{:S(2)}) copy-start(s32[1,256]{1,0:T(1,128)} %param.12) | copy-start | bytes 3076
  56.9 152.3 %reduce-scatter.4.cloned.1.call-start = ((), (), s32[]{:S(2)}) async-start(), calls=%async_computation.5 | async-start | bytes 7077888 | tf_op jit(solution)/shard_map/reduce_scatter | solution.py:70
  147.3 125.5 %reduce-scatter.8.cloned.1.call-start = ((), (), s32[]{:S(2)}) async-start(), calls=%async_computation.8 | async-start | bytes 3932160 | tf_op jit(solution)/shard_map/reduce_scatter | solution.py:67
  160.6 242.1 %all-reduce.2.cloned.1.call-start = ((), (), s32[]{:S(2)}) async-start(), calls=%async_computation.6 | async-start | bytes 393216 | tf_op jit(solution)/shard_map/psum | solution.py:101
  225.9 320.5 %reduce-scatter.6.cloned.1.call-start = ((), (), s32[]{:S(2)}) async-start(), calls=%async_computation.7 | async-start | bytes 9732096 | tf_op jit(solution)/shard_map/reduce_scatter | solution.py:78
  232.7 42.7 %copy-start.10 = (f32[1536]{0:T(1024)S(1)}, f32[1536]{0:T(1024)}, u32[]{:S(2)}) copy-start(f32[1536]{0:T(1024)} %copy-done.9) | copy-start | bytes 18436
  232.7 42.7 %copy-start.12 = (f32[1536]{0:T(1024)S(1)}, f32[1536]{0:T(1024)}, u32[]{:S(2)}) copy-start(f32[1536]{0:T(1024)} %copy-done.11) | copy-start | bytes 18436
  232.7 42.7 %copy-start.14 = (f32[1536]{0:T(1024)S(1)}, f32[1536]{0:T(1024)}, u32[]{:S(2)}) copy-start(f32[1536]{0:T(1024)} %copy-done.13) | copy-start | bytes 18436
  232.7 42.7 %copy-start.16 = (f32[1536]{0:T(1024)S(1)}, f32[1536]{0:T(1024)}, u32[]{:S(2)}) copy-start(f32[1536]{0:T(1024)} %copy-done.15) | copy-start | bytes 18436
  232.7 42.7 %copy-start.18 = (f32[1536]{0:T(1024)S(1)}, f32[1536]{0:T(1024)}, u32[]{:S(2)}) copy-start(f32[1536]{0:T(1024)} %copy-done.17) | copy-start | bytes 18436
  232.7 42.7 %copy-start.20 = (f32[1536]{0:T(1024)S(1)}, f32[1536]{0:T(1024)}, u32[]{:S(2)}) copy-start(f32[1536]{0:T(1024)} %copy-done.19) | copy-start | bytes 18436
  232.7 42.7 %copy-start.22 = (f32[1536]{0:T(1024)S(1)}, f32[1536]{0:T(1024)}, u32[]{:S(2)}) copy-start(f32[1536]{0:T(1024)} %copy-done.21) | copy-start | bytes 18436
  232.7 42.7 %copy-start.24 = (f32[1536]{0:T(1024)S(1)}, f32[1536]{0:T(1024)}, u32[]{:S(2)}) copy-start(f32[1536]{0:T(1024)} %copy-done.23) | copy-start | bytes 18436
  232.7 42.7 %copy-start.26 = (f32[1536]{0:T(1024)S(1)}, f32[1536]{0:T(1024)}, u32[]{:S(2)}) copy-start(f32[1536]{0:T(1024)} %copy-done.25) | copy-start | bytes 18436
  232.8 42.7 %copy-start.28 = (f32[1536]{0:T(1024)S(1)}, f32[1536]{0:T(1024)}, u32[]{:S(2)}) copy-start(f32[1536]{0:T(1024)} %copy-done.27) | copy-start | bytes 18436
  232.8 42.7 %copy-start.30 = (f32[1536]{0:T(1024)S(1)}, f32[1536]{0:T(1024)}, u32[]{:S(2)}) copy-start(f32[1536]{0:T(1024)} %copy-done.29) | copy-start | bytes 18436
  232.8 42.7 %copy-start.32 = (f32[1536]{0:T(1024)S(1)}, f32[1536]{0:T(1024)}, u32[]{:S(2)}) copy-start(f32[1536]{0:T(1024)} %copy-done.31) | copy-start | bytes 18436
  232.8 42.7 %copy-start.34 = (f32[1536]{0:T(1024)S(1)}, f32[1536]{0:T(1024)}, u32[]{:S(2)}) copy-start(f32[1536]{0:T(1024)} %copy-done.33) | copy-start | bytes 18436
  232.8 42.7 %copy-start.36 = (f32[1536]{0:T(1024)S(1)}, f32[1536]{0:T(1024)}, u32[]{:S(2)}) copy-start(f32[1536]{0:T(1024)} %copy-done.35) | copy-start | bytes 18436
  232.8 42.7 %copy-start.38 = (f32[1536]{0:T(1024)S(1)}, f32[1536]{0:T(1024)}, u32[]{:S(2)}) copy-start(f32[1536]{0:T(1024)} %copy-done.37) | copy-start | bytes 18436
  232.8 42.7 %copy-start.40 = (f32[1536]{0:T(1024)S(1)}, f32[1536]{0:T(1024)}, u32[]{:S(2)}) copy-start(f32[1536]{0:T(1024)} %copy-done.39) | copy-start | bytes 18436
  232.8 42.7 %copy-start.42 = (f32[1536]{0:T(1024)S(1)}, f32[1536]{0:T(1024)}, u32[]{:S(2)}) copy-start(f32[1536]{0:T(1024)} %copy-done.41) | copy-start | bytes 18436
  232.8 42.7 %copy-start.44 = (f32[1536]{0:T(1024)S(1)}, f32[1536]{0:T(1024)}, u32[]{:S(2)}) copy-start(f32[1536]{0:T(1024)} %copy-done.43) | copy-start | bytes 18436
  232.8 42.7 %copy-start.46 = (f32[1536]{0:T(1024)S(1)}, f32[1536]{0:T(1024)}, u32[]{:S(2)}) copy-start(f32[1536]{0:T(1024)} %copy-done.45) | copy-start | bytes 18436
  233.8 41.6 %collective-permute-start.2 = (bf16[1,15,1536]{2,1,0:T(8,128)(2,1)S(1)}, bf16[1,15,1536]{2,1,0:T(8,128)(2,1)S(1)}, u32[]{:S(2)}, u32[]{:S(2)}) collective-permute-start(bf16[1,15,1536]{2,1,0:T(8,128)(2,1)S(1)} %get-tuple-element.110), channel_id=1, source_target_pairs={{8,0},{16,8},{24,16},{9,1},{17,9},{25,17},{10,2},{18,10},{26,18},{... | collective-permute-start | bytes 138248 | tf_op jit(solution)/shard_map/ppermute | solution.py:15
  235.1 40.3 %collective-permute-start.3 = (bf16[1,15,1536]{2,1,0:T(8,128)(2,1)S(1)}, bf16[1,15,1536]{2,1,0:T(8,128)(2,1)}, u32[]{:S(2)}, u32[]{:S(2)}) collective-permute-start(bf16[1,15,1536]{2,1,0:T(8,128)(2,1)S(1)} %get-tuple-element.111), channel_id=1, source_target_pairs={{0,8},{8,16},{16,24},{1,9},{9,17},{17,25},{2,10},{10,18},{18,26},{... | collective-permute-start | bytes 138248 | tf_op jit(solution)/shard_map/ppermute | solution.py:12
  (29 other events, 200.1 us)
Sparse Core Ops, SparseCore 0:
  9.9 41.6 all-gather.6
  57.0 45.5 all-gather.8
  147.4 61.7 reduce-scatter.3
  211.5 61.3 reduce-scatter.7
  279.7 122.9 all-reduce.1
  410.0 136.3 reduce-scatter.5
where the time goes:
time: 556 us; the launch traced here: 555 us
  waiting for transfers between devices  394 us (71%)
  matrix products  58.3 us (10%)
  blocking collectives  34.4 us (6%)
  other arithmetic  26.7 us (5%)
  between operations  15.2 us (3%)
  starting transfers between devices  13.1 us (2%)
  local copies, waits for them, and re-layouts  13 us (2%)
    reduce_scatter x1, waiting for transfers between devices, body(): lax.psum_scatter(lax.dot_general(gated, dmixed, (((0,), (0,)), ((), ())),...  144 us
    psum x1, waiting for transfers between devices, body(): kernel_grad = lax.psum(kernel_term, ('seq', 'fsdp'))  118 us
    reduce_scatter x1, waiting for transfers between devices, body(): lax.psum_scatter(lax.dot_general(dlogits, head_weight, (((1,), (1,)), (()...  48.4 us
    reduce_scatter x1, waiting for transfers between devices, body(): lax.psum_scatter(head_term.astype(jnp.bfloat16), 'seq', scatter_dimension...  32.5 us
    all_gather x1, waiting for transfers between devices, body(): lax.all_gather(mixed, 'fsdp', axis=0, tiled=True)  27.6 us
    all_gather x1, waiting for transfers between devices, body(): pw_full = lax.all_gather(pw_weight, 'fsdp', axis=0, tiled=True)  23.3 us
    all_gather x2, blocking collectives, joined(): pieces = jax.tree.map(lambda part: lax.all_gather(part, axis), value)  17.6 us
    dot_general x1, matrix products, body(): lax.dot_general(dlogits, head_weight, (((1,), (1,)), ((), ())), preferred...  16.5 us
  transfers between devices with their start and end apart: 10, of which 6 were waited for; matrix products, arithmetic and copies ran while one was open for 11% of the time, Pallas kernels for 0%

commit v1 on v0

v1 whole, which is shorter than its diff:
```python
import jax
import jax.numpy as jnp
from jax import lax
from jax.sharding import PartitionSpec as P

BF = jnp.bfloat16
F32 = jnp.float32


def swap(value, mask):
    count = lax.axis_size("fsdp")
    return lax.ppermute(value, "fsdp", [(i, i ^ mask) for i in range(count)])


def gather_chips(block):
    chips = lax.axis_size("fsdp") // 2
    if chips != 4:
        return [block] + [swap(block, 2 * m) for m in range(1, chips)]
    half = block.shape[0] // 2
    from_x = swap(block, 2)
    from_y = swap(block, 4)
    far_low = swap(from_x[:half], 4)
    far_high = swap(from_y[half:], 2)
    return [block, from_x, from_y, jnp.concatenate([far_low, far_high], axis=0)]


def scatter_chips(parts):
    chips = len(parts)
    if chips != 4:
        total = parts[0]
        for m in range(1, chips):
            total = total + swap(parts[m].astype(BF), 2 * m).astype(F32)
        return total
    half = parts[0].shape[0] // 2
    far = parts[3].astype(BF)
    low = swap(far[:half], 2).astype(F32)
    high = swap(far[half:], 4).astype(F32)
    to_y = jnp.concatenate([parts[2][:half] + low, parts[2][half:]], axis=0).astype(BF)
    to_x = jnp.concatenate([parts[1][:half], parts[1][half:] + high], axis=0).astype(BF)
    return parts[0] + swap(to_x, 2).astype(F32) + swap(to_y, 4).astype(F32)


def line_scatter(term, kind):
    count = lax.axis_size("seq")
    here = lax.axis_index("seq")

    def block(index):
        index = jnp.clip(index, 0, count - 1)
        return lax.dynamic_index_in_dim(term, index, 0, keepdims=False).astype(F32)

    up = down = None
    for step in range(1, count):
        to_up = block(here + count - step)
        to_down = block(here - count + step)
        if up is not None:
            to_up = to_up + up.astype(F32)
            to_down = to_down + down.astype(F32)
        up = lax.ppermute(to_up.astype(kind), "seq", [(i, i + 1) for i in range(step)])
        down = lax.ppermute(
            to_down.astype(kind), "seq", [(i, i - 1) for i in range(count - step, count)]
        )
    return block(here) + up.astype(F32) + down.astype(F32)


def halo(block, width):
    count = lax.axis_size("seq")
    forward = [(i, i + 1) for i in range(count - 1)]
    backward = [(i + 1, i) for i in range(count - 1)]
    low = lax.ppermute(block[block.shape[0] - width :], "seq", forward)
    high = lax.ppermute(block[:width], "seq", backward)
    return jnp.concatenate([low, block, high], axis=0)


def body(frames, conv_kernel, pw_weight, head_weight, targets, frame_weight):
    frames = frames[0]
    rows, width = frames.shape
    taps = conv_kernel.shape[0]
    reach = (taps - 1) // 2
    seqs = lax.axis_size("seq")
    count = lax.axis_size("fsdp")
    chips = count // 2
    me = lax.axis_index("fsdp")
    chip = me // 2
    core = me % 2
    padded = halo(frames, reach)
    labels = jnp.stack([targets[0].astype(F32), frame_weight[0].astype(F32)])
    all_labels = [labels] + [swap(labels, 2 * m) for m in range(1, chips)]
    pw_mine = gather_chips(pw_weight)
    pw_other = swap(jnp.stack(pw_mine), 1)
    shard = pw_weight.shape[0]
    pw_full = jnp.zeros((count, shard, width), BF)
    for m in range(chips):
        pw_full = lax.dynamic_update_index_in_dim(pw_full, pw_mine[m], me ^ (2 * m), 0)
        pw_full = lax.dynamic_update_index_in_dim(pw_full, pw_other[m], me ^ (2 * m + 1), 0)
    pw_full = pw_full.reshape(width, width)
    head_other = swap(head_weight, 1)

    conv = jnp.zeros((rows, width), F32)
    for tap in range(taps):
        conv = conv + conv_kernel[tap] * padded[tap : tap + rows].astype(F32)
    gated = jax.nn.silu(conv).astype(BF)
    proj = jnp.dot(gated, pw_full, preferred_element_type=F32)
    mixed = (frames.astype(F32) + proj).astype(BF)

    all_mixed = gather_chips(mixed)
    piece = width // (seqs * count)
    gated_t = gated.T.reshape(seqs, chips, 2, piece, rows)
    gated_t = jnp.stack(
        [lax.dynamic_index_in_dim(gated_t, chip ^ m, 1, keepdims=False) for m in range(chips)]
    )
    gated_own = lax.dynamic_index_in_dim(gated_t, core, 2, keepdims=False)
    gated_sent = lax.dynamic_index_in_dim(gated_t, 1 - core, 2, keepdims=False)
    gated_got = swap(gated_sent, 1)
    gated_pair = jnp.concatenate([gated_own, gated_got], axis=-1)

    weights = (head_weight, head_other)
    vocab = head_weight.shape[1]
    logits = []
    stats = []
    for m in range(chips):
        pair = [jnp.dot(all_mixed[m], w, preferred_element_type=F32) for w in weights]
        top = jnp.maximum(jnp.max(pair[0], axis=1), jnp.max(pair[1], axis=1))
        total = sum(jnp.sum(jnp.exp(l - top[:, None]), axis=1) for l in pair)
        logits.append(pair)
        stats.append((top, total))
    mixed_other = swap(jnp.stack(all_mixed), 1)
    tops = jnp.stack([s[0] for s in stats])
    totals = jnp.stack([s[1] for s in stats])
    packed = jnp.concatenate([tops, totals], axis=0)
    got = [packed] + [swap(packed, 2 * m) for m in range(1, chips)]
    dl_own, dl_other = [], []
    entries = lax.broadcasted_iota(jnp.int32, (1, vocab), 1)
    for m in range(chips):
        part_tops = [got[o][m ^ o] for o in range(chips)]
        part_totals = [got[o][chips + (m ^ o)] for o in range(chips)]
        top = part_tops[0]
        for t in part_tops[1:]:
            top = jnp.maximum(top, t)
        total = sum(s * jnp.exp(t - top) for s, t in zip(part_totals, part_tops))
        inverse = 1.0 / total
        target = all_labels[m][0].astype(jnp.int32)
        weight = all_labels[m][1]
        for l, owner, into in ((logits[m][0], me, dl_own), (logits[m][1], me ^ 1, dl_other)):
            hit = ((target - owner * vocab)[:, None] == entries).astype(F32)
            probs = jnp.exp(l - top[:, None]) * inverse[:, None]
            into.append((weight[:, None] * (probs - hit)).astype(BF))
    dl_got = swap(jnp.stack(dl_other), 1)

    def back_head(m):
        rhs = (((1,), (1,)), ((), ()))
        return lax.dot_general(
            dl_own[m], head_weight, rhs, preferred_element_type=F32
        ) + lax.dot_general(dl_other[m], head_other, rhs, preferred_element_type=F32)

    dmixed = scatter_chips([back_head(m) for m in range(chips)]).astype(BF)

    left = jnp.concatenate([jnp.concatenate(all_mixed, 0), mixed_other.reshape(-1, width)], 0)
    right = jnp.concatenate([jnp.concatenate(dl_own, 0), dl_got.reshape(-1, vocab)], 0)
    head_term = lax.dot_general(
        left, right, (((0,), (0,)), ((), ())), preferred_element_type=F32
    )
    head_grad = line_scatter(head_term.reshape(seqs, width // seqs, vocab), BF)

    dmixed_pair = jnp.concatenate([dmixed, swap(dmixed, 1)], axis=0)
    pw_term = jnp.dot(
        gated_pair.reshape(-1, 2 * rows), dmixed_pair, preferred_element_type=F32
    ).reshape(chips, seqs * piece, width)
    pw_sum = scatter_chips([pw_term[m] for m in range(chips)])
    pw_grad = line_scatter(pw_sum.reshape(seqs, piece, width), BF)

    dgated = lax.dot_general(
        dmixed, pw_full, (((1,), (1,)), ((), ())), preferred_element_type=F32
    )
    sig = jax.nn.sigmoid(conv)
    dconv = (dgated * sig * (1.0 + conv * (1.0 - sig))).astype(BF)
    dpad = halo(dconv, reach)
    dconv_f = dconv.astype(F32)
    back = dmixed.astype(F32)
    kernel_rows = []
    for tap in range(taps):
        kernel_rows.append(jnp.sum(dconv_f * padded[tap : tap + rows].astype(F32), axis=0))
        back = back + conv_kernel[tap] * dpad[2 * reach - tap : 2 * reach - tap + rows].astype(F32)
    kernel_grad = jnp.stack(kernel_rows, axis=0)
    mask = 1
    while mask < count:
        kernel_grad = kernel_grad + swap(kernel_grad, mask)
        mask *= 2
    mask = 1
    while mask < seqs:
        kernel_grad = kernel_grad + lax.ppermute(
            kernel_grad, "seq", [(i, i ^ mask) for i in range(seqs)]
        )
        mask *= 2
    return (back.astype(BF)[None], kernel_grad, pw_grad, head_grad)


def solution(mesh):
    return jax.shard_map(
        body,
        mesh=mesh,
        in_specs=(
            P("fsdp", "seq", None),
            P(),
            P("fsdp", None),
            P(None, "fsdp"),
            P("fsdp", "seq"),
            P("fsdp", "seq"),
        ),
        out_specs=(P("fsdp", "seq", None), P(), P(("seq", "fsdp"), None), P("seq", "fsdp")),
        check_vma=False,
    )
```

time: 556 us -> 297 us (0.53)
  waiting for transfers between devices: 394 us -> 60 us
  starting transfers between devices: 13.1 us -> 85.7 us
  blocking collectives: 34.4 us -> 0 us
  other arithmetic: 26.7 us -> 55.4 us
  local copies, waits for them, and re-layouts: 13 us -> 30.6 us
  between operations: 15.2 us -> 3.51 us
    reduce_scatter x3 -> x0, waiting for transfers between devices: 225 us -> none  [the longest x1 144 us: body(): lax.psum_scatter(lax.dot_general(gated, dmixed, (((0,), (0,)), ((), ())),...]
    psum x1 -> x0, waiting for transfers between devices: 118 us -> none  [body(): kernel_grad = lax.psum(kernel_term, ('seq', 'fsdp'))]
    ppermute x4 -> x49, starting transfers between devices: 12.7 us -> 85.7 us  [the longest x6 32.3 us: line_scatter(): lax.ppermute(to_up.astype(kind), 'seq', [(i, i + 1) for i in range(step)])]
    ppermute x4 -> x49, waiting for transfers between devices: 0.01 us -> 60 us  [the longest x31 32.7 us: swap(): return lax.ppermute(value, 'fsdp', [(i, i ^ mask) for i in range(count)])]
    all_gather x2 -> x0, waiting for transfers between devices: 50.9 us -> none  [the longest x1 27.6 us: body(): lax.all_gather(mixed, 'fsdp', axis=0, tiled=True)]
    all_gather x4 -> x0, blocking collectives: 34.4 us -> none  [the longest x2 17.6 us: joined(): pieces = jax.tree.map(lambda part: lax.all_gather(part, axis), value)]
    dynamic_update_slice x0 -> x7, local copies, waits for them, and re-layouts: none -> 10.6 us  [the longest x4 7.97 us: body(): lax.dynamic_update_index_in_dim(pw_full, pw_other[m], me ^ 2 * m + 1, 0)]
    another operation x0 -> x13, other arithmetic: none -> 9.07 us  [the longest x1 3.51 us: body(): mixed_other = swap(jnp.stack(all_mixed), 1)]
  transfers between devices with their start and end apart: 10 -> 49, of which waited for: 6 -> 10; matrix products, arithmetic and copies ran while one was open for 11% -> 48% of each run, Pallas kernels for 0% -> 0%
where the time goes in v1:
time: 297 us; the launch traced here: 293 us
  starting transfers between devices  85.7 us (29%)
  waiting for transfers between devices  60 us (20%)
  matrix products  57.7 us (19%)
  other arithmetic  55.4 us (19%)
  local copies, waits for them, and re-layouts  30.6 us (10%)
  between operations  3.51 us (1%)
    ppermute x31, waiting for transfers between devices, swap(): return lax.ppermute(value, 'fsdp', [(i, i ^ mask) for i in range(count)])  32.7 us
    ppermute x6, starting transfers between devices, line_scatter(): lax.ppermute(to_up.astype(kind), 'seq', [(i, i + 1) for i in range(step)])  32.3 us
    ppermute x31, starting transfers between devices, swap(): return lax.ppermute(value, 'fsdp', [(i, i ^ mask) for i in range(count)])  29.1 us
    ppermute x6, waiting for transfers between devices, line_scatter(): lax.ppermute(to_up.astype(kind), 'seq', [(i, i + 1) for i in range(step)])  24.4 us
    dot_general x8, matrix products, body(): jnp.dot(all_mixed[m], w, preferred_element_type=F32)  18.9 us
    dot_general x4, matrix products, back_head(): lax.dot_general(dl_other[m], head_other, rhs, preferred_element_type=F32)  13.2 us
    dot_general x1, matrix products, body(): lax.dot_general(left, right, (((0,), (0,)), ((), ())), preferred_element_...  9.29 us
    ppermute x2, starting transfers between devices, halo(): low = lax.ppermute(block[block.shape[0] - width:], 'seq', forward)  9.07 us
  transfers between devices with their start and end apart: 49, of which 10 were waited for; matrix products, arithmetic and copies ran while one was open for 48% of the time, Pallas kernels for 0%

profile of v1, /device:TPU:0, one launch (start us, length us, event | category | flops | bytes accessed | tf_op | source)
XLA Modules:
  0.0 292.9 jit_solution(18242951788176734365)
XLA Ops:
  0.6 3.0 %collective-permute-start.3 = (bf16[192,1536]{1,0:T(8,128)(2,1)}, bf16[192,1536]{1,0:T(8,128)(2,1)S(1)}, u32[]{:S(2)}, u32[]{:S(2)}) collective-permute-start(bf16[192,1536]{1,0:T(8,128)(2,1)} %param.8), channel_id=1, source_target_pairs={{0,4},{1,5},{2,6},{3,7},{4,0},{5,1},{6,2},{7,3},{8,12},{9,13},{10,... | collective-permute-start | bytes 1769480 | tf_op jit(solution)/shard_map/ppermute | solution.py:12
  15.4 2.6 broadcast_in_dim.15
  19.0 3.5 %collective-permute-start = (bf16[15,1536]{1,0:T(8,128)(2,1)S(1)}, bf16[15,1536]{1,0:T(8,128)(2,1)S(1)}, u32[]{:S(2)}, u32[]{:S(2)}) collective-permute-start(bf16[15,1536]{1,0:T(8,128)(2,1)S(1)} %get-tuple-element.100), channel_id=1, source_target_pairs={{0,8},{8,16},{16,24},{1,9},{9,17},{17,25},{2,10},{10,18},{18,26},{... | collective-permute-start | bytes 138248 | tf_op jit(solution)/shard_map/ppermute | solution.py:69
  28.9 2.7 collective-permute-done.5
  35.2 8.4 %fusion.175 = (bf16[1536,256]{0,1:T(8,128)(2,1)S(1)}, f32[256,1536]{1,0:T(8,128)}) fusion(bf16[15,1536]{1,0:T(8,128)(2,1)S(1)} %collective-permute-done.1, bf16[256,1536]{1,0:T(8,128)(2,1)S(1)} %bitcast.176, f32[1536]{0:T(1024)S(1)} %copy-done.87, f32[1536]{0:T(1024)S(1)} %copy-done.89, f32[1536]{0:T(1024)S(1)} %get-tuple-element.36, ...), kind=kLoop, calls=%fused_computation.451 | loop fusion | flops 73531392 | bytes 3428352 | tf_op jit(solution)/shard_map/transpose | solution.py:107
  56.1 3.9 %constant_dynamic-update-slice_fusion.7 = (bf16[2048,1536]{1,0:T(8,128)(2,1)S(1)}, bf16[256,1536]{1,0:T(8,128)(2,1)S(1)}) fusion(bf16[1536,1536]{1,0:T(8,128)(2,1)} %bitcast.8, f32[256,1536]{1,0:T(8,128)S(1)} %copy-done.22, bf16[1,256,1536]{2,1,0:T(8,128)(2,1)S(1)} %copy-done), kind=kOutput, calls=%fused_computation.388 | convolution fusion | flops 1211105280 | bytes 8650752 | tf_op jit(solution)/shard_map/dot_general | solution.py:102
  63.1 3.3 %fusion.189 = (f32[256]{0:T(256)S(1)}, f32[256,1024]{1,0:T(8,128)S(1)}) fusion(bf16[256,1536]{1,0:T(8,128)(2,1)S(1)} %get-tuple-element.160, bf16[1536,1024]{1,0:T(8,128)(2,1)} %collective-permute-done.7), kind=kOutput, calls=%fused_computation.464 | convolution fusion | flops 805568256 | bytes 4981760 | tf_op jit(solution)/shard_map/dot_general | solution.py:121
  66.9 12.6 %collective-permute-done.8 = bf16[256,1536]{1,0:T(8,128)(2,1)S(1)} collective-permute-done((bf16[256,1536]{1,0:T(8,128)(2,1)S(1)}, bf16[256,1536]{1,0:T(8,128)(2,1)S(1)}, u32[]{:S(2)}, u32[]{:S(2)}) %collective-permute-start.8) | collective-permute-done | bytes 786464 | tf_op jit(solution)/shard_map/ppermute | solution.py:12
  82.8 3.3 %fusion.191 = (f32[256]{0:T(256)S(1)}, f32[256,1024]{1,0:T(8,128)S(1)}) fusion(bf16[256,1536]{1,0:T(8,128)(2,1)S(1)} %collective-permute-done.8, bf16[1536,1024]{1,0:T(8,128)(2,1)} %collective-permute-done.7), kind=kOutput, calls=%fused_computation.466 | convolution fusion | flops 805568256 | bytes 4981760 | tf_op jit(solution)/shard_map/dot_general | solution.py:121
  87.2 3.3 %fusion.193 = (f32[256]{0:T(256)S(1)}, f32[256,1024]{1,0:T(8,128)S(1)}) fusion(bf16[256,1536]{1,0:T(8,128)(2,1)S(1)} %collective-permute-done.9, bf16[1536,1024]{1,0:T(8,128)(2,1)} %collective-permute-done.7), kind=kOutput, calls=%fused_computation.468 | convolution fusion | flops 805568256 | bytes 4981760 | tf_op jit(solution)/shard_map/dot_general | solution.py:121
  92.8 4.7 %fusion.195 = (f32[256]{0:T(256)S(1)}, f32[256,1024]{1,0:T(8,128)S(1)}) fusion(bf16[256,1536]{1,0:T(8,128)(2,1)S(1)} %get-tuple-element.103, bf16[1536,1024]{1,0:T(8,128)(2,1)} %collective-permute-done.7), kind=kOutput, calls=%fused_computation.470 | convolution fusion | flops 805568256 | bytes 4981760 | tf_op jit(solution)/shard_map/dot_general | solution.py:121
  102.1 3.5 %pad_maximum_fusion = bf16[4,256,1536]{2,1,0:T(8,128)(2,1)} fusion(bf16[1,256,1536]{2,1,0:T(8,128)(2,1)} %bitcast.197, bf16[1,256,1536]{2,1,0:T(8,128)(2,1)} %bitcast.192, bf16[1,256,1536]{2,1,0:T(8,128)(2,1)} %bitcast.191, bf16[1,256,1536]{2,1,0:T(8,128)(2,1)} %bitcast.199), kind=kLoop, calls=%fused_computation.88 | loop fusion | flops 4718592 | bytes 6291456 | tf_op jit(solution)/shard_map/stack | solution.py:126
  108.1 3.2 %convolution_add_fusion = f32[256,1536]{1,0:T(8,128)S(1)} fusion(f32[256,1536]{1,0:T(8,128)S(1)} %fusion.179, bf16[1536,1024]{1,0:T(8,128)(2,1)} %collective-permute-done.7, f32[256,1024]{1,0:T(8,128)S(1)} %get-tuple-element.158, s32[256]{0:T(256)S(1)} %bitcast.223, f32[256]{0:T(256)S(1)} %get-tuple-element.135, f32[256]{0:T(256)S(1)} %get-tuple-element.134, ...), kind=kOutput, calls=%fused_computation.89 | convolution fusion | flops 807534592 | bytes 7344128 | tf_op jit(solution)/shard_map/dot_general | solution.py:153
  113.2 3.1 %fusion.5 = bf16[256,1536]{1,0:T(8,128)(2,1)S(1)} fusion(f32[256,1536]{1,0:T(8,128)S(1)} %fusion.178, bf16[1536,1024]{1,0:T(8,128)(2,1)} %collective-permute-done.7, f32[256,1024]{1,0:T(8,128)S(1)} %copy-done.18, s32[256]{0:T(256)S(1)} %bitcast.239, f32[256]{0:T(256)S(1)} %get-tuple-element.133, f32[256]{0:T(256)S(1)} %get-tuple-element.132, ...), kind=kOutput, calls=%fused_computation.100 | convolution fusion | flops 807927808 | bytes 6557696 | tf_op jit(solution)/shard_map/dot_general | solution.py:153
  120.4 3.2 %convolution_add_fusion.2 = f32[256,1536]{1,0:T(8,128)S(1)} fusion(f32[256,1536]{1,0:T(8,128)S(1)} %fusion.177, bf16[1536,1024]{1,0:T(8,128)(2,1)} %collective-permute-done.7, f32[256,1024]{1,0:T(8,128)S(1)} %get-tuple-element.154, s32[256]{0:T(256)S(1)} %bitcast.221, f32[256]{0:T(256)S(1)} %get-tuple-element.131, f32[256]{0:T(256)S(1)} %get-tuple-element.130, ...), kind=kOutput, calls=%fused_computation.91 | convolution fusion | flops 807534592 | bytes 7344128 | tf_op jit(solution)/shard_map/dot_general | solution.py:153
  133.7 12.5 %collective-permute-done.21 = bf16[256,1536]{1,0:T(8,128)(2,1)S(1)} collective-permute-done((bf16[256,1536]{1,0:T(8,128)(2,1)S(1)}, bf16[256,1536]{1,0:T(8,128)(2,1)S(1)}, u32[]{:S(2)}, u32[]{:S(2)}) %collective-permute-start.21) | collective-permute-done | bytes 786464 | tf_op jit(solution)/shard_map/ppermute | solution.py:12
  147.4 3.7 %fusion.3 = bf16[256,1536]{1,0:T(8,128)(2,1)S(1)} fusion(f32[256,1536]{1,0:T(8,128)S(1)} %fusion.176, bf16[1536,1024]{1,0:T(8,128)(2,1)} %collective-permute-done.7, bf16[256,1536]{1,0:T(8,128)(2,1)S(1)} %collective-permute-done.21, bf16[256,1536]{1,0:T(8,128)(2,1)S(1)} %collective-permute-done.18, f32[256,1024]{1,0:T(8,128)S(1)} %copy-done.12, ...), kind=kOutput, calls=%fused_computation.98 | convolution fusion | flops 809500672 | bytes 8130560 | tf_op jit(solution)/shard_map/dot_general | solution.py:153
  151.2 4.9 %fusion.66 = (f32[1536]{0:T(1024)S(1)}, f32[1536]{0:T(1024)S(1)}, f32[1536]{0:T(1024)S(1)}, f32[1536]{0:T(1024)S(1)}, f32[1536]{0:T(1024)S(1)}, /*index=5*/f32[1536]{0:T(1024)S(1)}, bf16[256,1536]{1,0:T(8,128)(2,1)S(1)}) fusion(bf16[256,1536]{1,0:T(8,128)(2,1)S(1)} %bitcast.177, bf16[15,1536]{1,0:T(8,128)(2,1)S(1)} %copy-done.32, ...), kind=kOutput, calls=%fused_computation.194 | convolution fusion | flops 1226038272 | bytes 8733696 | tf_op jit(solution)/shard_map/dot_general | solution.py:171
  166.9 2.6 fusion.196
  174.9 3.2 %constant_dynamic-update-slice_fusion.8 = bf16[2048,1024]{1,0:T(8,128)(2,1)} fusion(bf16[2048,1024]{1,0:T(8,128)(2,1)} %constant_dynamic-update-slice_fusion.9, bf16[1024,1024]{1,0:T(8,128)(2,1)} %bitcast.79), kind=kLoop, calls=%fused_computation.389 | loop fusion | bytes 4194304 | tf_op jit(solution)/shard_map/concatenate | solution.py:158
  184.1 9.3 %fusion.197 = f32[1536,1024]{1,0:T(8,128)S(1)} fusion(bf16[2048,1536]{1,0:T(8,128)(2,1)S(1)} %constant_dynamic-update-slice_fusion.2, bf16[2048,1024]{1,0:T(8,128)(2,1)} %constant_dynamic-update-slice_fusion.8), kind=kOutput, calls=%fused_computation.472 | convolution fusion | flops 6442450944 | bytes 16777216 | tf_op jit(solution)/shard_map/dot_general | solution.py:159
  193.6 4.3 %collective-permute-start.43 = (bf16[384,1024]{1,0:T(8,128)(2,1)S(1)}, bf16[384,1024]{1,0:T(8,128)(2,1)S(1)}, u32[]{:S(2)}, u32[]{:S(2)}) collective-permute-start(bf16[384,1024]{1,0:T(8,128)(2,1)S(1)} %get-tuple-element.78), channel_id=1, source_target_pairs={{0,8},{1,9},{2,10},{3,11},{4,12},{5,13},{6,14},{7,15}} | collective-permute-start | bytes 2359304 | tf_op jit(solution)/shard_map/ppermute | solution.py:58
  203.3 11.0 %collective-permute-done.43 = bf16[384,1024]{1,0:T(8,128)(2,1)S(1)} collective-permute-done((bf16[384,1024]{1,0:T(8,128)(2,1)S(1)}, bf16[384,1024]{1,0:T(8,128)(2,1)S(1)}, u32[]{:S(2)}, u32[]{:S(2)}) %collective-permute-start.43) | collective-permute-done | bytes 786464 | tf_op jit(solution)/shard_map/ppermute | solution.py:58
  215.5 5.4 %collective-permute-start.44 = (bf16[384,1024]{1,0:T(8,128)(2,1)}, bf16[384,1024]{1,0:T(8,128)(2,1)}, u32[]{:S(2)}, u32[]{:S(2)}) collective-permute-start(bf16[384,1024]{1,0:T(8,128)(2,1)} %fusion.90), channel_id=1, source_target_pairs={{0,8},{8,16},{1,9},{9,17},{2,10},{10,18},{3,11},{11,19},{4,12},{12... | collective-permute-start | bytes 2359304 | tf_op jit(solution)/shard_map/ppermute | solution.py:58
  224.7 13.4 %collective-permute-done.36 = bf16[48,1536]{1,0:T(8,128)(2,1)} collective-permute-done((bf16[48,1536]{1,0:T(8,128)(2,1)}, bf16[48,1536]{1,0:T(8,128)(2,1)}, u32[]{:S(2)}, u32[]{:S(2)}) %collective-permute-start.36) | collective-permute-done | bytes 147488 | tf_op jit(solution)/shard_map/ppermute | solution.py:58
  239.9 3.0 %fusion.91 = (bf16[384,1024]{1,0:T(8,128)(2,1)S(1)}, bf16[384,1024]{1,0:T(8,128)(2,1)S(1)}) fusion(bf16[384,1024]{1,0:T(8,128)(2,1)} %collective-permute-done.44, f32[4,384,1024]{2,1,0:T(8,128)} %bitcast.183, s32[]{:T(128)S(6)} %min.30, bf16[384,1024]{1,0:T(8,128)(2,1)} %collective-permute-done.46, s32[]{:T(128)S(6)} %min.34), kind=kLoop, calls=%fused_computation.223 | loop fusion | flops 2359296 | bytes 6291464 | tf_op jit(solution)/shard_map/convert_element_type | solution.py:58
  243.8 5.6 %collective-permute-start.23 = (bf16[15,1536]{1,0:T(8,128)(2,1)S(1)}, bf16[15,1536]{1,0:T(8,128)(2,1)S(1)}, u32[]{:S(2)}, u32[]{:S(2)}) collective-permute-start(bf16[15,1536]{1,0:T(8,128)(2,1)S(1)} %get-tuple-element.97), channel_id=1, source_target_pairs={{0,8},{8,16},{16,24},{1,9},{9,17},{17,25},{2,10},{10,18},{18,26},{... | collective-permute-start | bytes 138248 | tf_op jit(solution)/shard_map/ppermute | solution.py:69
  250.7 5.5 %collective-permute-start.28 = (f32[31,1536]{1,0:T(8,128)S(1)}, f32[31,1536]{1,0:T(8,128)S(1)}, u32[]{:S(2)}, u32[]{:S(2)}) collective-permute-start(f32[31,1536]{1,0:T(8,128)S(1)} %add.637), channel_id=1, source_target_pairs={{0,16},{8,24},{16,0},{24,8},{1,17},{9,25},{17,1},{25,9},{2,18},{10... | collective-permute-start | bytes 571400 | tf_op jit(solution)/shard_map/ppermute | solution.py:190
  256.2 3.9 %collective-permute-start.37 = (bf16[48,1536]{1,0:T(8,128)(2,1)S(1)}, bf16[48,1536]{1,0:T(8,128)(2,1)S(1)}, u32[]{:S(2)}, u32[]{:S(2)}) collective-permute-start(bf16[48,1536]{1,0:T(8,128)(2,1)S(1)} %get-tuple-element.86), channel_id=1, source_target_pairs={{0,8},{8,16},{16,24},{1,9},{9,17},{17,25},{2,10},{10,18},{18,26},{... | collective-permute-start | bytes 442376 | tf_op jit(solution)/shard_map/ppermute | solution.py:58
  262.2 15.1 %collective-permute-start.45 = (bf16[384,1024]{1,0:T(8,128)(2,1)S(1)}, bf16[384,1024]{1,0:T(8,128)(2,1)S(1)}, u32[]{:S(2)}, u32[]{:S(2)}) collective-permute-start(bf16[384,1024]{1,0:T(8,128)(2,1)S(1)} %get-tuple-element.76), channel_id=1, source_target_pairs={{0,8},{8,16},{16,24},{1,9},{9,17},{17,25},{2,10},{10,18},{18,26},{... | collective-permute-start | bytes 2359304 | tf_op jit(solution)/shard_map/ppermute | solution.py:58
  278.9 8.0 %fusion.158 = bf16[1,256,1536]{2,1,0:T(8,128)(2,1)} fusion(bf16[256,1536]{1,0:T(8,128)(2,1)S(1)} %get-tuple-element.165, bf16[15,1536]{1,0:T(8,128)(2,1)S(1)} %collective-permute-done.23, f32[1536]{0:T(1024)S(1)} %copy-done.88, f32[1536]{0:T(1024)S(1)} %copy-done.90, f32[1536]{0:T(1024)S(1)} %get-tuple-element.36, f32[1536]{0:T(1024)S(1)} %copy-done.34, ...), kind=kLoop, calls=%fused_computation.348 | loop fusion | flops 72744960 | bytes 2641920 | tf_op jit(solution)/shard_map/broadcast_in_dim | solution.py:194
  288.4 2.8 collective-permute-done.48
  (453 shorter events, 110.6 us)
Async XLA Ops:
  0.6 22.5 %collective-permute-start.3 = (bf16[192,1536]{1,0:T(8,128)(2,1)}, bf16[192,1536]{1,0:T(8,128)(2,1)S(1)}, u32[]{:S(2)}, u32[]{:S(2)}) collective-permute-start(bf16[192,1536]{1,0:T(8,128)(2,1)} %param.8), channel_id=1, source_target_pairs={{0,4},{1,5},{2,6},{3,7},{4,0},{5,1},{6,2},{7,3},{8,12},{9,13},{10,... | collective-permute-start | bytes 1769480 | tf_op jit(solution)/shard_map/ppermute | solution.py:12
  3.7 20.8 %collective-permute-start.2 = (bf16[192,1536]{1,0:T(8,128)(2,1)}, bf16[192,1536]{1,0:T(8,128)(2,1)S(1)}, u32[]{:S(2)}, u32[]{:S(2)}) collective-permute-start(bf16[192,1536]{1,0:T(8,128)(2,1)} %param.8), channel_id=1, source_target_pairs={{0,2},{1,3},{2,0},{3,1},{4,6},{5,7},{6,4},{7,5},{8,10},{9,11},{10,... | collective-permute-start | bytes 1769480 | tf_op jit(solution)/shard_map/ppermute | solution.py:12
  7.7 17.4 %collective-permute-start.16 = (f32[2,256]{1,0:T(2,128)S(1)}, f32[2,256]{1,0:T(2,128)S(1)}, u32[]{:S(2)}, u32[]{:S(2)}) collective-permute-start(f32[2,256]{1,0:T(2,128)S(1)} %pad_maximum_fusion.12), channel_id=1, source_target_pairs={{0,6},{1,7},{2,4},{3,5},{4,2},{5,3},{6,0},{7,1},{8,14},{9,15},{10,... | collective-permute-start | bytes 6152 | tf_op jit(solution)/shard_map/ppermute | solution.py:12
  9.2 18.6 %collective-permute-start.15 = (f32[2,256]{1,0:T(2,128)S(1)}, f32[2,256]{1,0:T(2,128)S(1)}, u32[]{:S(2)}, u32[]{:S(2)}) collective-permute-start(f32[2,256]{1,0:T(2,128)S(1)} %pad_maximum_fusion.12), channel_id=1, source_target_pairs={{0,2},{1,3},{2,0},{3,1},{4,6},{5,7},{6,4},{7,5},{8,10},{9,11},{10,... | collective-permute-start | bytes 6152 | tf_op jit(solution)/shard_map/ppermute | solution.py:12
  19.0 15.8 %collective-permute-start = (bf16[15,1536]{1,0:T(8,128)(2,1)S(1)}, bf16[15,1536]{1,0:T(8,128)(2,1)S(1)}, u32[]{:S(2)}, u32[]{:S(2)}) collective-permute-start(bf16[15,1536]{1,0:T(8,128)(2,1)S(1)} %get-tuple-element.100), channel_id=1, source_target_pairs={{0,8},{8,16},{16,24},{1,9},{9,17},{17,25},{2,10},{10,18},{18,26},{... | collective-permute-start | bytes 138248 | tf_op jit(solution)/shard_map/ppermute | solution.py:69
  27.7 35.4 %collective-permute-start.7 = (bf16[1536,1024]{1,0:T(8,128)(2,1)}, bf16[1536,1024]{1,0:T(8,128)(2,1)}, u32[]{:S(2)}, u32[]{:S(2)}) collective-permute-start(bf16[1536,1024]{1,0:T(8,128)(2,1)} %param.9), channel_id=1, source_target_pairs={{0,1},{1,0},{2,3},{3,2},{4,5},{5,4},{6,7},{7,6},{8,9},{9,8},{10,11... | collective-permute-start | bytes 9437192 | tf_op jit(solution)/shard_map/ppermute | solution.py:12
  45.0 121.9 %collective-permute-start.29 = (bf16[4,4,48,256]{3,2,1,0:T(8,128)(2,1)}, bf16[4,4,48,256]{3,2,1,0:T(8,128)(2,1)}, u32[]{:S(2)}, u32[]{:S(2)}) collective-permute-start(bf16[4,4,48,256]{3,2,1,0:T(8,128)(2,1)} %get-tuple-element.91), channel_id=1, source_target_pairs={{0,1},{1,0},{2,3},{3,2},{4,5},{5,4},{6,7},{7,6},{8,9},{9,8},{10,11... | collective-permute-start | bytes 1179656 | tf_op jit(solution)/shard_map/ppermute | solution.py:12
  60.0 19.5 %collective-permute-start.8 = (bf16[256,1536]{1,0:T(8,128)(2,1)S(1)}, bf16[256,1536]{1,0:T(8,128)(2,1)S(1)}, u32[]{:S(2)}, u32[]{:S(2)}) collective-permute-start(bf16[256,1536]{1,0:T(8,128)(2,1)S(1)} %get-tuple-element.160), channel_id=1, source_target_pairs={{0,2},{1,3},{2,0},{3,1},{4,6},{5,7},{6,4},{7,5},{8,10},{9,11},{10,... | collective-permute-start | bytes 2359304 | tf_op jit(solution)/shard_map/ppermute | solution.py:12
  61.2 19.5 %collective-permute-start.9 = (bf16[256,1536]{1,0:T(8,128)(2,1)S(1)}, bf16[256,1536]{1,0:T(8,128)(2,1)S(1)}, u32[]{:S(2)}, u32[]{:S(2)}) collective-permute-start(bf16[256,1536]{1,0:T(8,128)(2,1)S(1)} %get-tuple-element.160), channel_id=1, source_target_pairs={{0,4},{1,5},{2,6},{3,7},{4,0},{5,1},{6,2},{7,3},{8,12},{9,13},{10,... | collective-permute-start | bytes 2359304 | tf_op jit(solution)/shard_map/ppermute | solution.py:12
  105.6 76.4 %collective-permute-start.41 = (bf16[4,256,1536]{2,1,0:T(8,128)(2,1)}, bf16[4,256,1536]{2,1,0:T(8,128)(2,1)}, u32[]{:S(2)}, u32[]{:S(2)}) collective-permute-start(bf16[4,256,1536]{2,1,0:T(8,128)(2,1)} %pad_maximum_fusion), channel_id=1, source_target_pairs={{0,1},{1,0},{2,3},{3,2},{4,5},{5,4},{6,7},{7,6},{8,9},{9,8},{10,11... | collective-permute-start | bytes 9437192 | tf_op jit(solution)/shard_map/ppermute | solution.py:12
  125.8 49.1 %collective-permute-start.42 = (bf16[4,256,1024]{2,1,0:T(8,128)(2,1)}, bf16[4,256,1024]{2,1,0:T(8,128)(2,1)}, u32[]{:S(2)}, u32[]{:S(2)}) collective-permute-start(bf16[4,256,1024]{2,1,0:T(8,128)(2,1)} %pad_maximum_fusion.2), channel_id=1, source_target_pairs={{0,1},{1,0},{2,3},{3,2},{4,5},{5,4},{6,7},{7,6},{8,9},{9,8},{10,11... | collective-permute-start | bytes 6291464 | tf_op jit(solution)/shard_map/ppermute | solution.py:12
  127.6 18.6 %collective-permute-start.21 = (bf16[256,1536]{1,0:T(8,128)(2,1)S(1)}, bf16[256,1536]{1,0:T(8,128)(2,1)S(1)}, u32[]{:S(2)}, u32[]{:S(2)}) collective-permute-start(bf16[256,1536]{1,0:T(8,128)(2,1)S(1)} %pad_maximum_fusion.8), channel_id=1, source_target_pairs={{0,4},{1,5},{2,6},{3,7},{4,0},{5,1},{6,2},{7,3},{8,12},{9,13},{10,... | collective-permute-start | bytes 2359304 | tf_op jit(solution)/shard_map/ppermute | solution.py:12
  129.0 18.3 %collective-permute-start.18 = (bf16[256,1536]{1,0:T(8,128)(2,1)S(1)}, bf16[256,1536]{1,0:T(8,128)(2,1)S(1)}, u32[]{:S(2)}, u32[]{:S(2)}) collective-permute-start(bf16[256,1536]{1,0:T(8,128)(2,1)S(1)} %pad_maximum_fusion.7), channel_id=1, source_target_pairs={{0,2},{1,3},{2,0},{3,1},{4,6},{5,7},{6,4},{7,5},{8,10},{9,11},{10,... | collective-permute-start | bytes 2359304 | tf_op jit(solution)/shard_map/ppermute | solution.py:12
  151.1 15.9 %collective-permute-start.30 = (bf16[256,1536]{1,0:T(8,128)(2,1)S(1)}, bf16[256,1536]{1,0:T(8,128)(2,1)}, u32[]{:S(2)}, u32[]{:S(2)}) collective-permute-start(bf16[256,1536]{1,0:T(8,128)(2,1)S(1)} %fusion.3), channel_id=1, source_target_pairs={{0,1},{1,0},{2,3},{3,2},{4,5},{5,4},{6,7},{7,6},{8,9},{9,8},{10,11... | collective-permute-start | bytes 2359304 | tf_op jit(solution)/shard_map/ppermute | solution.py:12
  173.7 49.9 %collective-permute-start.26 = (f32[31,1536]{1,0:T(8,128)}, f32[31,1536]{1,0:T(8,128)}, u32[]{:S(2)}, u32[]{:S(2)}) collective-permute-start(f32[31,1536]{1,0:T(8,128)} %add.635), channel_id=1, source_target_pairs={{0,4},{1,5},{2,6},{3,7},{4,0},{5,1},{6,2},{7,3},{8,12},{9,13},{10,... | collective-permute-start | bytes 571400 | tf_op jit(solution)/shard_map/ppermute | solution.py:12
  179.9 18.1 %collective-permute-start.34 = (bf16[192,1536]{1,0:T(8,128)(2,1)S(1)}, bf16[192,1536]{1,0:T(8,128)(2,1)S(1)}, u32[]{:S(2)}, u32[]{:S(2)}) collective-permute-start(bf16[192,1536]{1,0:T(8,128)(2,1)S(1)} %pad_maximum_fusion.11), channel_id=1, source_target_pairs={{0,4},{1,5},{2,6},{3,7},{4,0},{5,1},{6,2},{7,3},{8,12},{9,13},{10,... | collective-permute-start | bytes 1769480 | tf_op jit(solution)/shard_map/ppermute | solution.py:12
  181.0 17.0 %collective-permute-start.32 = (bf16[192,1536]{1,0:T(8,128)(2,1)S(1)}, bf16[192,1536]{1,0:T(8,128)(2,1)S(1)}, u32[]{:S(2)}, u32[]{:S(2)}) collective-permute-start(bf16[192,1536]{1,0:T(8,128)(2,1)S(1)} %pad_maximum_fusion.10), channel_id=1, source_target_pairs={{0,2},{1,3},{2,0},{3,1},{4,6},{5,7},{6,4},{7,5},{8,10},{9,11},{10,... | collective-permute-start | bytes 1769480 | tf_op jit(solution)/shard_map/ppermute | solution.py:12
  193.6 20.7 %collective-permute-start.43 = (bf16[384,1024]{1,0:T(8,128)(2,1)S(1)}, bf16[384,1024]{1,0:T(8,128)(2,1)S(1)}, u32[]{:S(2)}, u32[]{:S(2)}) collective-permute-start(bf16[384,1024]{1,0:T(8,128)(2,1)S(1)} %get-tuple-element.78), channel_id=1, source_target_pairs={{0,8},{1,9},{2,10},{3,11},{4,12},{5,13},{6,14},{7,15}} | collective-permute-start | bytes 2359304 | tf_op jit(solution)/shard_map/ppermute | solution.py:58
  198.9 22.0 %collective-permute-start.35 = (bf16[48,1536]{1,0:T(8,128)(2,1)S(1)}, bf16[48,1536]{1,0:T(8,128)(2,1)S(1)}, u32[]{:S(2)}, u32[]{:S(2)}) collective-permute-start(bf16[48,1536]{1,0:T(8,128)(2,1)S(1)} %get-tuple-element.88), channel_id=1, source_target_pairs={{0,8},{1,9},{2,10},{3,11},{4,12},{5,13},{6,14},{7,15}} | collective-permute-start | bytes 442376 | tf_op jit(solution)/shard_map/ppermute | solution.py:58
  200.5 24.2 %collective-permute-start.38 = (bf16[48,1536]{1,0:T(8,128)(2,1)}, bf16[48,1536]{1,0:T(8,128)(2,1)}, u32[]{:S(2)}, u32[]{:S(2)}) collective-permute-start(bf16[48,1536]{1,0:T(8,128)(2,1)} %get-tuple-element.89), channel_id=1, source_target_pairs={{24,16},{25,17},{26,18},{27,19},{28,20},{29,21},{30,22},{31,23}} | collective-permute-start | bytes 442376 | tf_op jit(solution)/shard_map/ppermute | solution.py:59
  201.8 38.1 %collective-permute-start.46 = (bf16[384,1024]{1,0:T(8,128)(2,1)S(1)}, bf16[384,1024]{1,0:T(8,128)(2,1)}, u32[]{:S(2)}, u32[]{:S(2)}) collective-permute-start(bf16[384,1024]{1,0:T(8,128)(2,1)S(1)} %get-tuple-element.79), channel_id=1, source_target_pairs={{24,16},{25,17},{26,18},{27,19},{28,20},{29,21},{30,22},{31,23}} | collective-permute-start | bytes 2359304 | tf_op jit(solution)/shard_map/ppermute | solution.py:59
  215.5 24.4 %collective-permute-start.44 = (bf16[384,1024]{1,0:T(8,128)(2,1)}, bf16[384,1024]{1,0:T(8,128)(2,1)}, u32[]{:S(2)}, u32[]{:S(2)}) collective-permute-start(bf16[384,1024]{1,0:T(8,128)(2,1)} %fusion.90), channel_id=1, source_target_pairs={{0,8},{8,16},{1,9},{9,17},{2,10},{10,18},{3,11},{11,19},{4,12},{12... | collective-permute-start | bytes 2359304 | tf_op jit(solution)/shard_map/ppermute | solution.py:58
  221.6 16.5 %collective-permute-start.36 = (bf16[48,1536]{1,0:T(8,128)(2,1)}, bf16[48,1536]{1,0:T(8,128)(2,1)}, u32[]{:S(2)}, u32[]{:S(2)}) collective-permute-start(bf16[48,1536]{1,0:T(8,128)(2,1)} %fusion.163), channel_id=1, source_target_pairs={{0,8},{8,16},{1,9},{9,17},{2,10},{10,18},{3,11},{11,19},{4,12},{12... | collective-permute-start | bytes 442376 | tf_op jit(solution)/shard_map/ppermute | solution.py:58
  224.6 26.1 %collective-permute-start.27 = (f32[31,1536]{1,0:T(8,128)S(1)}, f32[31,1536]{1,0:T(8,128)S(1)}, u32[]{:S(2)}, u32[]{:S(2)}) collective-permute-start(f32[31,1536]{1,0:T(8,128)S(1)} %add.636), channel_id=1, source_target_pairs={{0,8},{8,0},{16,24},{24,16},{1,9},{9,1},{17,25},{25,17},{2,10},{10... | collective-permute-start | bytes 571400 | tf_op jit(solution)/shard_map/ppermute | solution.py:190
  239.2 17.0 %collective-permute-start.39 = (bf16[48,1536]{1,0:T(8,128)(2,1)S(1)}, bf16[48,1536]{1,0:T(8,128)(2,1)S(1)}, u32[]{:S(2)}, u32[]{:S(2)}) collective-permute-start(bf16[48,1536]{1,0:T(8,128)(2,1)S(1)} %get-tuple-element.87), channel_id=1, source_target_pairs={{16,8},{24,16},{17,9},{25,17},{18,10},{26,18},{19,11},{27,19},{20,... | collective-permute-start | bytes 442376 | tf_op jit(solution)/shard_map/ppermute | solution.py:59
  242.9 17.5 %collective-permute-start.47 = (bf16[384,1024]{1,0:T(8,128)(2,1)S(1)}, bf16[384,1024]{1,0:T(8,128)(2,1)S(1)}, u32[]{:S(2)}, u32[]{:S(2)}) collective-permute-start(bf16[384,1024]{1,0:T(8,128)(2,1)S(1)} %get-tuple-element.77), channel_id=1, source_target_pairs={{16,8},{24,16},{17,9},{25,17},{18,10},{26,18},{19,11},{27,19},{20,... | collective-permute-start | bytes 2359304 | tf_op jit(solution)/shard_map/ppermute | solution.py:59
  243.8 18.4 %collective-permute-start.23 = (bf16[15,1536]{1,0:T(8,128)(2,1)S(1)}, bf16[15,1536]{1,0:T(8,128)(2,1)S(1)}, u32[]{:S(2)}, u32[]{:S(2)}) collective-permute-start(bf16[15,1536]{1,0:T(8,128)(2,1)S(1)} %get-tuple-element.97), channel_id=1, source_target_pairs={{0,8},{8,16},{16,24},{1,9},{9,17},{17,25},{2,10},{10,18},{18,26},{... | collective-permute-start | bytes 138248 | tf_op jit(solution)/shard_map/ppermute | solution.py:69
  249.4 27.9 %collective-permute-start.22 = (bf16[15,1536]{1,0:T(8,128)(2,1)S(1)}, bf16[15,1536]{1,0:T(8,128)(2,1)S(1)}, u32[]{:S(2)}, u32[]{:S(2)}) collective-permute-start(bf16[15,1536]{1,0:T(8,128)(2,1)S(1)} %get-tuple-element.96), channel_id=1, source_target_pairs={{8,0},{16,8},{24,16},{9,1},{17,9},{25,17},{10,2},{18,10},{26,18},{... | collective-permute-start | bytes 138248 | tf_op jit(solution)/shard_map/ppermute | solution.py:70
  250.7 36.2 %collective-permute-start.28 = (f32[31,1536]{1,0:T(8,128)S(1)}, f32[31,1536]{1,0:T(8,128)S(1)}, u32[]{:S(2)}, u32[]{:S(2)}) collective-permute-start(f32[31,1536]{1,0:T(8,128)S(1)} %add.637), channel_id=1, source_target_pairs={{0,16},{8,24},{16,0},{24,8},{1,17},{9,25},{17,1},{25,9},{2,18},{10... | collective-permute-start | bytes 571400 | tf_op jit(solution)/shard_map/ppermute | solution.py:190
  256.2 31.4 %collective-permute-start.37 = (bf16[48,1536]{1,0:T(8,128)(2,1)S(1)}, bf16[48,1536]{1,0:T(8,128)(2,1)S(1)}, u32[]{:S(2)}, u32[]{:S(2)}) collective-permute-start(bf16[48,1536]{1,0:T(8,128)(2,1)S(1)} %get-tuple-element.86), channel_id=1, source_target_pairs={{0,8},{8,16},{16,24},{1,9},{9,17},{17,25},{2,10},{10,18},{18,26},{... | collective-permute-start | bytes 442376 | tf_op jit(solution)/shard_map/ppermute | solution.py:58
  260.5 27.2 %collective-permute-start.40 = (bf16[48,1536]{1,0:T(8,128)(2,1)S(1)}, bf16[48,1536]{1,0:T(8,128)(2,1)S(1)}, u32[]{:S(2)}, u32[]{:S(2)}) collective-permute-start(bf16[48,1536]{1,0:T(8,128)(2,1)S(1)} %fusion.162), channel_id=1, source_target_pairs={{8,0},{16,8},{24,16},{9,1},{17,9},{25,17},{10,2},{18,10},{26,18},{... | collective-permute-start | bytes 442376 | tf_op jit(solution)/shard_map/ppermute | solution.py:59
  262.2 26.2 %collective-permute-start.45 = (bf16[384,1024]{1,0:T(8,128)(2,1)S(1)}, bf16[384,1024]{1,0:T(8,128)(2,1)S(1)}, u32[]{:S(2)}, u32[]{:S(2)}) collective-permute-start(bf16[384,1024]{1,0:T(8,128)(2,1)S(1)} %get-tuple-element.76), channel_id=1, source_target_pairs={{0,8},{8,16},{16,24},{1,9},{9,17},{17,25},{2,10},{10,18},{18,26},{... | collective-permute-start | bytes 2359304 | tf_op jit(solution)/shard_map/ppermute | solution.py:58
  (134 other events, 1251.2 us)

commit v2 on v1

v2 whole, which is shorter than its diff:
```python
import jax
import jax.numpy as jnp
from jax import lax
from jax.experimental import pallas as pl
from jax.experimental.pallas import tpu as pltpu
from jax.sharding import PartitionSpec as P

BF = jnp.bfloat16
F32 = jnp.float32


def swap(value, mask):
    count = lax.axis_size("fsdp")
    return lax.ppermute(value, "fsdp", [(i, i ^ mask) for i in range(count)])


VMEM_BYTES = 56 * 2**20
CHEAP = pl.CostEstimate(flops=0, bytes_accessed=0, transcendentals=0)


def halves_to_forward(from_x, from_y, *earlier):
    rows, width = from_x.shape
    half = rows // 2

    def kernel(x_ref, y_ref, *refs):
        low_ref, high_ref = refs[len(earlier) :]
        low_ref[...] = x_ref[...]
        high_ref[...] = y_ref[...]

    made = jax.ShapeDtypeStruct((half, width), from_x.dtype)
    whole = pl.BlockSpec((half, width), lambda j: (0, 0))
    return pl.pallas_call(
        kernel,
        grid=(1,),
        out_shape=(made, made),
        in_specs=[
            pl.BlockSpec((half, width), lambda j: (0, 0)),
            pl.BlockSpec((half, width), lambda j: (1, 0)),
        ]
        + [pl.BlockSpec(memory_space=pl.ANY)] * len(earlier),
        out_specs=(whole, whole),
        compiler_params=pltpu.CompilerParams(vmem_limit_bytes=VMEM_BYTES),
        cost_estimate=CHEAP,
        name="forward",
    )(from_x, from_y, *earlier)


def near_and_forward(block, from_x, from_y, *earlier):
    rows, width = block.shape
    half = rows // 2

    def kernel(own_ref, x_ref, y_ref, *refs):
        near_ref, low_ref, high_ref = refs[len(earlier) :]
        near_ref[:rows, :] = own_ref[...]
        near_ref[rows : 2 * rows, :] = x_ref[...]
        near_ref[2 * rows :, :] = y_ref[...]
        low_ref[...] = x_ref[:half, :]
        high_ref[...] = y_ref[half:, :]

    def spec(count):
        return pl.BlockSpec((count, width), lambda j: (0, 0))

    made = jax.ShapeDtypeStruct((half, width), block.dtype)
    return pl.pallas_call(
        kernel,
        grid=(1,),
        out_shape=(jax.ShapeDtypeStruct((3 * rows, width), block.dtype), made, made),
        in_specs=[spec(rows)] * 3 + [pl.BlockSpec(memory_space=pl.ANY)] * len(earlier),
        out_specs=(spec(3 * rows), spec(half), spec(half)),
        compiler_params=pltpu.CompilerParams(vmem_limit_bytes=VMEM_BYTES),
        cost_estimate=CHEAP,
        name="near_and_forward",
    )(block, from_x, from_y, *earlier)


def stack_halves(low, high, *earlier):
    half, width = low.shape

    def kernel(low_ref, high_ref, *refs):
        refs[-1][:half, :] = low_ref[...]
        refs[-1][half:, :] = high_ref[...]

    part = pl.BlockSpec((half, width), lambda j: (0, 0))
    return pl.pallas_call(
        kernel,
        grid=(1,),
        out_shape=jax.ShapeDtypeStruct((2 * half, width), low.dtype),
        in_specs=[part, part] + [pl.BlockSpec(memory_space=pl.ANY)] * len(earlier),
        out_specs=pl.BlockSpec((2 * half, width), lambda j: (0, 0)),
        compiler_params=pltpu.CompilerParams(vmem_limit_bytes=VMEM_BYTES),
        cost_estimate=CHEAP,
        name="stack_halves",
    )(low, high, *earlier)


def gather_rows(block, earlier, between):
    chips = lax.axis_size("fsdp") // 2
    if chips != 4:
        near = jnp.concatenate([block] + [swap(block, 2 * m) for m in range(1, chips - 1)])
        between(near)
        return near, swap(block, 2 * (chips - 1))
    near, to_y, to_x = near_and_forward(block, swap(block, 2), swap(block, 4), *earlier)
    low = swap(to_y, 4)
    high = swap(to_x, 2)
    return near, stack_halves(low, high, *between(near))


def join_halves(near_y, near_x, low, high, earlier, passed=()):
    half, width = low.shape
    rows = 2 * half
    tile = 512 if width % 512 == 0 else width
    count = len(passed)

    def kernel(y_ref, x_ref, low_ref, high_ref, *refs):
        to_y_ref, to_x_ref = refs[len(earlier) + count : len(earlier) + count + 2]
        to_y_ref[:half, :] = (y_ref[:half, :] + low_ref[...].astype(F32)).astype(BF)
        to_y_ref[half:, :] = y_ref[half:, :].astype(BF)
        to_x_ref[:half, :] = x_ref[:half, :].astype(BF)
        to_x_ref[half:, :] = (x_ref[half:, :] + high_ref[...].astype(F32)).astype(BF)
        for n in range(count):
            refs[len(earlier) + count + 2 + n][...] = refs[n][...]

    def block(size, index):
        return pl.BlockSpec((size, tile), lambda j: (index, j))

    made = jax.ShapeDtypeStruct((rows, width), BF)
    return pl.pallas_call(
        kernel,
        grid=(width // tile,),
        out_shape=(made, made)
        + tuple(jax.ShapeDtypeStruct((size, width), value.dtype) for value, size, _ in passed),
        in_specs=[block(rows, near_y[1]), block(rows, near_x[1]), block(half, 0), block(half, 0)]
        + [block(size, index) for _, size, index in passed]
        + [pl.BlockSpec(memory_space=pl.ANY)] * len(earlier),
        out_specs=(block(rows, 0), block(rows, 0)) + tuple(block(size, 0) for _, size, _ in passed),
        compiler_params=pltpu.CompilerParams(vmem_limit_bytes=VMEM_BYTES),
        cost_estimate=CHEAP,
        name="join_halves",
    )(near_y[0], near_x[0], low, high, *[value for value, _, _ in passed], *earlier)


def gather_pieces(block, *earlier):
    chips = lax.axis_size("fsdp") // 2
    if chips != 4:
        return [(block, 0, 0)] + [(swap(block, 2 * m), m, 0) for m in range(1, chips)]
    half = block.shape[0] // 2
    from_x = swap(block, 2)
    from_y = swap(block, 4)
    if earlier:
        to_y, to_x = halves_to_forward(from_x, from_y, *earlier)
    else:
        to_y, to_x = from_x[:half], from_y[half:]
    far_low = swap(to_y, 4)
    far_high = swap(to_x, 2)
    return [(block, 0, 0), (from_x, 1, 0), (from_y, 2, 0), (far_low, 3, 0), (far_high, 3, half)]


def finish_sum(own, recv_x, recv_y, index, passed, dtype, *earlier):
    rows, width = recv_x.shape
    tile = 512 if width % 512 == 0 else width
    count = len(passed)

    def kernel(own_ref, x_ref, y_ref, *refs):
        outs = refs[count + len(earlier) :]
        total = own_ref[...] + x_ref[...].astype(F32) + y_ref[...].astype(F32)
        outs[0][...] = total.astype(dtype)
        for n in range(count):
            outs[1 + n][...] = refs[n][...]

    def block(size, at):
        return pl.BlockSpec((size, tile), lambda j: (at, j))

    return pl.pallas_call(
        kernel,
        grid=(width // tile,),
        out_shape=(jax.ShapeDtypeStruct((rows, width), dtype),)
        + tuple(jax.ShapeDtypeStruct(v.shape, v.dtype) for v in passed),
        in_specs=[block(rows, index), block(rows, 0), block(rows, 0)]
        + [block(v.shape[0], 0) for v in passed]
        + [pl.BlockSpec(memory_space=pl.ANY)] * len(earlier),
        out_specs=(block(rows, 0),) + tuple(block(v.shape[0], 0) for v in passed),
        compiler_params=pltpu.CompilerParams(vmem_limit_bytes=VMEM_BYTES),
        cost_estimate=CHEAP,
        name="finish_sum",
    )(own, recv_x, recv_y, *passed, *earlier)


def scatter_and_finish(part, near, chips, passed, last, dtype):
    if chips != 4:
        total = part(0)
        for m in range(1, chips):
            total = total + swap(part(m).astype(BF), 2 * m).astype(F32)
        kept = [v[size * index : size * (index + 1)] for v, size, index in passed]
        return total.astype(dtype), kept, last(kept, total)[0]
    far = part(3).astype(BF)
    half = far.shape[0] // 2
    low = swap(far[:half], 2)
    high = swap(far[half:], 4)
    own, index = near(0)
    to_y, to_x, *kept = join_halves(near(2), near(1), low, high, (own,), passed)
    recv_x, recv_y = swap(to_x, 2), swap(to_y, 4)
    handed, waited = last(kept, to_x)
    total, *handed = finish_sum(own, recv_x, recv_y, index, handed, dtype, *waited)
    return total, kept, handed


def project(gated, frames, pieces, places):
    rows, width = gated.shape
    count = len(pieces)
    tile = 512

    def kernel(*refs):
        place = refs[0]
        gated_ref, frames_ref = refs[1:3]
        piece_refs = refs[3 : 3 + count]
        mixed_ref, full_ref, held, sems, out_sem = refs[3 + count :]
        copies = []
        for n in range(count):
            size = piece_refs[n].shape[0]
            start = pl.multiple_of(place[n], 16)
            copy = pltpu.make_async_copy(piece_refs[n], held.at[pl.ds(start, size)], sems.at[n])
            copy.start()
            copies.append(copy)
        for copy in copies:
            copy.wait()
        out = pltpu.make_async_copy(held, full_ref, out_sem)
        out.start()
        for col in range(0, width, tile):
            at = slice(col, col + tile)
            proj = jnp.dot(gated_ref[...], held[:, at], preferred_element_type=F32)
            mixed_ref[:, at] = (frames_ref[:, at].astype(F32) + proj).astype(BF)
        out.wait()

    vmem = pl.BlockSpec(memory_space=pltpu.VMEM)
    hbm = pl.BlockSpec(memory_space=pl.ANY)
    return pl.pallas_call(
        kernel,
        out_shape=(
            jax.ShapeDtypeStruct((rows, width), BF),
            jax.ShapeDtypeStruct((width, width), BF),
        ),
        in_specs=[pl.BlockSpec(memory_space=pltpu.SMEM), vmem, vmem] + [hbm] * count,
        out_specs=(vmem, hbm),
        scratch_shapes=[
            pltpu.VMEM((width, width), BF),
            pltpu.SemaphoreType.DMA((count,)),
            pltpu.SemaphoreType.DMA,
        ],
        compiler_params=pltpu.CompilerParams(vmem_limit_bytes=VMEM_BYTES),
        cost_estimate=pl.CostEstimate(
            flops=2 * rows * width * width, bytes_accessed=4 * width * width, transcendentals=0
        ),
        name="project",
    )(places, gated, frames, *pieces)


def line_scatter(term, kind):
    count = lax.axis_size("seq")
    here = lax.axis_index("seq")

    def block(index):
        index = jnp.clip(index, 0, count - 1)
        return lax.dynamic_index_in_dim(term, index, 0, keepdims=False).astype(F32)

    up = down = None
    for step in range(1, count):
        to_up = block(here + count - step)
        to_down = block(here - count + step)
        if up is not None:
            to_up = to_up + up.astype(F32)
            to_down = to_down + down.astype(F32)
        up = lax.ppermute(to_up.astype(kind), "seq", [(i, i + 1) for i in range(step)])
        down = lax.ppermute(
            to_down.astype(kind), "seq", [(i, i - 1) for i in range(count - step, count)]
        )
    return block(here) + up.astype(F32) + down.astype(F32)


def halo_edges(first, last):
    count = lax.axis_size("seq")
    forward = [(i, i + 1) for i in range(count - 1)]
    backward = [(i + 1, i) for i in range(count - 1)]
    return lax.ppermute(last, "seq", forward), lax.ppermute(first, "seq", backward)


EDGE = 16
LOGIT_TILE = 512
LANES = 128


def channel_tile(width):
    return 256 if width % 256 == 0 else width


def fill(pad_ref, low_ref, mid_ref, high_ref):
    rows = mid_ref.shape[0]
    pad_ref[:EDGE, :] = low_ref[...].astype(F32)
    pad_ref[EDGE : EDGE + rows, :] = mid_ref[...].astype(F32)
    pad_ref[EDGE + rows :, :] = high_ref[...].astype(F32)


def tap_specs(rows, tile):
    edge = pl.BlockSpec((EDGE, tile), lambda j: (0, j))
    return edge, pl.BlockSpec((rows, tile), lambda j: (0, j))


def convolve(low, frames, high, taps):
    rows, width = frames.shape
    count = taps.shape[0]
    first = EDGE - (count - 1) // 2
    tile = channel_tile(width)

    def kernel(
        low_ref, mid_ref, high_ref, taps_ref, conv_ref, gated_ref, turned_ref, mark_ref, pad_ref
    ):
        mark_ref[...] = jnp.zeros_like(mark_ref)
        fill(pad_ref, low_ref, mid_ref, high_ref)
        for lane in range(0, tile, LANES):
            at = slice(lane, lane + LANES)
            conv = jnp.zeros((rows, LANES), F32)
            for k in range(count):
                conv = conv + taps_ref[k : k + 1, at] * pad_ref[first + k : first + k + rows, at]
            conv_ref[:, at] = conv
            gated = conv / (1.0 + jnp.exp(-conv))
            gated_ref[:, at] = gated.astype(BF)
            turned_ref[at, :] = gated.T.astype(BF)

    edge, body_spec = tap_specs(rows, tile)
    return pl.pallas_call(
        kernel,
        grid=(width // tile,),
        out_shape=(
            jax.ShapeDtypeStruct((rows, width), F32),
            jax.ShapeDtypeStruct((rows, width), BF),
            jax.ShapeDtypeStruct((width, rows), BF),
            jax.ShapeDtypeStruct((8, LANES), F32),
        ),
        in_specs=[edge, body_spec, edge, pl.BlockSpec((count, tile), lambda j: (0, j))],
        out_specs=(
            body_spec,
            body_spec,
            pl.BlockSpec((tile, rows), lambda j: (j, 0)),
            pl.BlockSpec((8, LANES), lambda j: (0, 0)),
        ),
        scratch_shapes=[pltpu.VMEM((rows + 2 * EDGE, tile), F32)],
        compiler_params=pltpu.CompilerParams(vmem_limit_bytes=VMEM_BYTES),
        cost_estimate=CHEAP,
        name="convolve",
    )(low, frames, high, taps)


def convolve_back(low, dconv, high, taps, dmixed):
    rows, width = dconv.shape
    count = taps.shape[0]
    last = EDGE + (count - 1) // 2
    tile = channel_tile(width)

    def kernel(low_ref, mid_ref, high_ref, taps_ref, dmixed_ref, out_ref, pad_ref):
        fill(pad_ref, low_ref, mid_ref, high_ref)
        for lane in range(0, tile, LANES):
            at = slice(lane, lane + LANES)
            back = dmixed_ref[:, at].astype(F32)
            for k in range(count):
                back = back + taps_ref[k : k + 1, at] * pad_ref[last - k : last - k + rows, at]
            out_ref[:, at] = back.astype(BF)

    edge, body_spec = tap_specs(rows, tile)
    return pl.pallas_call(
        kernel,
        grid=(width // tile,),
        out_shape=jax.ShapeDtypeStruct((rows, width), BF),
        in_specs=[edge, body_spec, edge, pl.BlockSpec((count, tile), lambda j: (0, j)), body_spec],
        out_specs=body_spec,
        scratch_shapes=[pltpu.VMEM((rows + 2 * EDGE, tile), F32)],
        compiler_params=pltpu.CompilerParams(vmem_limit_bytes=VMEM_BYTES),
        cost_estimate=CHEAP,
        name="convolve_back",
    )(low, dconv, high, taps, dmixed)


def gate_back(dmixed, pw_full, conv, low, frames, high, count, earlier):
    rows, width = dmixed.shape
    first = EDGE - (count - 1) // 2
    tile = channel_tile(width)
    held = -(-count // 16) * 16

    def kernel(
        dmixed_ref, pw_ref, conv_ref, low_ref, mid_ref, high_ref, _, dconv_ref, taps_ref, pad_ref
    ):
        fill(pad_ref, low_ref, mid_ref, high_ref)
        dgated = lax.dot_general(
            dmixed_ref[...], pw_ref[...], (((1,), (1,)), ((), ())), preferred_element_type=F32
        )
        conv = conv_ref[...]
        sig = 1.0 / (1.0 + jnp.exp(-conv))
        dconv_ref[...] = (dgated * sig * (1.0 + conv * (1.0 - sig))).astype(BF)
        taps_ref[...] = jnp.zeros_like(taps_ref)
        for lane in range(0, tile, LANES):
            at = slice(lane, lane + LANES)
            dconv = dconv_ref[:, at].astype(F32)
            for k in range(count):
                term = dconv * pad_ref[first + k : first + k + rows, at]
                taps_ref[k : k + 1, at] = jnp.sum(term, axis=0, keepdims=True)

    edge, body_spec = tap_specs(rows, tile)
    return pl.pallas_call(
        kernel,
        grid=(width // tile,),
        out_shape=(
            jax.ShapeDtypeStruct((rows, width), BF),
            jax.ShapeDtypeStruct((held, width), F32),
        ),
        in_specs=[
            pl.BlockSpec((rows, width), lambda j: (0, 0)),
            pl.BlockSpec((tile, width), lambda j: (j, 0)),
            body_spec,
            edge,
            body_spec,
            edge,
            pl.BlockSpec(memory_space=pl.ANY),
        ],
        out_specs=(body_spec, pl.BlockSpec((held, tile), lambda j: (0, j))),
        scratch_shapes=[pltpu.VMEM((rows + 2 * EDGE, tile), F32)],
        compiler_params=pltpu.CompilerParams(vmem_limit_bytes=VMEM_BYTES),
        cost_estimate=pl.CostEstimate(
            flops=6 * 10**9, bytes_accessed=44 * 10**6, transcendentals=0
        ),
        name="gate_back",
    )(dmixed, pw_full, conv, low, frames, high, earlier)


def head_terms(left_own, left_other, right_own, right_other, earlier):
    width = left_own[0].shape[1]
    depth, vocab = right_own.shape
    split = left_own[0].shape[0]
    tile = channel_tile(width)

    def kernel(near_a, far_a, near_b, far_b, ra_ref, rb_ref, _, out_ref):
        lhs = (((0,), (0,)), ((), ()))
        term = jnp.zeros(out_ref.shape, F32)
        for near, far, right in ((near_a, far_a, ra_ref), (near_b, far_b, rb_ref)):
            term += lax.dot_general(near[...], right[:split], lhs, preferred_element_type=F32)
            term += lax.dot_general(far[...], right[split:], lhs, preferred_element_type=F32)
        out_ref[...] = term.astype(BF)

    near = pl.BlockSpec((split, tile), lambda j: (0, j))
    far = pl.BlockSpec((depth - split, tile), lambda j: (0, j))
    right = pl.BlockSpec((depth, vocab), lambda j: (0, 0))
    return pl.pallas_call(
        kernel,
        grid=(width // tile,),
        out_shape=jax.ShapeDtypeStruct((width, vocab), BF),
        in_specs=[near, far, near, far, right, right, pl.BlockSpec(memory_space=pl.ANY)],
        out_specs=pl.BlockSpec((tile, vocab), lambda j: (j, 0)),
        compiler_params=pltpu.CompilerParams(vmem_limit_bytes=VMEM_BYTES),
        cost_estimate=pl.CostEstimate(
            flops=13 * 10**9, bytes_accessed=40 * 10**6, transcendentals=0
        ),
        name="head_terms",
    )(*left_own, *left_other, right_own, right_other, earlier)


def logits_and_stats(mixed, head, other):
    rows, width = mixed.shape
    vocab = head.shape[1]
    tile = min(LOGIT_TILE, vocab)
    steps = vocab // tile

    def kernel(x_ref, a_ref, b_ref, la_ref, lb_ref, stats_ref, top_ref, total_ref):
        step = pl.program_id(0)

        @pl.when(step == 0)
        def _():
            top_ref[...] = jnp.full_like(top_ref, -jnp.inf)
            total_ref[...] = jnp.zeros_like(total_ref)

        la_ref[...] = jnp.dot(x_ref[...], a_ref[...], preferred_element_type=F32)
        lb_ref[...] = jnp.dot(x_ref[...], b_ref[...], preferred_element_type=F32)
        parts = [
            ref[:, lane : lane + LANES] for ref in (la_ref, lb_ref) for lane in range(0, tile, LANES)
        ]
        old = top_ref[...]
        new = old
        for part in parts:
            new = jnp.maximum(new, part)
        total = total_ref[...] * jnp.exp(old - new)
        for part in parts:
            total = total + jnp.exp(part - new)
        top_ref[...] = new
        total_ref[...] = total

        @pl.when(step == steps - 1)
        def _():
            tops, totals = new.T, total.T
            top = jnp.max(tops, axis=0, keepdims=True)
            total_row = jnp.sum(totals * jnp.exp(tops - top), axis=0, keepdims=True)
            row = lax.broadcasted_iota(jnp.int32, (8, rows), 0)
            stats_ref[...] = jnp.where(row == 0, top, total_row)

    columns = pl.BlockSpec((width, tile), lambda j: (0, j))
    made = pl.BlockSpec((rows, tile), lambda j: (0, j))
    return pl.pallas_call(
        kernel,
        grid=(steps,),
        out_shape=(
            jax.ShapeDtypeStruct((rows, vocab), F32),
            jax.ShapeDtypeStruct((rows, vocab), F32),
            jax.ShapeDtypeStruct((8, rows), F32),
        ),
        in_specs=[pl.BlockSpec((rows, width), lambda j: (0, 0)), columns, columns],
        out_specs=(made, made, pl.BlockSpec((8, rows), lambda j: (0, 0))),
        scratch_shapes=[pltpu.VMEM((rows, 128), F32), pltpu.VMEM((rows, 128), F32)],
        compiler_params=pltpu.CompilerParams(vmem_limit_bytes=VMEM_BYTES),
        cost_estimate=pl.CostEstimate(flops=0, bytes_accessed=0, transcendentals=0),
        name="logits",
    )(mixed, head, other)


def logit_gradients(firsts, near, far, stats, labels):
    chips = len(stats)
    rows, vocab = far[0].shape
    tile = min(LOGIT_TILE, vocab)

    def kernel(*refs):
        first_ref = refs[0]
        logit_refs = [refs[1 + 2 * m : 3 + 2 * m] for m in range(chips)]
        stat_refs = refs[1 + 2 * chips : 1 + 3 * chips]
        label_refs = refs[1 + 3 * chips : 1 + 4 * chips]
        own_ref, other_ref, columns_ref = refs[1 + 4 * chips :]
        step = pl.program_id(0)

        @pl.when(step == 0)
        def _():
            for m in range(chips):
                tops, totals = [], []
                for o in range(chips):
                    at = m ^ o
                    tops.append(stat_refs[o][at : at + 1, :])
                    totals.append(stat_refs[o][chips + at : chips + at + 1, :])
                top = tops[0]
                for t in tops[1:]:
                    top = jnp.maximum(top, t)
                total = sum(s * jnp.exp(t - top) for s, t in zip(totals, tops))
                values = jnp.concatenate(
                    [
                        top,
                        1.0 / total,
                        label_refs[m][0:1, :],
                        label_refs[m][1:2, :],
                        jnp.zeros((124, rows), F32),
                    ],
                    axis=0,
                )
                columns_ref[m] = values.T

        entries = lax.broadcasted_iota(jnp.int32, (rows, tile), 1) + step * tile
        for m in range(chips):
            columns = columns_ref[m]
            top, inverse = columns[:, 0:1], columns[:, 1:2]
            target = columns[:, 2:3].astype(jnp.int32)
            weight = columns[:, 3:4]
            for k, out_ref in enumerate((own_ref, other_ref)):
                probs = jnp.exp(logit_refs[m][k][...] - top) * inverse
                hit = (entries == target - first_ref[k]).astype(F32)
                out_ref[m * rows : (m + 1) * rows, :] = (weight * (probs - hit)).astype(BF)

    def block(index):
        return pl.BlockSpec((rows, tile), lambda j: (index, j))

    made = pl.BlockSpec((chips * rows, tile), lambda j: (0, j))
    return pl.pallas_call(
        kernel,
        grid=(vocab // tile,),
        out_shape=(
            jax.ShapeDtypeStruct((chips * rows, vocab), BF),
            jax.ShapeDtypeStruct((chips * rows, vocab), BF),
        ),
        in_specs=[pl.BlockSpec(memory_space=pltpu.SMEM)]
        + [block(m) for m in range(chips - 1) for _ in range(2)]
        + [block(0)] * 2
        + [pl.BlockSpec((2 * chips, rows), lambda j: (0, 0))] * chips
        + [pl.BlockSpec((2, rows), lambda j: (0, 0))] * chips,
        out_specs=(made, made),
        scratch_shapes=[pltpu.VMEM((chips, rows, 128), F32)],
        compiler_params=pltpu.CompilerParams(vmem_limit_bytes=VMEM_BYTES),
        cost_estimate=pl.CostEstimate(flops=0, bytes_accessed=0, transcendentals=0),
        name="dlogits",
    )(firsts, *(list(near) * (chips - 1)), *far, *stats, *labels)


def body(frames, conv_kernel, pw_weight, head_weight, targets, frame_weight):
    frames = frames[0]
    rows, width = frames.shape
    taps = conv_kernel.shape[0]
    seqs = lax.axis_size("seq")
    count = lax.axis_size("fsdp")
    chips = count // 2
    me = lax.axis_index("fsdp")
    chip = me // 2
    core = me % 2
    low, high = halo_edges(frames[:EDGE], frames[-EDGE:])
    conv, gated, turned, mark = convolve(low, frames, high, conv_kernel)
    shard = pw_weight.shape[0]
    pieces, places = [], []
    gathered = gather_pieces(pw_weight, mark)
    for piece, m, first in gathered:
        pieces += [piece, swap(piece, 1)]
        places += [(me ^ (2 * m)) * shard + first, (me ^ (2 * m + 1)) * shard + first]
    places = jnp.stack(places).astype(jnp.int32)
    head_other = swap(head_weight, 1)

    mixed, pw_full = project(gated, frames, pieces, places)
    labels = jnp.stack([targets[0].astype(F32), frame_weight[0].astype(F32)])
    all_labels = [labels] + [swap(labels, 2 * m) for m in range(1, chips)]

    piece = width // (seqs * count)
    gated_t = turned.reshape(seqs, chips, 2, piece, rows)
    gated_t = jnp.stack(
        [lax.dynamic_index_in_dim(gated_t, chip ^ m, 1, keepdims=False) for m in range(chips)]
    )
    gated_own = lax.dynamic_index_in_dim(gated_t, core, 2, keepdims=False)
    gated_sent = lax.dynamic_index_in_dim(gated_t, 1 - core, 2, keepdims=False)
    gated_got = swap(gated_sent, 1)
    gated_pair = jnp.concatenate([gated_own, gated_got], axis=-1)

    weights = (head_weight, head_other)
    vocab = head_weight.shape[1]
    pairs, tops, totals = [], [], []

    def near_logits(block):
        own, other, stats = logits_and_stats(block, *weights)
        pairs.append((own, other))
        tops.append(stats[0].reshape(-1, rows))
        totals.append(stats[1].reshape(-1, rows))
        return (stats,)

    near_own, far_own = gather_rows(mixed, (gated_got,), near_logits)
    pair = [jnp.dot(far_own, w, preferred_element_type=F32) for w in weights]
    top = jnp.maximum(jnp.max(pair[0], axis=1), jnp.max(pair[1], axis=1))
    total = sum(jnp.sum(jnp.exp(l - top[:, None]), axis=1) for l in pair)
    pairs.append(pair)
    tops.append(top.reshape(-1, rows))
    totals.append(total.reshape(-1, rows))
    near_other = swap(near_own, 1)
    far_other = swap(far_own, 1)
    packed = jnp.concatenate(tops + totals)
    got = [packed] + [swap(packed, 2 * m) for m in range(1, chips)]
    firsts = jnp.stack([me * vocab, (me ^ 1) * vocab]).astype(jnp.int32)
    right_own, right_sent = logit_gradients(firsts, pairs[0], pairs[1], got, all_labels)
    right_other = swap(right_sent, 1)

    def back_head(m):
        rhs = (((1,), (1,)), ((), ()))
        at = slice(m * rows, (m + 1) * rows)
        return lax.dot_general(
            right_own[at], head_weight, rhs, preferred_element_type=F32
        ) + lax.dot_general(right_sent[at], head_other, rhs, preferred_element_type=F32)

    terms = []

    def while_dmixed_travels(_, sent):
        terms.append(
            head_terms((near_own, far_own), (near_other, far_other), right_own, right_other, sent)
        )
        return (), (terms[0],)

    dmixed, _, _ = scatter_and_finish(
        back_head, lambda m: (back_head(m), 0), chips, (), while_dmixed_travels, BF
    )
    head_grad = lax.psum_scatter(terms[0], "seq", scatter_dimension=0, tiled=True).astype(F32)

    dmixed_pair = jnp.concatenate([dmixed, swap(dmixed, 1)], axis=0)
    pw_term = jnp.dot(
        gated_pair.reshape(-1, 2 * rows), dmixed_pair, preferred_element_type=F32
    )
    dconv, kernel_rows = gate_back(
        dmixed, pw_full, conv, low, frames, high, taps, pw_term[:8, :LANES]
    )
    size = seqs * piece
    first = core == 0
    share = kernel_rows.shape[0] // 2

    def while_pw_travels(kept, _):
        dlow, dhigh = halo_edges(*kept[:2])
        low_taps, high_taps = kept[2][:share], kept[2][share:]
        part = jnp.where(first, low_taps, high_taps) + swap(
            jnp.where(first, high_taps, low_taps), 1
        )
        terms = [part] + [
            lax.ppermute(part, "seq", [(i, i ^ m) for i in range(seqs)]) for m in range(1, seqs)
        ]
        while len(terms) > 1:
            terms = [terms[n] + terms[n + 1] for n in range(0, len(terms), 2)]
        total = terms[0]
        backs.append(convolve_back(dlow, dconv, dhigh, conv_kernel, dmixed))
        return (total,), (backs[0],)

    backs = []
    pw_sum, _, (kernel_sum,) = scatter_and_finish(
        lambda m: pw_term[m * size : (m + 1) * size],
        lambda m: (pw_term, m),
        chips,
        (
            (dconv, EDGE, 0),
            (dconv, EDGE, rows // EDGE - 1),
            (kernel_rows, kernel_rows.shape[0], 0),
        ),
        while_pw_travels,
        F32,
    )
    back = backs[0]
    pw_sum = pw_sum.reshape(seqs, piece, width)
    here = lax.axis_index("seq")

    def shard_of(m):
        return lax.dynamic_index_in_dim(pw_sum, here ^ m, 0, keepdims=False)

    pw_grad = shard_of(0)
    for m in range(1, seqs):
        moved = lax.ppermute(
            shard_of(m).astype(BF), "seq", [(i, i ^ m) for i in range(seqs)]
        )
        pw_grad = pw_grad + moved.astype(F32)

    mask = 2
    while mask < count:
        kernel_sum = kernel_sum + swap(kernel_sum, mask)
        mask *= 2
    kernel_got = swap(kernel_sum, 1)
    kernel_grad = jnp.concatenate(
        [
            jnp.where(first, kernel_sum, kernel_got),
            jnp.where(first, kernel_got, kernel_sum)[: taps - share],
        ],
        axis=0,
    )
    return (back[None], kernel_grad, pw_grad, head_grad)


def solution(mesh):
    return jax.shard_map(
        body,
        mesh=mesh,
        in_specs=(
            P("fsdp", "seq", None),
            P(),
            P("fsdp", None),
            P(None, "fsdp"),
            P("fsdp", "seq"),
            P("fsdp", "seq"),
        ),
        out_specs=(P("fsdp", "seq", None), P(), P(("seq", "fsdp"), None), P("seq", "fsdp")),
        check_vma=False,
    )
```

time: 297 us -> 261 us (0.88)
  Pallas kernels: 0 us -> 89.5 us
  other arithmetic: 55.4 us -> 9.6 us
  matrix products: 57.7 us -> 21.8 us
  starting transfers between devices: 85.7 us -> 51.9 us
  local copies, waits for them, and re-layouts: 30.6 us -> 15.5 us
  between operations: 3.51 us -> 14.6 us
  waiting for transfers between devices: 60 us -> 56.9 us
    pallas_call x0 -> x14, Pallas kernels: none -> 89.5 us  [the longest x1 12.1 us: gate_back(): pl.pallas_call(kernel, grid=(width // tile,), out_shape=(jax.ShapeDtypeSt...]
    dot_general x19 -> x10, matrix products: 55.1 us -> 19.3 us  [the longest x4 7.73 us: back_head(): lax.dot_general(right_own[at], head_weight, rhs, preferred_element_type=F32)]
    ppermute x18 -> x10, starting transfers between devices: 56.6 us -> 23.1 us  [the longest x3 7.98 us: body(): lax.ppermute(shard_of(m).astype(BF), 'seq', [(i, i ^ m) for i in range(se...]
    dynamic_update_slice x7 -> x0, local copies, waits for them, and re-layouts: 10.6 us -> none  [the longest x4 7.97 us: body(): lax.dynamic_update_index_in_dim(pw_full, pw_other[m], me ^ 2 * m + 1, 0)]
    ppermute x18 -> x10, waiting for transfers between devices: 27.2 us -> 17.2 us  [the longest x3 5.41 us: body(): lax.ppermute(shard_of(m).astype(BF), 'seq', [(i, i ^ m) for i in range(se...]
    transpose x1 -> x0, other arithmetic: 8.44 us -> none  [body(): gated_t = gated.T.reshape(seqs, chips, 2, piece, rows)]
    another operation x11 -> x1, other arithmetic: 8.96 us -> 0.62 us  [body(): firsts = jnp.stack([me * vocab, (me ^ 1) * vocab]).astype(jnp.int32)]
    broadcast_in_dim x1 -> x0, other arithmetic: 8.03 us -> none  [body(): return (back.astype(BF)[None], kernel_grad, pw_grad, head_grad)]
  transfers between devices with their start and end apart: 49 -> 48, of which waited for: 10 -> 17; matrix products, arithmetic and copies ran while one was open for 48% -> 13% of each run, Pallas kernels for 0% -> 34%
where the time goes in v2:
time: 261 us; the launch traced here: 260 us
  Pallas kernels  89.5 us (34%)
  waiting for transfers between devices  56.9 us (22%)
  starting transfers between devices  51.9 us (20%)
  matrix products  21.8 us (8%)
  local copies, waits for them, and re-layouts  15.5 us (6%)
  between operations  14.6 us (6%)
  other arithmetic  9.6 us (4%)
    ppermute x37, waiting for transfers between devices, swap(): return lax.ppermute(value, 'fsdp', [(i, i ^ mask) for i in range(count)])  39.7 us
    ppermute x37, starting transfers between devices, swap(): return lax.ppermute(value, 'fsdp', [(i, i ^ mask) for i in range(count)])  28.7 us
    pallas_call x1, Pallas kernels, gate_back(): pl.pallas_call(kernel, grid=(width // tile,), out_shape=(jax.ShapeDtypeSt...  12.1 us
    pallas_call x1, Pallas kernels, head_terms(): pl.pallas_call(kernel, grid=(width // tile,), out_shape=jax.ShapeDtypeStr...  11.4 us
    pallas_call x1, Pallas kernels, logits_and_stats(): pl.pallas_call(kernel, grid=(steps,), out_shape=(jax.ShapeDtypeStruct((ro...  10.8 us
    pallas_call x1, Pallas kernels, convolve(): pl.pallas_call(kernel, grid=(width // tile,), out_shape=(jax.ShapeDtypeSt...  10.7 us
    unnamed x78, local copies, waits for them, and re-layouts  9.79 us
    pallas_call x1, Pallas kernels, convolve_back(): pl.pallas_call(kernel, grid=(width // tile,), out_shape=jax.ShapeDtypeStr...  8.72 us
  transfers between devices with their start and end apart: 48, of which 17 were waited for; matrix products, arithmetic and copies ran while one was open for 13% of the time, Pallas kernels for 34%

profile of v2, /device:TPU:0, one launch (start us, length us, event | category | flops | bytes accessed | tf_op | source)
XLA Modules:
  0.0 259.7 jit_solution(2932607029523947661)
XLA Ops:
  7.7 2.6 collective-permute-start.4
  12.6 3.5 %collective-permute-start = (bf16[16,1536]{1,0:T(8,128)(2,1)S(1)}, bf16[16,1536]{1,0:T(8,128)(2,1)S(1)}, u32[]{:S(2)}, u32[]{:S(2)}) collective-permute-start(bf16[16,1536]{1,0:T(8,128)(2,1)S(1)} %get-tuple-element.76), channel_id=1, source_target_pairs={{0,8},{8,16},{16,24},{1,9},{9,17},{17,25},{2,10},{10,18},{18,26},{... | collective-permute-start | bytes 147464 | tf_op jit(solution)/shard_map/ppermute | solution.py:283
  19.1 5.1 %collective-permute-done.1.high_ref = bf16[16,1536]{1,0:T(8,128)(2,1)S(1)} collective-permute-done((bf16[16,1536]{1,0:T(8,128)(2,1)S(1)}, bf16[16,1536]{1,0:T(8,128)(2,1)S(1)}, u32[]{:S(2)}, u32[]{:S(2)}) %collective-permute-start.1) | collective-permute-done | bytes 49184 | tf_op jit(solution)/shard_map/ppermute | solution.py:283
  24.8 10.7 %convolve.1 = (f32[256,1536]{1,0:T(8,128)}, bf16[256,1536]{1,0:T(8,128)(2,1)}, bf16[1536,256]{1,0:T(8,128)(2,1)}, f32[8,128]{1,0:T(8,128)}) custom-call(bf16[16,1536]{1,0:T(8,128)(2,1)} %copy-done.27, bf16[256,1536]{1,0:T(8,128)(2,1)} %bitcast.58, bf16[16,1536]{1,0:T(8,128)(2,1)} %copy-done.28, f32[31,1536]{1,0:T(8,128)} %taps_ref.3), custom_call_target="tpu_custom_call" | custom-call | tf_op jit(solution)/shard_map/convolve/pallas_call | solution.py:329
  40.7 6.0 %collective-permute-done.10.refs_11_ = bf16[96,1536]{1,0:T(8,128)(2,1)S(1)} collective-permute-done((bf16[96,1536]{1,0:T(8,128)(2,1)}, bf16[96,1536]{1,0:T(8,128)(2,1)S(1)}, u32[]{:S(2)}, u32[]{:S(2)}) %collective-permute-start.10) | collective-permute-done | bytes 294944 | tf_op jit(solution)/shard_map/ppermute | solution.py:14
  49.7 6.8 %project.1 = (bf16[256,1536]{1,0:T(8,128)(2,1)}, bf16[1536,1536]{1,0:T(8,128)(2,1)}) custom-call(s32[10]{0:T(128)} %stack.80.refs_0_, bf16[256,1536]{1,0:T(8,128)(2,1)} %get-tuple-element.32.refs_1_, bf16[256,1536]{1,0:T(8,128)(2,1)} %bitcast.59, bf16[192,1536]{1,0:T(8,128)(2,1)} %refs_3_.1, bf16[192,1536]{1,0:T(8,128)(2,1)} %collective-permute-done.3.refs_4_, ...), custom_call_target="tpu_custom_call" | custom-call | flops 1207959552 | bytes 9437184 | tf_op jit(solution)/shard_map/project/pallas_call | solution.py:236
  60.5 15.8 %collective-permute-done.12.x_ref = bf16[256,1536]{1,0:T(8,128)(2,1)S(1)} collective-permute-done((bf16[256,1536]{1,0:T(8,128)(2,1)}, bf16[256,1536]{1,0:T(8,128)(2,1)S(1)}, u32[]{:S(2)}, u32[]{:S(2)}) %collective-permute-start.12) | collective-permute-done | bytes 786464 | tf_op jit(solution)/shard_map/ppermute | solution.py:14
  78.4 3.4 %near_and_forward.1 = (bf16[768,1536]{1,0:T(8,128)(2,1)}, bf16[128,1536]{1,0:T(8,128)(2,1)}, bf16[128,1536]{1,0:T(8,128)(2,1)}) custom-call(bf16[256,1536]{1,0:T(8,128)(2,1)} %get-tuple-element.36.own_ref, bf16[256,1536]{1,0:T(8,128)(2,1)} %copy-done.16, bf16[256,1536]{1,0:T(8,128)(2,1)} %copy-done.17, bf16[4,4,48,256]{3,2,1,0:T(8,128)(2,1)} %copy-done.12), custom_call_target="tpu_custom_call" | custom-call | tf_op jit(solution)/shard_map/near_and_forward/pallas_call | solution.py:64
  87.7 10.8 %logits.1 = (f32[768,1024]{1,0:T(8,128)}, f32[768,1024]{1,0:T(8,128)}, f32[8,768]{1,0:T(8,128)}) custom-call(bf16[768,1536]{1,0:T(8,128)(2,1)} %get-tuple-element.37.x_ref.near_a, bf16[1536,1024]{1,0:T(8,128)(2,1)} %a_ref.1, bf16[1536,1024]{1,0:T(8,128)(2,1)} %copy-done.1), custom_call_target="tpu_custom_call" | custom-call | tf_op jit(solution)/shard_map/logits/pallas_call | solution.py:502
  101.4 3.8 %fusion.28 = (f32[256]{0:T(256)}, f32[256,1024]{1,0:T(8,128)}) fusion(bf16[256,1536]{1,0:T(8,128)(2,1)} %stack_halves.1.far_a, bf16[1536,1024]{1,0:T(8,128)(2,1)S(1)} %copy-done.3), kind=kOutput, calls=%fused_computation.62 | convolution fusion | flops 805568256 | bytes 4981760 | tf_op jit(solution)/shard_map/dot_general | solution.py:638
  105.2 2.3 fusion.29
  115.1 6.9 %dlogits.1 = (bf16[1024,1024]{1,0:T(8,128)(2,1)}, bf16[1024,1024]{1,0:T(8,128)(2,1)}) custom-call(s32[2]{0:T(128)} %pad_add_fusion.refs_0_, f32[768,1024]{1,0:T(8,128)} %get-tuple-element.38.refs_1_.refs_3_.refs_5_, f32[768,1024]{1,0:T(8,128)} %get-tuple-element.39.refs_2_.refs_4_.refs_6_, f32[768,1024]{1,0:T(8,128)} %get-tuple-element.38.refs_1_.refs_3_.refs_5_, ...), custom_call_target="tpu_custom_call" | custom-call | tf_op jit(solution)/shard_map/dlogits/pallas_call | solution.py:571
  122.0 2.2 fusion.8
  131.3 2.3 convolution_add_fusion.1.x_ref
  135.8 2.2 convolution_add_fusion.3.refs_0_.own_ref
  139.5 3.9 %join_halves.2 = (bf16[256,1536]{1,0:T(8,128)(2,1)}, bf16[256,1536]{1,0:T(8,128)(2,1)}) custom-call(f32[256,1536]{1,0:T(8,128)} %convolution_add_fusion.2.y_ref, f32[256,1536]{1,0:T(8,128)} %convolution_add_fusion.1.x_ref, bf16[128,1536]{1,0:T(8,128)(2,1)} %copy-done.20, bf16[128,1536]{1,0:T(8,128)(2,1)} %copy-done.21, ...), custom_call_target="tpu_custom_call" | custom-call | tf_op jit(solution)/shard_map/join_halves/pallas_call | solution.py:127
  145.2 11.4 %head_terms.1.refs_0_ = bf16[1536,1024]{1,0:T(8,128)(2,1)} custom-call(bf16[768,1536]{1,0:T(8,128)(2,1)} %get-tuple-element.37.x_ref.near_a, bf16[256,1536]{1,0:T(8,128)(2,1)} %stack_halves.1.far_a, bf16[768,1536]{1,0:T(8,128)(2,1)} %collective-permute-done.27.near_b, bf16[256,1536]{1,0:T(8,128)(2,1)} %collective-permute-done.28.far_b, ...), custom_call_target="tpu_custom_call" | custom-call | flops 12999999488 | bytes 40000000 | tf_op jit(solution)/shard_map/head_terms/pallas_call | solution.py:449
  156.7 5.9 %collective-permute-done.25.x_ref = bf16[256,1536]{1,0:T(8,128)(2,1)S(1)} collective-permute-done((bf16[256,1536]{1,0:T(8,128)(2,1)}, bf16[256,1536]{1,0:T(8,128)(2,1)S(1)}, u32[]{:S(2)}, u32[]{:S(2)}) %collective-permute-start.25) | collective-permute-done | bytes 786464 | tf_op jit(solution)/shard_map/ppermute | solution.py:14
  164.4 3.5 %finish_sum.2.dmixed_ref = bf16[256,1536]{1,0:T(8,128)(2,1)} custom-call(f32[256,1536]{1,0:T(8,128)} %convolution_add_fusion.3.refs_0_.own_ref, bf16[256,1536]{1,0:T(8,128)(2,1)} %copy-done.14, bf16[256,1536]{1,0:T(8,128)(2,1)} %copy-done.15, bf16[1536,1024]{1,0:T(8,128)(2,1)} %head_terms.1.refs_0_), custom_call_target="tpu_custom_call" | custom-call | tf_op jit(solution)/shard_map/finish_sum/pallas_call | solution.py:173
  167.9 2.5 collective-permute-done.30
  170.4 2.5 fusion.30
  175.5 12.1 %gate_back.1 = (bf16[256,1536]{1,0:T(8,128)(2,1)}, f32[32,1536]{1,0:T(8,128)}) custom-call(bf16[256,1536]{1,0:T(8,128)(2,1)} %finish_sum.2.dmixed_ref, bf16[1536,1536]{1,0:T(8,128)(2,1)} %get-tuple-element.47.pw_ref, f32[256,1536]{1,0:T(8,128)} %get-tuple-element.48.conv_ref, bf16[16,1536]{1,0:T(8,128)(2,1)} %copy-done.27, bf16[256,1536]{1,0:T(8,128)(2,1)} %bitcast.60, ...), custom_call_target="tpu_custom_call" | custom-call | flops 6000000000 | bytes 44000000 | tf_op jit(solution)/shard_map/gate_back/pallas_call | solution.py:406
  188.4 3.7 %join_halves.3 = (bf16[192,1536]{1,0:T(8,128)(2,1)}, bf16[192,1536]{1,0:T(8,128)(2,1)}, bf16[16,1536]{1,0:T(8,128)(2,1)}, bf16[16,1536]{1,0:T(8,128)(2,1)}, f32[32,1536]{1,0:T(8,128)}) custom-call(f32[768,1536]{1,0:T(8,128)} %copy-done, f32[768,1536]{1,0:T(8,128)} %copy-done, bf16[96,1536]{1,0:T(8,128)(2,1)} %copy-done.25, bf16[96,1536]{1,0:T(8,128)(2,1)} %copy-done.26, ...), custom_call_target="tpu_custom_call" | custom-call | tf_op jit(solution)/shard_map/join_halves/pallas_call | solution.py:127
  193.2 3.6 %collective-permute-start.33 = (bf16[16,1536]{1,0:T(8,128)(2,1)}, bf16[16,1536]{1,0:T(8,128)(2,1)S(1)}, u32[]{:S(2)}, u32[]{:S(2)}) collective-permute-start(bf16[16,1536]{1,0:T(8,128)(2,1)} %get-tuple-element.51), channel_id=1, source_target_pairs={{0,8},{8,16},{16,24},{1,9},{9,17},{17,25},{2,10},{10,18},{18,26},{... | collective-permute-start | bytes 147464 | tf_op jit(solution)/shard_map/ppermute | solution.py:283
  201.6 2.7 %collective-permute-start.38 = (f32[16,1536]{1,0:T(8,128)S(1)}, f32[16,1536]{1,0:T(8,128)S(1)}, u32[]{:S(2)}, u32[]{:S(2)}) collective-permute-start(f32[16,1536]{1,0:T(8,128)S(1)} %select_add_fusion), channel_id=1, source_target_pairs={{0,8},{8,0},{16,24},{24,16},{1,9},{9,1},{17,25},{25,17},{2,10},{10... | collective-permute-start | bytes 294920 | tf_op jit(solution)/shard_map/ppermute | solution.py:690
  206.9 8.7 %convolve_back.1.refs_1_ = bf16[256,1536]{1,0:T(8,128)(2,1)} custom-call(bf16[16,1536]{1,0:T(8,128)(2,1)} %copy-done.29, bf16[256,1536]{1,0:T(8,128)(2,1)} %get-tuple-element.49.refs_0_.refs_1_.mid_ref, bf16[16,1536]{1,0:T(8,128)(2,1)} %copy-done.30, f32[31,1536]{1,0:T(8,128)} %taps_ref.3, bf16[256,1536]{1,0:T(8,128)(2,1)} %finish_sum.2.dmixed_ref), custom_call_target="tpu_custom_call" | custom-call | tf_op jit(solution)/shard_map/convolve_back/pallas_call | solution.py:368
  215.7 2.8 %collective-permute-done.39 = f32[16,1536]{1,0:T(8,128)S(1)} collective-permute-done((f32[16,1536]{1,0:T(8,128)S(1)}, f32[16,1536]{1,0:T(8,128)S(1)}, u32[]{:S(2)}, u32[]{:S(2)}) %collective-permute-start.39) | collective-permute-done | bytes 98336 | tf_op jit(solution)/shard_map/ppermute | solution.py:690
  223.0 3.5 %finish_sum.3 = (f32[192,1536]{1,0:T(8,128)}, f32[16,1536]{1,0:T(8,128)}) custom-call(f32[768,1536]{1,0:T(8,128)} %copy-done, bf16[192,1536]{1,0:T(8,128)(2,1)} %copy-done.18, bf16[192,1536]{1,0:T(8,128)(2,1)} %copy-done.19, f32[16,1536]{1,0:T(8,128)} %add_add_fusion.refs_0_, bf16[256,1536]{1,0:T(8,128)(2,1)} %convolve_back.1.refs_1_), custom_call_target="tpu_custom_call" | custom-call | tf_op jit(solution)/shard_map/finish_sum/pallas_call | solution.py:173
  228.8 5.5 %collective-permute-start.44 = (bf16[48,1536]{1,0:T(8,128)(2,1)S(1)}, bf16[48,1536]{1,0:T(8,128)(2,1)S(1)}, u32[]{:S(2)}, u32[]{:S(2)}) collective-permute-start(bf16[48,1536]{1,0:T(8,128)(2,1)S(1)} %get-tuple-element.64), channel_id=1, source_target_pairs={{0,8},{8,0},{16,24},{24,16},{1,9},{9,1},{17,25},{25,17},{2,10},{10... | collective-permute-start | bytes 442376 | tf_op jit(solution)/shard_map/ppermute | solution.py:720
  239.1 3.3 %collective-permute-done.42 = f32[16,1536]{1,0:T(8,128)S(1)} collective-permute-done((f32[16,1536]{1,0:T(8,128)S(1)}, f32[16,1536]{1,0:T(8,128)S(1)}, u32[]{:S(2)}, u32[]{:S(2)}) %collective-permute-start.42) | collective-permute-done | bytes 98336 | tf_op jit(solution)/shard_map/ppermute | solution.py:14
  242.5 5.4 %collective-permute-done.45 = bf16[48,1536]{1,0:T(8,128)(2,1)S(1)} collective-permute-done((bf16[48,1536]{1,0:T(8,128)(2,1)S(1)}, bf16[48,1536]{1,0:T(8,128)(2,1)S(1)}, u32[]{:S(2)}, u32[]{:S(2)}) %collective-permute-start.45) | collective-permute-done | bytes 147488 | tf_op jit(solution)/shard_map/ppermute | solution.py:720
  250.4 2.5 convert_element_type.54
  (200 shorter events, 77.1 us)
Async XLA Ops:
  7.2 243.2 %reduce-scatter.2.cloned.1.call-start = ((), (), s32[]{:S(2)}) async-start(), calls=%async_computation.1 | async-start | bytes 3932160 | tf_op jit(solution)/shard_map/reduce_scatter | solution.py:670
  7.2 78.7 %collective-permute-start.14 = (bf16[1536,1024]{1,0:T(8,128)(2,1)}, bf16[1536,1024]{1,0:T(8,128)(2,1)S(1)}, u32[]{:S(2)}, u32[]{:S(2)}) collective-permute-start(bf16[1536,1024]{1,0:T(8,128)(2,1)} %a_ref.1), channel_id=1, source_target_pairs={{0,1},{1,0},{2,3},{3,2},{4,5},{5,4},{6,7},{7,6},{8,9},{9,8},{10,11... | collective-permute-start | bytes 9437192 | tf_op jit(solution)/shard_map/ppermute | solution.py:14
  7.7 27.8 %collective-permute-start.4 = (bf16[192,1536]{1,0:T(8,128)(2,1)}, bf16[192,1536]{1,0:T(8,128)(2,1)S(1)}, u32[]{:S(2)}, u32[]{:S(2)}) collective-permute-start(bf16[192,1536]{1,0:T(8,128)(2,1)} %refs_3_.1), channel_id=1, source_target_pairs={{0,2},{1,3},{2,0},{3,1},{4,6},{5,7},{6,4},{7,5},{8,10},{9,11},{10,... | collective-permute-start | bytes 1769480 | tf_op jit(solution)/shard_map/ppermute | solution.py:14
  10.3 25.3 %collective-permute-start.6 = (bf16[192,1536]{1,0:T(8,128)(2,1)}, bf16[192,1536]{1,0:T(8,128)(2,1)S(1)}, u32[]{:S(2)}, u32[]{:S(2)}) collective-permute-start(bf16[192,1536]{1,0:T(8,128)(2,1)} %refs_3_.1), channel_id=1, source_target_pairs={{0,4},{1,5},{2,6},{3,7},{4,0},{5,1},{6,2},{7,3},{8,12},{9,13},{10,... | collective-permute-start | bytes 1769480 | tf_op jit(solution)/shard_map/ppermute | solution.py:14
  11.8 27.7 %collective-permute-start.3 = (bf16[192,1536]{1,0:T(8,128)(2,1)}, bf16[192,1536]{1,0:T(8,128)(2,1)}, u32[]{:S(2)}, u32[]{:S(2)}) collective-permute-start(bf16[192,1536]{1,0:T(8,128)(2,1)} %refs_3_.1), channel_id=1, source_target_pairs={{0,1},{1,0},{2,3},{3,2},{4,5},{5,4},{6,7},{7,6},{8,9},{9,8},{10,11... | collective-permute-start | bytes 1769480 | tf_op jit(solution)/shard_map/ppermute | solution.py:14
  39.5 9.5 %collective-permute-start.5 = (bf16[192,1536]{1,0:T(8,128)(2,1)}, bf16[192,1536]{1,0:T(8,128)(2,1)}, u32[]{:S(2)}, u32[]{:S(2)}) collective-permute-start(bf16[192,1536]{1,0:T(8,128)(2,1)} %copy-done.7), channel_id=1, source_target_pairs={{0,1},{1,0},{2,3},{3,2},{4,5},{5,4},{6,7},{7,6},{8,9},{9,8},{10,11... | collective-permute-start | bytes 1769480 | tf_op jit(solution)/shard_map/ppermute | solution.py:14
  56.5 19.9 %collective-permute-start.12 = (bf16[256,1536]{1,0:T(8,128)(2,1)}, bf16[256,1536]{1,0:T(8,128)(2,1)S(1)}, u32[]{:S(2)}, u32[]{:S(2)}) collective-permute-start(bf16[256,1536]{1,0:T(8,128)(2,1)} %get-tuple-element.36.own_ref), channel_id=1, source_target_pairs={{0,2},{1,3},{2,0},{3,1},{4,6},{5,7},{6,4},{7,5},{8,10},{9,11},{10,... | collective-permute-start | bytes 2359304 | tf_op jit(solution)/shard_map/ppermute | solution.py:14
  58.0 19.5 %collective-permute-start.13 = (bf16[256,1536]{1,0:T(8,128)(2,1)}, bf16[256,1536]{1,0:T(8,128)(2,1)S(1)}, u32[]{:S(2)}, u32[]{:S(2)}) collective-permute-start(bf16[256,1536]{1,0:T(8,128)(2,1)} %get-tuple-element.36.own_ref), channel_id=1, source_target_pairs={{0,4},{1,5},{2,6},{3,7},{4,0},{5,1},{6,2},{7,3},{8,12},{9,13},{10,... | collective-permute-start | bytes 2359304 | tf_op jit(solution)/shard_map/ppermute | solution.py:14
  81.8 17.5 %collective-permute-start.15 = (bf16[128,1536]{1,0:T(8,128)(2,1)}, bf16[128,1536]{1,0:T(8,128)(2,1)}, u32[]{:S(2)}, u32[]{:S(2)}) collective-permute-start(bf16[128,1536]{1,0:T(8,128)(2,1)} %get-tuple-element.40), channel_id=1, source_target_pairs={{0,4},{1,5},{2,6},{3,7},{4,0},{5,1},{6,2},{7,3},{8,12},{9,13},{10,... | collective-permute-start | bytes 1179656 | tf_op jit(solution)/shard_map/ppermute | solution.py:14
  82.3 17.0 %collective-permute-start.16 = (bf16[128,1536]{1,0:T(8,128)(2,1)}, bf16[128,1536]{1,0:T(8,128)(2,1)}, u32[]{:S(2)}, u32[]{:S(2)}) collective-permute-start(bf16[128,1536]{1,0:T(8,128)(2,1)} %get-tuple-element.41), channel_id=1, source_target_pairs={{0,2},{1,3},{2,0},{3,1},{4,6},{5,7},{6,4},{7,5},{8,10},{9,11},{10,... | collective-permute-start | bytes 1179656 | tf_op jit(solution)/shard_map/ppermute | solution.py:14
  83.5 26.4 %collective-permute-start.20 = (f32[2,256]{1,0:T(2,128)S(1)}, f32[2,256]{1,0:T(2,128)}, u32[]{:S(2)}, u32[]{:S(2)}) collective-permute-start(f32[2,256]{1,0:T(2,128)S(1)} %pad_maximum_fusion.3.refs_13_), channel_id=1, source_target_pairs={{0,2},{1,3},{2,0},{3,1},{4,6},{5,7},{6,4},{7,5},{8,10},{9,11},{10,... | collective-permute-start | bytes 6152 | tf_op jit(solution)/shard_map/ppermute | solution.py:14
  84.4 27.8 %collective-permute-start.21 = (f32[2,256]{1,0:T(2,128)S(1)}, f32[2,256]{1,0:T(2,128)}, u32[]{:S(2)}, u32[]{:S(2)}) collective-permute-start(f32[2,256]{1,0:T(2,128)S(1)} %pad_maximum_fusion.3.refs_13_), channel_id=1, source_target_pairs={{0,4},{1,5},{2,6},{3,7},{4,0},{5,1},{6,2},{7,3},{8,12},{9,13},{10,... | collective-permute-start | bytes 6152 | tf_op jit(solution)/shard_map/ppermute | solution.py:14
  85.9 26.3 %collective-permute-start.22 = (f32[2,256]{1,0:T(2,128)S(1)}, f32[2,256]{1,0:T(2,128)}, u32[]{:S(2)}, u32[]{:S(2)}) collective-permute-start(f32[2,256]{1,0:T(2,128)S(1)} %pad_maximum_fusion.3.refs_13_), channel_id=1, source_target_pairs={{0,6},{1,7},{2,4},{3,5},{4,2},{5,3},{6,0},{7,1},{8,14},{9,15},{10,... | collective-permute-start | bytes 6152 | tf_op jit(solution)/shard_map/ppermute | solution.py:14
  112.3 33.0 %collective-permute-start.27 = (bf16[768,1536]{1,0:T(8,128)(2,1)S(1)}, bf16[768,1536]{1,0:T(8,128)(2,1)}, u32[]{:S(2)}, u32[]{:S(2)}) collective-permute-start(bf16[768,1536]{1,0:T(8,128)(2,1)S(1)} %copy-done.9), channel_id=1, source_target_pairs={{0,1},{1,0},{2,3},{3,2},{4,5},{5,4},{6,7},{7,6},{8,9},{9,8},{10,11... | collective-permute-start | bytes 7077896 | tf_op jit(solution)/shard_map/ppermute | solution.py:14
  112.3 32.9 %collective-permute-start.28 = (bf16[256,1536]{1,0:T(8,128)(2,1)}, bf16[256,1536]{1,0:T(8,128)(2,1)}, u32[]{:S(2)}, u32[]{:S(2)}) collective-permute-start(bf16[256,1536]{1,0:T(8,128)(2,1)} %stack_halves.1.far_a), channel_id=1, source_target_pairs={{0,1},{1,0},{2,3},{3,2},{4,5},{5,4},{6,7},{7,6},{8,9},{9,8},{10,11... | collective-permute-start | bytes 2359304 | tf_op jit(solution)/shard_map/ppermute | solution.py:14
  122.0 23.3 %collective-permute-start.29 = (bf16[1024,1024]{1,0:T(8,128)(2,1)}, bf16[1024,1024]{1,0:T(8,128)(2,1)}, u32[]{:S(2)}, u32[]{:S(2)}) collective-permute-start(bf16[1024,1024]{1,0:T(8,128)(2,1)} %get-tuple-element.44), channel_id=1, source_target_pairs={{0,1},{1,0},{2,3},{3,2},{4,5},{5,4},{6,7},{7,6},{8,9},{9,8},{10,11... | collective-permute-start | bytes 6291464 | tf_op jit(solution)/shard_map/ppermute | solution.py:14
  125.7 12.3 %collective-permute-start.23 = (bf16[128,1536]{1,0:T(8,128)(2,1)S(1)}, bf16[128,1536]{1,0:T(8,128)(2,1)S(1)}, u32[]{:S(2)}, u32[]{:S(2)}) collective-permute-start(bf16[128,1536]{1,0:T(8,128)(2,1)S(1)} %get-tuple-element.70), channel_id=1, source_target_pairs={{0,2},{1,3},{2,0},{3,1},{4,6},{5,7},{6,4},{7,5},{8,10},{9,11},{10,... | collective-permute-start | bytes 1179656 | tf_op jit(solution)/shard_map/ppermute | solution.py:14
  127.0 11.1 %collective-permute-start.24 = (bf16[128,1536]{1,0:T(8,128)(2,1)S(1)}, bf16[128,1536]{1,0:T(8,128)(2,1)S(1)}, u32[]{:S(2)}, u32[]{:S(2)}) collective-permute-start(bf16[128,1536]{1,0:T(8,128)(2,1)S(1)} %get-tuple-element.69), channel_id=1, source_target_pairs={{0,4},{1,5},{2,6},{3,7},{4,0},{5,1},{6,2},{7,3},{8,12},{9,13},{10,... | collective-permute-start | bytes 1179656 | tf_op jit(solution)/shard_map/ppermute | solution.py:14
  143.5 19.1 %collective-permute-start.25 = (bf16[256,1536]{1,0:T(8,128)(2,1)}, bf16[256,1536]{1,0:T(8,128)(2,1)S(1)}, u32[]{:S(2)}, u32[]{:S(2)}) collective-permute-start(bf16[256,1536]{1,0:T(8,128)(2,1)} %get-tuple-element.45._), channel_id=1, source_target_pairs={{0,2},{1,3},{2,0},{3,1},{4,6},{5,7},{6,4},{7,5},{8,10},{9,11},{10,... | collective-permute-start | bytes 2359304 | tf_op jit(solution)/shard_map/ppermute | solution.py:14
  144.6 18.8 %collective-permute-start.26 = (bf16[256,1536]{1,0:T(8,128)(2,1)}, bf16[256,1536]{1,0:T(8,128)(2,1)S(1)}, u32[]{:S(2)}, u32[]{:S(2)}) collective-permute-start(bf16[256,1536]{1,0:T(8,128)(2,1)} %get-tuple-element.46), channel_id=1, source_target_pairs={{0,4},{1,5},{2,6},{3,7},{4,0},{5,1},{6,2},{7,3},{8,12},{9,13},{10,... | collective-permute-start | bytes 2359304 | tf_op jit(solution)/shard_map/ppermute | solution.py:14
  173.6 14.0 %collective-permute-start.31 = (bf16[96,1536]{1,0:T(8,128)(2,1)S(1)}, bf16[96,1536]{1,0:T(8,128)(2,1)S(1)}, u32[]{:S(2)}, u32[]{:S(2)}) collective-permute-start(bf16[96,1536]{1,0:T(8,128)(2,1)S(1)} %get-tuple-element.63), channel_id=1, source_target_pairs={{0,2},{1,3},{2,0},{3,1},{4,6},{5,7},{6,4},{7,5},{8,10},{9,11},{10,... | collective-permute-start | bytes 884744 | tf_op jit(solution)/shard_map/ppermute | solution.py:14
  174.9 12.8 %collective-permute-start.32 = (bf16[96,1536]{1,0:T(8,128)(2,1)S(1)}, bf16[96,1536]{1,0:T(8,128)(2,1)S(1)}, u32[]{:S(2)}, u32[]{:S(2)}) collective-permute-start(bf16[96,1536]{1,0:T(8,128)(2,1)S(1)} %get-tuple-element.62), channel_id=1, source_target_pairs={{0,4},{1,5},{2,6},{3,7},{4,0},{5,1},{6,2},{7,3},{8,12},{9,13},{10,... | collective-permute-start | bytes 884744 | tf_op jit(solution)/shard_map/ppermute | solution.py:14
  193.2 11.1 %collective-permute-start.33 = (bf16[16,1536]{1,0:T(8,128)(2,1)}, bf16[16,1536]{1,0:T(8,128)(2,1)S(1)}, u32[]{:S(2)}, u32[]{:S(2)}) collective-permute-start(bf16[16,1536]{1,0:T(8,128)(2,1)} %get-tuple-element.51), channel_id=1, source_target_pairs={{0,8},{8,16},{16,24},{1,9},{9,17},{17,25},{2,10},{10,18},{18,26},{... | collective-permute-start | bytes 147464 | tf_op jit(solution)/shard_map/ppermute | solution.py:283
  198.3 23.0 %collective-permute-start.35 = (bf16[192,1536]{1,0:T(8,128)(2,1)}, bf16[192,1536]{1,0:T(8,128)(2,1)S(1)}, u32[]{:S(2)}, u32[]{:S(2)}) collective-permute-start(bf16[192,1536]{1,0:T(8,128)(2,1)} %get-tuple-element.53), channel_id=1, source_target_pairs={{0,2},{1,3},{2,0},{3,1},{4,6},{5,7},{6,4},{7,5},{8,10},{9,11},{10,... | collective-permute-start | bytes 1769480 | tf_op jit(solution)/shard_map/ppermute | solution.py:14
  199.6 21.8 %collective-permute-start.36 = (bf16[192,1536]{1,0:T(8,128)(2,1)}, bf16[192,1536]{1,0:T(8,128)(2,1)S(1)}, u32[]{:S(2)}, u32[]{:S(2)}) collective-permute-start(bf16[192,1536]{1,0:T(8,128)(2,1)} %get-tuple-element.54), channel_id=1, source_target_pairs={{0,4},{1,5},{2,6},{3,7},{4,0},{5,1},{6,2},{7,3},{8,12},{9,13},{10,... | collective-permute-start | bytes 1769480 | tf_op jit(solution)/shard_map/ppermute | solution.py:14
  201.6 14.0 %collective-permute-start.38 = (f32[16,1536]{1,0:T(8,128)S(1)}, f32[16,1536]{1,0:T(8,128)S(1)}, u32[]{:S(2)}, u32[]{:S(2)}) collective-permute-start(f32[16,1536]{1,0:T(8,128)S(1)} %select_add_fusion), channel_id=1, source_target_pairs={{0,8},{8,0},{16,24},{24,16},{1,9},{9,1},{17,25},{25,17},{2,10},{10... | collective-permute-start | bytes 294920 | tf_op jit(solution)/shard_map/ppermute | solution.py:690
  204.3 14.1 %collective-permute-start.39 = (f32[16,1536]{1,0:T(8,128)S(1)}, f32[16,1536]{1,0:T(8,128)S(1)}, u32[]{:S(2)}, u32[]{:S(2)}) collective-permute-start(f32[16,1536]{1,0:T(8,128)S(1)} %select_add_fusion), channel_id=1, source_target_pairs={{0,16},{8,24},{16,0},{24,8},{1,17},{9,25},{17,1},{25,9},{2,18},{10... | collective-permute-start | bytes 294920 | tf_op jit(solution)/shard_map/ppermute | solution.py:690
  205.7 15.0 %collective-permute-start.40 = (f32[16,1536]{1,0:T(8,128)S(1)}, f32[16,1536]{1,0:T(8,128)S(1)}, u32[]{:S(2)}, u32[]{:S(2)}) collective-permute-start(f32[16,1536]{1,0:T(8,128)S(1)} %select_add_fusion), channel_id=1, source_target_pairs={{0,24},{8,16},{16,8},{24,0},{1,25},{9,17},{17,9},{25,1},{2,26},{10... | collective-permute-start | bytes 294920 | tf_op jit(solution)/shard_map/ppermute | solution.py:690
  226.5 10.3 %collective-permute-start.41 = (f32[16,1536]{1,0:T(8,128)}, f32[16,1536]{1,0:T(8,128)S(1)}, u32[]{:S(2)}, u32[]{:S(2)}) collective-permute-start(f32[16,1536]{1,0:T(8,128)} %get-tuple-element.56), channel_id=1, source_target_pairs={{0,2},{1,3},{2,0},{3,1},{4,6},{5,7},{6,4},{7,5},{8,10},{9,11},{10,... | collective-permute-start | bytes 294920 | tf_op jit(solution)/shard_map/ppermute | solution.py:14
  228.8 13.7 %collective-permute-start.44 = (bf16[48,1536]{1,0:T(8,128)(2,1)S(1)}, bf16[48,1536]{1,0:T(8,128)(2,1)S(1)}, u32[]{:S(2)}, u32[]{:S(2)}) collective-permute-start(bf16[48,1536]{1,0:T(8,128)(2,1)S(1)} %get-tuple-element.64), channel_id=1, source_target_pairs={{0,8},{8,0},{16,24},{24,16},{1,9},{9,1},{17,25},{25,17},{2,10},{10... | collective-permute-start | bytes 442376 | tf_op jit(solution)/shard_map/ppermute | solution.py:720
  234.3 13.5 %collective-permute-start.45 = (bf16[48,1536]{1,0:T(8,128)(2,1)S(1)}, bf16[48,1536]{1,0:T(8,128)(2,1)S(1)}, u32[]{:S(2)}, u32[]{:S(2)}) collective-permute-start(bf16[48,1536]{1,0:T(8,128)(2,1)S(1)} %get-tuple-element.66), channel_id=1, source_target_pairs={{0,16},{8,24},{16,0},{24,8},{1,17},{9,25},{17,1},{25,9},{2,18},{10... | collective-permute-start | bytes 442376 | tf_op jit(solution)/shard_map/ppermute | solution.py:720
  234.6 13.3 %collective-permute-start.46 = (bf16[48,1536]{1,0:T(8,128)(2,1)S(1)}, bf16[48,1536]{1,0:T(8,128)(2,1)S(1)}, u32[]{:S(2)}, u32[]{:S(2)}) collective-permute-start(bf16[48,1536]{1,0:T(8,128)(2,1)S(1)} %get-tuple-element.65), channel_id=1, source_target_pairs={{0,24},{8,16},{16,8},{24,0},{1,25},{9,17},{17,9},{25,1},{2,26},{10... | collective-permute-start | bytes 442376 | tf_op jit(solution)/shard_map/ppermute | solution.py:720
  (55 other events, 278.1 us)
Sparse Core Ops, SparseCore 0:
  156.8 67.2 reduce-scatter.1

commit v3 on v2

--- a/solution.py
+++ b/solution.py
@@ -108,7 +108,7 @@
 def join_halves(near_y, near_x, low, high, earlier, passed=()):
     half, width = low.shape
     rows = 2 * half
-    tile = 512 if width % 512 == 0 else width
+    tile = width
     count = len(passed)
 
     def kernel(y_ref, x_ref, low_ref, high_ref, *refs):
@@ -157,7 +157,7 @@
 
 def finish_sum(own, recv_x, recv_y, index, passed, dtype, *earlier):
     rows, width = recv_x.shape
-    tile = 512 if width % 512 == 0 else width
+    tile = width
     count = len(passed)
 
     def kernel(own_ref, x_ref, y_ref, *refs):

time: 261 us -> 259 us (level)
  transfers between devices with their start and end apart: 48 -> 48, of which waited for: 17 -> 18; matrix products, arithmetic and copies ran while one was open for 13% -> 13% of each run, Pallas kernels for 34% -> 34%
where the time goes in v3:
time: 259 us; the launch traced here: 258 us
  Pallas kernels  86.9 us (34%)
  waiting for transfers between devices  57.4 us (22%)
  starting transfers between devices  52 us (20%)
  matrix products  21.8 us (8%)
  local copies, waits for them, and re-layouts  15.5 us (6%)
  between operations  14.6 us (6%)
  other arithmetic  9.59 us (4%)
    ppermute x37, waiting for transfers between devices, swap(): return lax.ppermute(value, 'fsdp', [(i, i ^ mask) for i in range(count)])  39.7 us
    ppermute x37, starting transfers between devices, swap(): return lax.ppermute(value, 'fsdp', [(i, i ^ mask) for i in range(count)])  28.8 us
    pallas_call x1, Pallas kernels, gate_back(): pl.pallas_call(kernel, grid=(width // tile,), out_shape=(jax.ShapeDtypeSt...  12.1 us
    pallas_call x1, Pallas kernels, head_terms(): pl.pallas_call(kernel, grid=(width // tile,), out_shape=jax.ShapeDtypeStr...  11.4 us
    pallas_call x1, Pallas kernels, logits_and_stats(): pl.pallas_call(kernel, grid=(steps,), out_shape=(jax.ShapeDtypeStruct((ro...  10.8 us
    pallas_call x1, Pallas kernels, convolve(): pl.pallas_call(kernel, grid=(width // tile,), out_shape=(jax.ShapeDtypeSt...  10.7 us
    unnamed x78, local copies, waits for them, and re-layouts  9.79 us
    ppermute x3, starting transfers between devices, body(): lax.ppermute(shard_of(m).astype(BF), 'seq', [(i, i ^ m) for i in range(se...  9.06 us
  transfers between devices with their start and end apart: 48, of which 18 were waited for; matrix products, arithmetic and copies ran while one was open for 13% of the time, Pallas kernels for 34%

profile of v3, /device:TPU:0, one launch (start us, length us, event | category | flops | bytes accessed | tf_op | source)
XLA Modules:
  0.0 257.8 jit_solution(7801757208140877343)
XLA Ops:
  7.7 2.6 collective-permute-start.4
  12.6 3.5 %collective-permute-start = (bf16[16,1536]{1,0:T(8,128)(2,1)S(1)}, bf16[16,1536]{1,0:T(8,128)(2,1)S(1)}, u32[]{:S(2)}, u32[]{:S(2)}) collective-permute-start(bf16[16,1536]{1,0:T(8,128)(2,1)S(1)} %get-tuple-element.76), channel_id=1, source_target_pairs={{0,8},{8,16},{16,24},{1,9},{9,17},{17,25},{2,10},{10,18},{18,26},{... | collective-permute-start | bytes 147464 | tf_op jit(solution)/shard_map/ppermute | solution.py:283
  19.1 5.1 %collective-permute-done.1.high_ref = bf16[16,1536]{1,0:T(8,128)(2,1)S(1)} collective-permute-done((bf16[16,1536]{1,0:T(8,128)(2,1)S(1)}, bf16[16,1536]{1,0:T(8,128)(2,1)S(1)}, u32[]{:S(2)}, u32[]{:S(2)}) %collective-permute-start.1) | collective-permute-done | bytes 49184 | tf_op jit(solution)/shard_map/ppermute | solution.py:283
  24.8 10.7 %convolve.1 = (f32[256,1536]{1,0:T(8,128)}, bf16[256,1536]{1,0:T(8,128)(2,1)}, bf16[1536,256]{1,0:T(8,128)(2,1)}, f32[8,128]{1,0:T(8,128)}) custom-call(bf16[16,1536]{1,0:T(8,128)(2,1)} %copy-done.27, bf16[256,1536]{1,0:T(8,128)(2,1)} %bitcast.58, bf16[16,1536]{1,0:T(8,128)(2,1)} %copy-done.28, f32[31,1536]{1,0:T(8,128)} %taps_ref.3), custom_call_target="tpu_custom_call" | custom-call | tf_op jit(solution)/shard_map/convolve/pallas_call | solution.py:329
  40.7 6.0 %collective-permute-done.10.refs_11_ = bf16[96,1536]{1,0:T(8,128)(2,1)S(1)} collective-permute-done((bf16[96,1536]{1,0:T(8,128)(2,1)}, bf16[96,1536]{1,0:T(8,128)(2,1)S(1)}, u32[]{:S(2)}, u32[]{:S(2)}) %collective-permute-start.10) | collective-permute-done | bytes 294944 | tf_op jit(solution)/shard_map/ppermute | solution.py:14
  49.7 6.8 %project.1 = (bf16[256,1536]{1,0:T(8,128)(2,1)}, bf16[1536,1536]{1,0:T(8,128)(2,1)}) custom-call(s32[10]{0:T(128)} %stack.80.refs_0_, bf16[256,1536]{1,0:T(8,128)(2,1)} %get-tuple-element.32.refs_1_, bf16[256,1536]{1,0:T(8,128)(2,1)} %bitcast.59, bf16[192,1536]{1,0:T(8,128)(2,1)} %refs_3_.1, bf16[192,1536]{1,0:T(8,128)(2,1)} %collective-permute-done.3.refs_4_, ...), custom_call_target="tpu_custom_call" | custom-call | flops 1207959552 | bytes 9437184 | tf_op jit(solution)/shard_map/project/pallas_call | solution.py:236
  60.5 15.8 %collective-permute-done.12.x_ref = bf16[256,1536]{1,0:T(8,128)(2,1)S(1)} collective-permute-done((bf16[256,1536]{1,0:T(8,128)(2,1)}, bf16[256,1536]{1,0:T(8,128)(2,1)S(1)}, u32[]{:S(2)}, u32[]{:S(2)}) %collective-permute-start.12) | collective-permute-done | bytes 786464 | tf_op jit(solution)/shard_map/ppermute | solution.py:14
  78.4 3.4 %near_and_forward.1 = (bf16[768,1536]{1,0:T(8,128)(2,1)}, bf16[128,1536]{1,0:T(8,128)(2,1)}, bf16[128,1536]{1,0:T(8,128)(2,1)}) custom-call(bf16[256,1536]{1,0:T(8,128)(2,1)} %get-tuple-element.36.own_ref, bf16[256,1536]{1,0:T(8,128)(2,1)} %copy-done.16, bf16[256,1536]{1,0:T(8,128)(2,1)} %copy-done.17, bf16[4,4,48,256]{3,2,1,0:T(8,128)(2,1)} %copy-done.12), custom_call_target="tpu_custom_call" | custom-call | tf_op jit(solution)/shard_map/near_and_forward/pallas_call | solution.py:64
  87.7 10.8 %logits.1 = (f32[768,1024]{1,0:T(8,128)}, f32[768,1024]{1,0:T(8,128)}, f32[8,768]{1,0:T(8,128)}) custom-call(bf16[768,1536]{1,0:T(8,128)(2,1)} %get-tuple-element.37.x_ref.near_a, bf16[1536,1024]{1,0:T(8,128)(2,1)} %a_ref.1, bf16[1536,1024]{1,0:T(8,128)(2,1)} %copy-done.1), custom_call_target="tpu_custom_call" | custom-call | tf_op jit(solution)/shard_map/logits/pallas_call | solution.py:502
  101.4 3.8 %fusion.28 = (f32[256]{0:T(256)}, f32[256,1024]{1,0:T(8,128)}) fusion(bf16[256,1536]{1,0:T(8,128)(2,1)} %stack_halves.1.far_a, bf16[1536,1024]{1,0:T(8,128)(2,1)S(1)} %copy-done.3), kind=kOutput, calls=%fused_computation.62 | convolution fusion | flops 805568256 | bytes 4981760 | tf_op jit(solution)/shard_map/dot_general | solution.py:638
  105.2 2.3 fusion.29
  115.1 6.9 %dlogits.1 = (bf16[1024,1024]{1,0:T(8,128)(2,1)}, bf16[1024,1024]{1,0:T(8,128)(2,1)}) custom-call(s32[2]{0:T(128)} %pad_add_fusion.refs_0_, f32[768,1024]{1,0:T(8,128)} %get-tuple-element.38.refs_1_.refs_3_.refs_5_, f32[768,1024]{1,0:T(8,128)} %get-tuple-element.39.refs_2_.refs_4_.refs_6_, f32[768,1024]{1,0:T(8,128)} %get-tuple-element.38.refs_1_.refs_3_.refs_5_, ...), custom_call_target="tpu_custom_call" | custom-call | tf_op jit(solution)/shard_map/dlogits/pallas_call | solution.py:571
  122.0 2.2 fusion.8
  131.3 2.3 convolution_add_fusion.1.x_ref
  135.8 2.2 convolution_add_fusion.3.refs_0_.own_ref
  139.5 3.3 %join_halves.2 = (bf16[256,1536]{1,0:T(8,128)(2,1)}, bf16[256,1536]{1,0:T(8,128)(2,1)}) custom-call(f32[256,1536]{1,0:T(8,128)} %convolution_add_fusion.2.y_ref, f32[256,1536]{1,0:T(8,128)} %convolution_add_fusion.1.x_ref, bf16[128,1536]{1,0:T(8,128)(2,1)} %copy-done.20, bf16[128,1536]{1,0:T(8,128)(2,1)} %copy-done.21, ...), custom_call_target="tpu_custom_call" | custom-call | tf_op jit(solution)/shard_map/join_halves/pallas_call | solution.py:127
  144.6 11.4 %head_terms.1.refs_0_ = bf16[1536,1024]{1,0:T(8,128)(2,1)} custom-call(bf16[768,1536]{1,0:T(8,128)(2,1)} %get-tuple-element.37.x_ref.near_a, bf16[256,1536]{1,0:T(8,128)(2,1)} %stack_halves.1.far_a, bf16[768,1536]{1,0:T(8,128)(2,1)} %collective-permute-done.27.near_b, bf16[256,1536]{1,0:T(8,128)(2,1)} %collective-permute-done.28.far_b, ...), custom_call_target="tpu_custom_call" | custom-call | flops 12999999488 | bytes 40000000 | tf_op jit(solution)/shard_map/head_terms/pallas_call | solution.py:449
  156.1 5.9 %collective-permute-done.25.x_ref = bf16[256,1536]{1,0:T(8,128)(2,1)S(1)} collective-permute-done((bf16[256,1536]{1,0:T(8,128)(2,1)}, bf16[256,1536]{1,0:T(8,128)(2,1)S(1)}, u32[]{:S(2)}, u32[]{:S(2)}) %collective-permute-start.25) | collective-permute-done | bytes 786464 | tf_op jit(solution)/shard_map/ppermute | solution.py:14
  163.8 3.0 %finish_sum.2.dmixed_ref = bf16[256,1536]{1,0:T(8,128)(2,1)} custom-call(f32[256,1536]{1,0:T(8,128)} %convolution_add_fusion.3.refs_0_.own_ref, bf16[256,1536]{1,0:T(8,128)(2,1)} %copy-done.14, bf16[256,1536]{1,0:T(8,128)(2,1)} %copy-done.15, bf16[1536,1024]{1,0:T(8,128)(2,1)} %head_terms.1.refs_0_), custom_call_target="tpu_custom_call" | custom-call | tf_op jit(solution)/shard_map/finish_sum/pallas_call | solution.py:173
  166.7 2.5 collective-permute-done.30
  169.2 2.5 fusion.30
  174.3 12.1 %gate_back.1 = (bf16[256,1536]{1,0:T(8,128)(2,1)}, f32[32,1536]{1,0:T(8,128)}) custom-call(bf16[256,1536]{1,0:T(8,128)(2,1)} %finish_sum.2.dmixed_ref, bf16[1536,1536]{1,0:T(8,128)(2,1)} %get-tuple-element.47.pw_ref, f32[256,1536]{1,0:T(8,128)} %get-tuple-element.48.conv_ref, bf16[16,1536]{1,0:T(8,128)(2,1)} %copy-done.27, bf16[256,1536]{1,0:T(8,128)(2,1)} %bitcast.60, ...), custom_call_target="tpu_custom_call" | custom-call | flops 6000000000 | bytes 44000000 | tf_op jit(solution)/shard_map/gate_back/pallas_call | solution.py:406
  187.2 3.1 %join_halves.3 = (bf16[192,1536]{1,0:T(8,128)(2,1)}, bf16[192,1536]{1,0:T(8,128)(2,1)}, bf16[16,1536]{1,0:T(8,128)(2,1)}, bf16[16,1536]{1,0:T(8,128)(2,1)}, f32[32,1536]{1,0:T(8,128)}) custom-call(f32[768,1536]{1,0:T(8,128)} %copy-done, f32[768,1536]{1,0:T(8,128)} %copy-done, bf16[96,1536]{1,0:T(8,128)(2,1)} %copy-done.25, bf16[96,1536]{1,0:T(8,128)(2,1)} %copy-done.26, ...), custom_call_target="tpu_custom_call" | custom-call | tf_op jit(solution)/shard_map/join_halves/pallas_call | solution.py:127
  191.4 3.6 %collective-permute-start.33 = (bf16[16,1536]{1,0:T(8,128)(2,1)}, bf16[16,1536]{1,0:T(8,128)(2,1)S(1)}, u32[]{:S(2)}, u32[]{:S(2)}) collective-permute-start(bf16[16,1536]{1,0:T(8,128)(2,1)} %get-tuple-element.51), channel_id=1, source_target_pairs={{0,8},{8,16},{16,24},{1,9},{9,17},{17,25},{2,10},{10,18},{18,26},{... | collective-permute-start | bytes 147464 | tf_op jit(solution)/shard_map/ppermute | solution.py:283
  199.5 2.7 %collective-permute-start.38 = (f32[16,1536]{1,0:T(8,128)S(1)}, f32[16,1536]{1,0:T(8,128)S(1)}, u32[]{:S(2)}, u32[]{:S(2)}) collective-permute-start(f32[16,1536]{1,0:T(8,128)S(1)} %select_add_fusion), channel_id=1, source_target_pairs={{0,8},{8,0},{16,24},{24,16},{1,9},{9,1},{17,25},{25,17},{2,10},{10... | collective-permute-start | bytes 294920 | tf_op jit(solution)/shard_map/ppermute | solution.py:690
  204.9 8.7 %convolve_back.1.refs_1_ = bf16[256,1536]{1,0:T(8,128)(2,1)} custom-call(bf16[16,1536]{1,0:T(8,128)(2,1)} %copy-done.29, bf16[256,1536]{1,0:T(8,128)(2,1)} %get-tuple-element.49.refs_0_.refs_1_.mid_ref, bf16[16,1536]{1,0:T(8,128)(2,1)} %copy-done.30, f32[31,1536]{1,0:T(8,128)} %taps_ref.3, bf16[256,1536]{1,0:T(8,128)(2,1)} %finish_sum.2.dmixed_ref), custom_call_target="tpu_custom_call" | custom-call | tf_op jit(solution)/shard_map/convolve_back/pallas_call | solution.py:368
  213.6 4.6 %collective-permute-done.39 = f32[16,1536]{1,0:T(8,128)S(1)} collective-permute-done((f32[16,1536]{1,0:T(8,128)S(1)}, f32[16,1536]{1,0:T(8,128)S(1)}, u32[]{:S(2)}, u32[]{:S(2)}) %collective-permute-start.39) | collective-permute-done | bytes 98336 | tf_op jit(solution)/shard_map/ppermute | solution.py:690
  220.9 2.8 %finish_sum.3 = (f32[192,1536]{1,0:T(8,128)}, f32[16,1536]{1,0:T(8,128)}) custom-call(f32[768,1536]{1,0:T(8,128)} %copy-done, bf16[192,1536]{1,0:T(8,128)(2,1)} %copy-done.18, bf16[192,1536]{1,0:T(8,128)(2,1)} %copy-done.19, f32[16,1536]{1,0:T(8,128)} %add_add_fusion.refs_0_, bf16[256,1536]{1,0:T(8,128)(2,1)} %convolve_back.1.refs_1_), custom_call_target="tpu_custom_call" | custom-call | tf_op jit(solution)/shard_map/finish_sum/pallas_call | solution.py:173
  226.1 6.6 %collective-permute-start.44 = (bf16[48,1536]{1,0:T(8,128)(2,1)S(1)}, bf16[48,1536]{1,0:T(8,128)(2,1)S(1)}, u32[]{:S(2)}, u32[]{:S(2)}) collective-permute-start(bf16[48,1536]{1,0:T(8,128)(2,1)S(1)} %get-tuple-element.64), channel_id=1, source_target_pairs={{0,8},{8,0},{16,24},{24,16},{1,9},{9,1},{17,25},{25,17},{2,10},{10... | collective-permute-start | bytes 442376 | tf_op jit(solution)/shard_map/ppermute | solution.py:720
  237.5 3.3 %collective-permute-done.42 = f32[16,1536]{1,0:T(8,128)S(1)} collective-permute-done((f32[16,1536]{1,0:T(8,128)S(1)}, f32[16,1536]{1,0:T(8,128)S(1)}, u32[]{:S(2)}, u32[]{:S(2)}) %collective-permute-start.42) | collective-permute-done | bytes 98336 | tf_op jit(solution)/shard_map/ppermute | solution.py:14
  240.9 5.1 %collective-permute-done.45 = bf16[48,1536]{1,0:T(8,128)(2,1)S(1)} collective-permute-done((bf16[48,1536]{1,0:T(8,128)(2,1)S(1)}, bf16[48,1536]{1,0:T(8,128)(2,1)S(1)}, u32[]{:S(2)}, u32[]{:S(2)}) %collective-permute-start.45) | collective-permute-done | bytes 147488 | tf_op jit(solution)/shard_map/ppermute | solution.py:720
  248.5 2.5 convert_element_type.54
  (200 shorter events, 75.2 us)
Async XLA Ops:
  7.2 241.3 %reduce-scatter.2.cloned.1.call-start = ((), (), s32[]{:S(2)}) async-start(), calls=%async_computation.1 | async-start | bytes 3932160 | tf_op jit(solution)/shard_map/reduce_scatter | solution.py:670
  7.2 78.7 %collective-permute-start.14 = (bf16[1536,1024]{1,0:T(8,128)(2,1)}, bf16[1536,1024]{1,0:T(8,128)(2,1)S(1)}, u32[]{:S(2)}, u32[]{:S(2)}) collective-permute-start(bf16[1536,1024]{1,0:T(8,128)(2,1)} %a_ref.1), channel_id=1, source_target_pairs={{0,1},{1,0},{2,3},{3,2},{4,5},{5,4},{6,7},{7,6},{8,9},{9,8},{10,11... | collective-permute-start | bytes 9437192 | tf_op jit(solution)/shard_map/ppermute | solution.py:14
  7.7 27.8 %collective-permute-start.4 = (bf16[192,1536]{1,0:T(8,128)(2,1)}, bf16[192,1536]{1,0:T(8,128)(2,1)S(1)}, u32[]{:S(2)}, u32[]{:S(2)}) collective-permute-start(bf16[192,1536]{1,0:T(8,128)(2,1)} %refs_3_.1), channel_id=1, source_target_pairs={{0,2},{1,3},{2,0},{3,1},{4,6},{5,7},{6,4},{7,5},{8,10},{9,11},{10,... | collective-permute-start | bytes 1769480 | tf_op jit(solution)/shard_map/ppermute | solution.py:14
  10.3 25.3 %collective-permute-start.6 = (bf16[192,1536]{1,0:T(8,128)(2,1)}, bf16[192,1536]{1,0:T(8,128)(2,1)S(1)}, u32[]{:S(2)}, u32[]{:S(2)}) collective-permute-start(bf16[192,1536]{1,0:T(8,128)(2,1)} %refs_3_.1), channel_id=1, source_target_pairs={{0,4},{1,5},{2,6},{3,7},{4,0},{5,1},{6,2},{7,3},{8,12},{9,13},{10,... | collective-permute-start | bytes 1769480 | tf_op jit(solution)/shard_map/ppermute | solution.py:14
  11.8 27.7 %collective-permute-start.3 = (bf16[192,1536]{1,0:T(8,128)(2,1)}, bf16[192,1536]{1,0:T(8,128)(2,1)}, u32[]{:S(2)}, u32[]{:S(2)}) collective-permute-start(bf16[192,1536]{1,0:T(8,128)(2,1)} %refs_3_.1), channel_id=1, source_target_pairs={{0,1},{1,0},{2,3},{3,2},{4,5},{5,4},{6,7},{7,6},{8,9},{9,8},{10,11... | collective-permute-start | bytes 1769480 | tf_op jit(solution)/shard_map/ppermute | solution.py:14
  39.5 9.5 %collective-permute-start.5 = (bf16[192,1536]{1,0:T(8,128)(2,1)}, bf16[192,1536]{1,0:T(8,128)(2,1)}, u32[]{:S(2)}, u32[]{:S(2)}) collective-permute-start(bf16[192,1536]{1,0:T(8,128)(2,1)} %copy-done.7), channel_id=1, source_target_pairs={{0,1},{1,0},{2,3},{3,2},{4,5},{5,4},{6,7},{7,6},{8,9},{9,8},{10,11... | collective-permute-start | bytes 1769480 | tf_op jit(solution)/shard_map/ppermute | solution.py:14
  56.5 19.9 %collective-permute-start.12 = (bf16[256,1536]{1,0:T(8,128)(2,1)}, bf16[256,1536]{1,0:T(8,128)(2,1)S(1)}, u32[]{:S(2)}, u32[]{:S(2)}) collective-permute-start(bf16[256,1536]{1,0:T(8,128)(2,1)} %get-tuple-element.36.own_ref), channel_id=1, source_target_pairs={{0,2},{1,3},{2,0},{3,1},{4,6},{5,7},{6,4},{7,5},{8,10},{9,11},{10,... | collective-permute-start | bytes 2359304 | tf_op jit(solution)/shard_map/ppermute | solution.py:14
  58.0 19.5 %collective-permute-start.13 = (bf16[256,1536]{1,0:T(8,128)(2,1)}, bf16[256,1536]{1,0:T(8,128)(2,1)S(1)}, u32[]{:S(2)}, u32[]{:S(2)}) collective-permute-start(bf16[256,1536]{1,0:T(8,128)(2,1)} %get-tuple-element.36.own_ref), channel_id=1, source_target_pairs={{0,4},{1,5},{2,6},{3,7},{4,0},{5,1},{6,2},{7,3},{8,12},{9,13},{10,... | collective-permute-start | bytes 2359304 | tf_op jit(solution)/shard_map/ppermute | solution.py:14
  81.8 17.5 %collective-permute-start.15 = (bf16[128,1536]{1,0:T(8,128)(2,1)}, bf16[128,1536]{1,0:T(8,128)(2,1)}, u32[]{:S(2)}, u32[]{:S(2)}) collective-permute-start(bf16[128,1536]{1,0:T(8,128)(2,1)} %get-tuple-element.40), channel_id=1, source_target_pairs={{0,4},{1,5},{2,6},{3,7},{4,0},{5,1},{6,2},{7,3},{8,12},{9,13},{10,... | collective-permute-start | bytes 1179656 | tf_op jit(solution)/shard_map/ppermute | solution.py:14
  82.3 17.0 %collective-permute-start.16 = (bf16[128,1536]{1,0:T(8,128)(2,1)}, bf16[128,1536]{1,0:T(8,128)(2,1)}, u32[]{:S(2)}, u32[]{:S(2)}) collective-permute-start(bf16[128,1536]{1,0:T(8,128)(2,1)} %get-tuple-element.41), channel_id=1, source_target_pairs={{0,2},{1,3},{2,0},{3,1},{4,6},{5,7},{6,4},{7,5},{8,10},{9,11},{10,... | collective-permute-start | bytes 1179656 | tf_op jit(solution)/shard_map/ppermute | solution.py:14
  83.5 26.4 %collective-permute-start.20 = (f32[2,256]{1,0:T(2,128)S(1)}, f32[2,256]{1,0:T(2,128)}, u32[]{:S(2)}, u32[]{:S(2)}) collective-permute-start(f32[2,256]{1,0:T(2,128)S(1)} %pad_maximum_fusion.3.refs_13_), channel_id=1, source_target_pairs={{0,2},{1,3},{2,0},{3,1},{4,6},{5,7},{6,4},{7,5},{8,10},{9,11},{10,... | collective-permute-start | bytes 6152 | tf_op jit(solution)/shard_map/ppermute | solution.py:14
  84.4 27.8 %collective-permute-start.21 = (f32[2,256]{1,0:T(2,128)S(1)}, f32[2,256]{1,0:T(2,128)}, u32[]{:S(2)}, u32[]{:S(2)}) collective-permute-start(f32[2,256]{1,0:T(2,128)S(1)} %pad_maximum_fusion.3.refs_13_), channel_id=1, source_target_pairs={{0,4},{1,5},{2,6},{3,7},{4,0},{5,1},{6,2},{7,3},{8,12},{9,13},{10,... | collective-permute-start | bytes 6152 | tf_op jit(solution)/shard_map/ppermute | solution.py:14
  85.9 26.3 %collective-permute-start.22 = (f32[2,256]{1,0:T(2,128)S(1)}, f32[2,256]{1,0:T(2,128)}, u32[]{:S(2)}, u32[]{:S(2)}) collective-permute-start(f32[2,256]{1,0:T(2,128)S(1)} %pad_maximum_fusion.3.refs_13_), channel_id=1, source_target_pairs={{0,6},{1,7},{2,4},{3,5},{4,2},{5,3},{6,0},{7,1},{8,14},{9,15},{10,... | collective-permute-start | bytes 6152 | tf_op jit(solution)/shard_map/ppermute | solution.py:14
  112.3 32.4 %collective-permute-start.27 = (bf16[768,1536]{1,0:T(8,128)(2,1)S(1)}, bf16[768,1536]{1,0:T(8,128)(2,1)}, u32[]{:S(2)}, u32[]{:S(2)}) collective-permute-start(bf16[768,1536]{1,0:T(8,128)(2,1)S(1)} %copy-done.9), channel_id=1, source_target_pairs={{0,1},{1,0},{2,3},{3,2},{4,5},{5,4},{6,7},{7,6},{8,9},{9,8},{10,11... | collective-permute-start | bytes 7077896 | tf_op jit(solution)/shard_map/ppermute | solution.py:14
  112.3 32.3 %collective-permute-start.28 = (bf16[256,1536]{1,0:T(8,128)(2,1)}, bf16[256,1536]{1,0:T(8,128)(2,1)}, u32[]{:S(2)}, u32[]{:S(2)}) collective-permute-start(bf16[256,1536]{1,0:T(8,128)(2,1)} %stack_halves.1.far_a), channel_id=1, source_target_pairs={{0,1},{1,0},{2,3},{3,2},{4,5},{5,4},{6,7},{7,6},{8,9},{9,8},{10,11... | collective-permute-start | bytes 2359304 | tf_op jit(solution)/shard_map/ppermute | solution.py:14
  122.0 22.7 %collective-permute-start.29 = (bf16[1024,1024]{1,0:T(8,128)(2,1)}, bf16[1024,1024]{1,0:T(8,128)(2,1)}, u32[]{:S(2)}, u32[]{:S(2)}) collective-permute-start(bf16[1024,1024]{1,0:T(8,128)(2,1)} %get-tuple-element.44), channel_id=1, source_target_pairs={{0,1},{1,0},{2,3},{3,2},{4,5},{5,4},{6,7},{7,6},{8,9},{9,8},{10,11... | collective-permute-start | bytes 6291464 | tf_op jit(solution)/shard_map/ppermute | solution.py:14
  125.7 12.3 %collective-permute-start.23 = (bf16[128,1536]{1,0:T(8,128)(2,1)S(1)}, bf16[128,1536]{1,0:T(8,128)(2,1)S(1)}, u32[]{:S(2)}, u32[]{:S(2)}) collective-permute-start(bf16[128,1536]{1,0:T(8,128)(2,1)S(1)} %get-tuple-element.70), channel_id=1, source_target_pairs={{0,2},{1,3},{2,0},{3,1},{4,6},{5,7},{6,4},{7,5},{8,10},{9,11},{10,... | collective-permute-start | bytes 1179656 | tf_op jit(solution)/shard_map/ppermute | solution.py:14
  127.0 11.1 %collective-permute-start.24 = (bf16[128,1536]{1,0:T(8,128)(2,1)S(1)}, bf16[128,1536]{1,0:T(8,128)(2,1)S(1)}, u32[]{:S(2)}, u32[]{:S(2)}) collective-permute-start(bf16[128,1536]{1,0:T(8,128)(2,1)S(1)} %get-tuple-element.69), channel_id=1, source_target_pairs={{0,4},{1,5},{2,6},{3,7},{4,0},{5,1},{6,2},{7,3},{8,12},{9,13},{10,... | collective-permute-start | bytes 1179656 | tf_op jit(solution)/shard_map/ppermute | solution.py:14
  142.9 19.1 %collective-permute-start.25 = (bf16[256,1536]{1,0:T(8,128)(2,1)}, bf16[256,1536]{1,0:T(8,128)(2,1)S(1)}, u32[]{:S(2)}, u32[]{:S(2)}) collective-permute-start(bf16[256,1536]{1,0:T(8,128)(2,1)} %get-tuple-element.45._), channel_id=1, source_target_pairs={{0,2},{1,3},{2,0},{3,1},{4,6},{5,7},{6,4},{7,5},{8,10},{9,11},{10,... | collective-permute-start | bytes 2359304 | tf_op jit(solution)/shard_map/ppermute | solution.py:14
  144.0 18.8 %collective-permute-start.26 = (bf16[256,1536]{1,0:T(8,128)(2,1)}, bf16[256,1536]{1,0:T(8,128)(2,1)S(1)}, u32[]{:S(2)}, u32[]{:S(2)}) collective-permute-start(bf16[256,1536]{1,0:T(8,128)(2,1)} %get-tuple-element.46), channel_id=1, source_target_pairs={{0,4},{1,5},{2,6},{3,7},{4,0},{5,1},{6,2},{7,3},{8,12},{9,13},{10,... | collective-permute-start | bytes 2359304 | tf_op jit(solution)/shard_map/ppermute | solution.py:14
  172.4 14.0 %collective-permute-start.31 = (bf16[96,1536]{1,0:T(8,128)(2,1)S(1)}, bf16[96,1536]{1,0:T(8,128)(2,1)S(1)}, u32[]{:S(2)}, u32[]{:S(2)}) collective-permute-start(bf16[96,1536]{1,0:T(8,128)(2,1)S(1)} %get-tuple-element.63), channel_id=1, source_target_pairs={{0,2},{1,3},{2,0},{3,1},{4,6},{5,7},{6,4},{7,5},{8,10},{9,11},{10,... | collective-permute-start | bytes 884744 | tf_op jit(solution)/shard_map/ppermute | solution.py:14
  173.7 12.8 %collective-permute-start.32 = (bf16[96,1536]{1,0:T(8,128)(2,1)S(1)}, bf16[96,1536]{1,0:T(8,128)(2,1)S(1)}, u32[]{:S(2)}, u32[]{:S(2)}) collective-permute-start(bf16[96,1536]{1,0:T(8,128)(2,1)S(1)} %get-tuple-element.62), channel_id=1, source_target_pairs={{0,4},{1,5},{2,6},{3,7},{4,0},{5,1},{6,2},{7,3},{8,12},{9,13},{10,... | collective-permute-start | bytes 884744 | tf_op jit(solution)/shard_map/ppermute | solution.py:14
  191.4 10.9 %collective-permute-start.33 = (bf16[16,1536]{1,0:T(8,128)(2,1)}, bf16[16,1536]{1,0:T(8,128)(2,1)S(1)}, u32[]{:S(2)}, u32[]{:S(2)}) collective-permute-start(bf16[16,1536]{1,0:T(8,128)(2,1)} %get-tuple-element.51), channel_id=1, source_target_pairs={{0,8},{8,16},{16,24},{1,9},{9,17},{17,25},{2,10},{10,18},{18,26},{... | collective-permute-start | bytes 147464 | tf_op jit(solution)/shard_map/ppermute | solution.py:283
  196.2 23.0 %collective-permute-start.35 = (bf16[192,1536]{1,0:T(8,128)(2,1)}, bf16[192,1536]{1,0:T(8,128)(2,1)S(1)}, u32[]{:S(2)}, u32[]{:S(2)}) collective-permute-start(bf16[192,1536]{1,0:T(8,128)(2,1)} %get-tuple-element.53), channel_id=1, source_target_pairs={{0,2},{1,3},{2,0},{3,1},{4,6},{5,7},{6,4},{7,5},{8,10},{9,11},{10,... | collective-permute-start | bytes 1769480 | tf_op jit(solution)/shard_map/ppermute | solution.py:14
  197.5 21.8 %collective-permute-start.36 = (bf16[192,1536]{1,0:T(8,128)(2,1)}, bf16[192,1536]{1,0:T(8,128)(2,1)S(1)}, u32[]{:S(2)}, u32[]{:S(2)}) collective-permute-start(bf16[192,1536]{1,0:T(8,128)(2,1)} %get-tuple-element.54), channel_id=1, source_target_pairs={{0,4},{1,5},{2,6},{3,7},{4,0},{5,1},{6,2},{7,3},{8,12},{9,13},{10,... | collective-permute-start | bytes 1769480 | tf_op jit(solution)/shard_map/ppermute | solution.py:14
  199.5 14.0 %collective-permute-start.38 = (f32[16,1536]{1,0:T(8,128)S(1)}, f32[16,1536]{1,0:T(8,128)S(1)}, u32[]{:S(2)}, u32[]{:S(2)}) collective-permute-start(f32[16,1536]{1,0:T(8,128)S(1)} %select_add_fusion), channel_id=1, source_target_pairs={{0,8},{8,0},{16,24},{24,16},{1,9},{9,1},{17,25},{25,17},{2,10},{10... | collective-permute-start | bytes 294920 | tf_op jit(solution)/shard_map/ppermute | solution.py:690
  202.3 15.9 %collective-permute-start.39 = (f32[16,1536]{1,0:T(8,128)S(1)}, f32[16,1536]{1,0:T(8,128)S(1)}, u32[]{:S(2)}, u32[]{:S(2)}) collective-permute-start(f32[16,1536]{1,0:T(8,128)S(1)} %select_add_fusion), channel_id=1, source_target_pairs={{0,16},{8,24},{16,0},{24,8},{1,17},{9,25},{17,1},{25,9},{2,18},{10... | collective-permute-start | bytes 294920 | tf_op jit(solution)/shard_map/ppermute | solution.py:690
  204.1 14.5 %collective-permute-start.40 = (f32[16,1536]{1,0:T(8,128)S(1)}, f32[16,1536]{1,0:T(8,128)S(1)}, u32[]{:S(2)}, u32[]{:S(2)}) collective-permute-start(f32[16,1536]{1,0:T(8,128)S(1)} %select_add_fusion), channel_id=1, source_target_pairs={{0,24},{8,16},{16,8},{24,0},{1,25},{9,17},{17,9},{25,1},{2,26},{10... | collective-permute-start | bytes 294920 | tf_op jit(solution)/shard_map/ppermute | solution.py:690
  223.7 11.4 %collective-permute-start.41 = (f32[16,1536]{1,0:T(8,128)}, f32[16,1536]{1,0:T(8,128)S(1)}, u32[]{:S(2)}, u32[]{:S(2)}) collective-permute-start(f32[16,1536]{1,0:T(8,128)} %get-tuple-element.56), channel_id=1, source_target_pairs={{0,2},{1,3},{2,0},{3,1},{4,6},{5,7},{6,4},{7,5},{8,10},{9,11},{10,... | collective-permute-start | bytes 294920 | tf_op jit(solution)/shard_map/ppermute | solution.py:14
  226.1 14.7 %collective-permute-start.44 = (bf16[48,1536]{1,0:T(8,128)(2,1)S(1)}, bf16[48,1536]{1,0:T(8,128)(2,1)S(1)}, u32[]{:S(2)}, u32[]{:S(2)}) collective-permute-start(bf16[48,1536]{1,0:T(8,128)(2,1)S(1)} %get-tuple-element.64), channel_id=1, source_target_pairs={{0,8},{8,0},{16,24},{24,16},{1,9},{9,1},{17,25},{25,17},{2,10},{10... | collective-permute-start | bytes 442376 | tf_op jit(solution)/shard_map/ppermute | solution.py:720
  232.7 13.3 %collective-permute-start.45 = (bf16[48,1536]{1,0:T(8,128)(2,1)S(1)}, bf16[48,1536]{1,0:T(8,128)(2,1)S(1)}, u32[]{:S(2)}, u32[]{:S(2)}) collective-permute-start(bf16[48,1536]{1,0:T(8,128)(2,1)S(1)} %get-tuple-element.66), channel_id=1, source_target_pairs={{0,16},{8,24},{16,0},{24,8},{1,17},{9,25},{17,1},{25,9},{2,18},{10... | collective-permute-start | bytes 442376 | tf_op jit(solution)/shard_map/ppermute | solution.py:720
  233.3 12.7 %collective-permute-start.46 = (bf16[48,1536]{1,0:T(8,128)(2,1)S(1)}, bf16[48,1536]{1,0:T(8,128)(2,1)S(1)}, u32[]{:S(2)}, u32[]{:S(2)}) collective-permute-start(bf16[48,1536]{1,0:T(8,128)(2,1)S(1)} %get-tuple-element.65), channel_id=1, source_target_pairs={{0,24},{8,16},{16,8},{24,0},{1,25},{9,17},{17,9},{25,1},{2,26},{10... | collective-permute-start | bytes 442376 | tf_op jit(solution)/shard_map/ppermute | solution.py:720
  (55 other events, 276.8 us)
Sparse Core Ops, SparseCore 0:
  156.2 67.1 reduce-scatter.1

commit v4 on v3

--- a/solution.py
+++ b/solution.py
@@ -292,11 +292,25 @@
     return 256 if width % 256 == 0 else width
 
 
-def fill(pad_ref, low_ref, mid_ref, high_ref):
+def fill(pad_ref, shifted_ref, low_ref, mid_ref, high_ref):
     rows = mid_ref.shape[0]
     pad_ref[:EDGE, :] = low_ref[...].astype(F32)
     pad_ref[EDGE : EDGE + rows, :] = mid_ref[...].astype(F32)
     pad_ref[EDGE + rows :, :] = high_ref[...].astype(F32)
+    for shift in range(8):
+        shifted_ref[shift] = pad_ref[shift : shift + rows + 24, :]
+
+
+def tap_rows(shifted_ref, start, rows, at):
+    shift = start % 8
+    return shifted_ref[shift, start - shift : start - shift + rows, at]
+
+
+def pad_scratch(rows, tile):
+    return [
+        pltpu.VMEM((rows + 2 * EDGE, tile), F32),
+        pltpu.VMEM((8, rows + 24, tile), F32),
+    ]
 
 
 def tap_specs(rows, tile):
@@ -311,15 +325,15 @@
     tile = channel_tile(width)
 
     def kernel(
-        low_ref, mid_ref, high_ref, taps_ref, conv_ref, gated_ref, turned_ref, mark_ref, pad_ref
+        low_ref, mid_ref, high_ref, taps_ref, conv_ref, gated_ref, turned_ref, mark_ref, pad_ref, shifted_ref
     ):
         mark_ref[...] = jnp.zeros_like(mark_ref)
-        fill(pad_ref, low_ref, mid_ref, high_ref)
+        fill(pad_ref, shifted_ref, low_ref, mid_ref, high_ref)
         for lane in range(0, tile, LANES):
             at = slice(lane, lane + LANES)
             conv = jnp.zeros((rows, LANES), F32)
             for k in range(count):
-                conv = conv + taps_ref[k : k + 1, at] * pad_ref[first + k : first + k + rows, at]
+                conv = conv + taps_ref[k : k + 1, at] * tap_rows(shifted_ref, first + k, rows, at)
             conv_ref[:, at] = conv
             gated = conv / (1.0 + jnp.exp(-conv))
             gated_ref[:, at] = gated.astype(BF)
@@ -342,7 +356,7 @@
             pl.BlockSpec((tile, rows), lambda j: (j, 0)),
             pl.BlockSpec((8, LANES), lambda j: (0, 0)),
         ),
-        scratch_shapes=[pltpu.VMEM((rows + 2 * EDGE, tile), F32)],
+        scratch_shapes=pad_scratch(rows, tile),
         compiler_params=pltpu.CompilerParams(vmem_limit_bytes=VMEM_BYTES),
         cost_estimate=CHEAP,
         name="convolve",
@@ -355,13 +369,13 @@
     last = EDGE + (count - 1) // 2
     tile = channel_tile(width)
 
-    def kernel(low_ref, mid_ref, high_ref, taps_ref, dmixed_ref, out_ref, pad_ref):
-        fill(pad_ref, low_ref, mid_ref, high_ref)
+    def kernel(low_ref, mid_ref, high_ref, taps_ref, dmixed_ref, out_ref, pad_ref, shifted_ref):
+        fill(pad_ref, shifted_ref, low_ref, mid_ref, high_ref)
         for lane in range(0, tile, LANES):
             at = slice(lane, lane + LANES)
             back = dmixed_ref[:, at].astype(F32)
             for k in range(count):
-                back = back + taps_ref[k : k + 1, at] * pad_ref[last - k : last - k + rows, at]
+                back = back + taps_ref[k : k + 1, at] * tap_rows(shifted_ref, last - k, rows, at)
             out_ref[:, at] = back.astype(BF)
 
     edge, body_spec = tap_specs(rows, tile)
@@ -371,7 +385,7 @@
         out_shape=jax.ShapeDtypeStruct((rows, width), BF),
         in_specs=[edge, body_spec, edge, pl.BlockSpec((count, tile), lambda j: (0, j)), body_spec],
         out_specs=body_spec,
-        scratch_shapes=[pltpu.VMEM((rows + 2 * EDGE, tile), F32)],
+        scratch_shapes=pad_scratch(rows, tile),
         compiler_params=pltpu.CompilerParams(vmem_limit_bytes=VMEM_BYTES),
         cost_estimate=CHEAP,
         name="convolve_back",
@@ -385,9 +399,10 @@
     held = -(-count // 16) * 16
 
     def kernel(
-        dmixed_ref, pw_ref, conv_ref, low_ref, mid_ref, high_ref, _, dconv_ref, taps_ref, pad_ref
+        dmixed_ref, pw_ref, conv_ref, low_ref, mid_ref, high_ref, _, dconv_ref, taps_ref, pad_ref,
+        shifted_ref,
     ):
-        fill(pad_ref, low_ref, mid_ref, high_ref)
+        fill(pad_ref, shifted_ref, low_ref, mid_ref, high_ref)
         dgated = lax.dot_general(
             dmixed_ref[...], pw_ref[...], (((1,), (1,)), ((), ())), preferred_element_type=F32
         )
@@ -399,7 +414,7 @@
             at = slice(lane, lane + LANES)
             dconv = dconv_ref[:, at].astype(F32)
             for k in range(count):
-                term = dconv * pad_ref[first + k : first + k + rows, at]
+                term = dconv * tap_rows(shifted_ref, first + k, rows, at)
                 taps_ref[k : k + 1, at] = jnp.sum(term, axis=0, keepdims=True)
 
     edge, body_spec = tap_specs(rows, tile)
@@ -420,7 +435,7 @@
             pl.BlockSpec(memory_space=pl.ANY),
         ],
         out_specs=(body_spec, pl.BlockSpec((held, tile), lambda j: (0, j))),
-        scratch_shapes=[pltpu.VMEM((rows + 2 * EDGE, tile), F32)],
+        scratch_shapes=pad_scratch(rows, tile),
         compiler_params=pltpu.CompilerParams(vmem_limit_bytes=VMEM_BYTES),
         cost_estimate=pl.CostEstimate(
             flops=6 * 10**9, bytes_accessed=44 * 10**6, transcendentals=0

time: 259 us -> 253 us (0.977)
  Pallas kernels: 86.9 us -> 80.7 us
    pallas_call x1, Pallas kernels: 10.7 us -> 7.31 us  [convolve(): pl.pallas_call(kernel, grid=(width // tile,), out_shape=(jax.ShapeDtypeSt...]
  transfers between devices with their start and end apart: 48 -> 48, of which waited for: 18 -> 17; matrix products, arithmetic and copies ran while one was open for 13% -> 14% of each run, Pallas kernels for 34% -> 32%
where the time goes in v4:
time: 253 us; the launch traced here: 252 us
  Pallas kernels  80.7 us (32%)
  waiting for transfers between devices  58.6 us (23%)
  starting transfers between devices  51 us (20%)
  matrix products  21.8 us (9%)
  local copies, waits for them, and re-layouts  15.7 us (6%)
  between operations  14.6 us (6%)
  other arithmetic  9.6 us (4%)
    ppermute x37, waiting for transfers between devices, swap(): return lax.ppermute(value, 'fsdp', [(i, i ^ mask) for i in range(count)])  40.2 us
    ppermute x37, starting transfers between devices, swap(): return lax.ppermute(value, 'fsdp', [(i, i ^ mask) for i in range(count)])  28.2 us
    pallas_call x1, Pallas kernels, head_terms(): pl.pallas_call(kernel, grid=(width // tile,), out_shape=jax.ShapeDtypeStr...  11.4 us
    pallas_call x1, Pallas kernels, logits_and_stats(): pl.pallas_call(kernel, grid=(steps,), out_shape=(jax.ShapeDtypeStruct((ro...  10.8 us
    pallas_call x1, Pallas kernels, gate_back(): pl.pallas_call(kernel, grid=(width // tile,), out_shape=(jax.ShapeDtypeSt...  10.6 us
    unnamed x78, local copies, waits for them, and re-layouts  10.1 us
    ppermute x3, starting transfers between devices, body(): lax.ppermute(shard_of(m).astype(BF), 'seq', [(i, i ^ m) for i in range(se...  8.79 us
    dot_general x4, matrix products, back_head(): lax.dot_general(right_own[at], head_weight, rhs, preferred_element_type=F32)  7.73 us
  transfers between devices with their start and end apart: 48, of which 17 were waited for; matrix products, arithmetic and copies ran while one was open for 14% of the time, Pallas kernels for 32%

profile of v4, /device:TPU:0, one launch (start us, length us, event | category | flops | bytes accessed | tf_op | source)
XLA Modules:
  0.0 252.0 jit_solution(9760713210610167548)
XLA Ops:
  7.7 2.6 %collective-permute-start.4 = (bf16[192,1536]{1,0:T(8,128)(2,1)}, bf16[192,1536]{1,0:T(8,128)(2,1)S(1)}, u32[]{:S(2)}, u32[]{:S(2)}) collective-permute-start(bf16[192,1536]{1,0:T(8,128)(2,1)} %refs_3_.1), channel_id=1, source_target_pairs={{0,2},{1,3},{2,0},{3,1},{4,6},{5,7},{6,4},{7,5},{8,10},{9,11},{10,... | collective-permute-start | bytes 1769480 | tf_op jit(solution)/shard_map/ppermute | solution.py:14
  12.6 3.5 %collective-permute-start = (bf16[16,1536]{1,0:T(8,128)(2,1)S(1)}, bf16[16,1536]{1,0:T(8,128)(2,1)S(1)}, u32[]{:S(2)}, u32[]{:S(2)}) collective-permute-start(bf16[16,1536]{1,0:T(8,128)(2,1)S(1)} %get-tuple-element.76), channel_id=1, source_target_pairs={{0,8},{8,16},{16,24},{1,9},{9,17},{17,25},{2,10},{10,18},{18,26},{... | collective-permute-start | bytes 147464 | tf_op jit(solution)/shard_map/ppermute | solution.py:283
  19.1 5.1 %collective-permute-done.1.high_ref = bf16[16,1536]{1,0:T(8,128)(2,1)S(1)} collective-permute-done((bf16[16,1536]{1,0:T(8,128)(2,1)S(1)}, bf16[16,1536]{1,0:T(8,128)(2,1)S(1)}, u32[]{:S(2)}, u32[]{:S(2)}) %collective-permute-start.1) | collective-permute-done | bytes 49184 | tf_op jit(solution)/shard_map/ppermute | solution.py:283
  24.8 7.3 %convolve.1 = (f32[256,1536]{1,0:T(8,128)}, bf16[256,1536]{1,0:T(8,128)(2,1)}, bf16[1536,256]{1,0:T(8,128)(2,1)}, f32[8,128]{1,0:T(8,128)}) custom-call(bf16[16,1536]{1,0:T(8,128)(2,1)} %copy-done.27, bf16[256,1536]{1,0:T(8,128)(2,1)} %bitcast.58, bf16[16,1536]{1,0:T(8,128)(2,1)} %copy-done.28, f32[31,1536]{1,0:T(8,128)} %taps_ref.3), custom_call_target="tpu_custom_call" | custom-call | tf_op jit(solution)/shard_map/convolve/pallas_call | solution.py:343
  37.3 6.0 %collective-permute-done.10.refs_11_ = bf16[96,1536]{1,0:T(8,128)(2,1)S(1)} collective-permute-done((bf16[96,1536]{1,0:T(8,128)(2,1)}, bf16[96,1536]{1,0:T(8,128)(2,1)S(1)}, u32[]{:S(2)}, u32[]{:S(2)}) %collective-permute-start.10) | collective-permute-done | bytes 294944 | tf_op jit(solution)/shard_map/ppermute | solution.py:14
  46.3 6.8 %project.1 = (bf16[256,1536]{1,0:T(8,128)(2,1)}, bf16[1536,1536]{1,0:T(8,128)(2,1)}) custom-call(s32[10]{0:T(128)} %stack.80.refs_0_, bf16[256,1536]{1,0:T(8,128)(2,1)} %get-tuple-element.32.refs_1_, bf16[256,1536]{1,0:T(8,128)(2,1)} %bitcast.59, bf16[192,1536]{1,0:T(8,128)(2,1)} %refs_3_.1, bf16[192,1536]{1,0:T(8,128)(2,1)} %collective-permute-done.3.refs_4_, ...), custom_call_target="tpu_custom_call" | custom-call | flops 1207959552 | bytes 9437184 | tf_op jit(solution)/shard_map/project/pallas_call | solution.py:236
  57.1 15.8 %collective-permute-done.12.x_ref = bf16[256,1536]{1,0:T(8,128)(2,1)S(1)} collective-permute-done((bf16[256,1536]{1,0:T(8,128)(2,1)}, bf16[256,1536]{1,0:T(8,128)(2,1)S(1)}, u32[]{:S(2)}, u32[]{:S(2)}) %collective-permute-start.12) | collective-permute-done | bytes 786464 | tf_op jit(solution)/shard_map/ppermute | solution.py:14
  75.0 3.4 %near_and_forward.1 = (bf16[768,1536]{1,0:T(8,128)(2,1)}, bf16[128,1536]{1,0:T(8,128)(2,1)}, bf16[128,1536]{1,0:T(8,128)(2,1)}) custom-call(bf16[256,1536]{1,0:T(8,128)(2,1)} %get-tuple-element.36.own_ref, bf16[256,1536]{1,0:T(8,128)(2,1)} %copy-done.16, bf16[256,1536]{1,0:T(8,128)(2,1)} %copy-done.17, bf16[4,4,48,256]{3,2,1,0:T(8,128)(2,1)} %copy-done.12), custom_call_target="tpu_custom_call" | custom-call | tf_op jit(solution)/shard_map/near_and_forward/pallas_call | solution.py:64
  84.3 10.8 %logits.1 = (f32[768,1024]{1,0:T(8,128)}, f32[768,1024]{1,0:T(8,128)}, f32[8,768]{1,0:T(8,128)}) custom-call(bf16[768,1536]{1,0:T(8,128)(2,1)} %get-tuple-element.37.x_ref.near_a, bf16[1536,1024]{1,0:T(8,128)(2,1)} %a_ref.1, bf16[1536,1024]{1,0:T(8,128)(2,1)} %copy-done.1), custom_call_target="tpu_custom_call" | custom-call | tf_op jit(solution)/shard_map/logits/pallas_call | solution.py:517
  97.9 3.8 %fusion.28 = (f32[256]{0:T(256)}, f32[256,1024]{1,0:T(8,128)}) fusion(bf16[256,1536]{1,0:T(8,128)(2,1)} %stack_halves.1.far_a, bf16[1536,1024]{1,0:T(8,128)(2,1)S(1)} %copy-done.3), kind=kOutput, calls=%fused_computation.62 | convolution fusion | flops 805568256 | bytes 4981760 | tf_op jit(solution)/shard_map/dot_general | solution.py:653
  101.8 2.3 fusion.29
  111.7 6.9 %dlogits.1 = (bf16[1024,1024]{1,0:T(8,128)(2,1)}, bf16[1024,1024]{1,0:T(8,128)(2,1)}) custom-call(s32[2]{0:T(128)} %pad_add_fusion.refs_0_, f32[768,1024]{1,0:T(8,128)} %get-tuple-element.38.refs_1_.refs_3_.refs_5_, f32[768,1024]{1,0:T(8,128)} %get-tuple-element.39.refs_2_.refs_4_.refs_6_, f32[768,1024]{1,0:T(8,128)} %get-tuple-element.38.refs_1_.refs_3_.refs_5_, ...), custom_call_target="tpu_custom_call" | custom-call | tf_op jit(solution)/shard_map/dlogits/pallas_call | solution.py:586
  118.6 2.2 fusion.8
  127.9 2.3 convolution_add_fusion.1.x_ref
  132.4 2.2 convolution_add_fusion.3.refs_0_.own_ref
  136.1 3.3 %join_halves.2 = (bf16[256,1536]{1,0:T(8,128)(2,1)}, bf16[256,1536]{1,0:T(8,128)(2,1)}) custom-call(f32[256,1536]{1,0:T(8,128)} %convolution_add_fusion.2.y_ref, f32[256,1536]{1,0:T(8,128)} %convolution_add_fusion.1.x_ref, bf16[128,1536]{1,0:T(8,128)(2,1)} %copy-done.20, bf16[128,1536]{1,0:T(8,128)(2,1)} %copy-done.21, ...), custom_call_target="tpu_custom_call" | custom-call | tf_op jit(solution)/shard_map/join_halves/pallas_call | solution.py:127
  141.2 11.4 %head_terms.1.refs_0_ = bf16[1536,1024]{1,0:T(8,128)(2,1)} custom-call(bf16[768,1536]{1,0:T(8,128)(2,1)} %get-tuple-element.37.x_ref.near_a, bf16[256,1536]{1,0:T(8,128)(2,1)} %stack_halves.1.far_a, bf16[768,1536]{1,0:T(8,128)(2,1)} %collective-permute-done.27.near_b, bf16[256,1536]{1,0:T(8,128)(2,1)} %collective-permute-done.28.far_b, ...), custom_call_target="tpu_custom_call" | custom-call | flops 12999999488 | bytes 40000000 | tf_op jit(solution)/shard_map/head_terms/pallas_call | solution.py:464
  152.7 5.8 %collective-permute-done.25.x_ref = bf16[256,1536]{1,0:T(8,128)(2,1)S(1)} collective-permute-done((bf16[256,1536]{1,0:T(8,128)(2,1)}, bf16[256,1536]{1,0:T(8,128)(2,1)S(1)}, u32[]{:S(2)}, u32[]{:S(2)}) %collective-permute-start.25) | collective-permute-done | bytes 786464 | tf_op jit(solution)/shard_map/ppermute | solution.py:14
  160.3 3.0 %finish_sum.2.dmixed_ref = bf16[256,1536]{1,0:T(8,128)(2,1)} custom-call(f32[256,1536]{1,0:T(8,128)} %convolution_add_fusion.3.refs_0_.own_ref, bf16[256,1536]{1,0:T(8,128)(2,1)} %copy-done.14, bf16[256,1536]{1,0:T(8,128)(2,1)} %copy-done.15, bf16[1536,1024]{1,0:T(8,128)(2,1)} %head_terms.1.refs_0_), custom_call_target="tpu_custom_call" | custom-call | tf_op jit(solution)/shard_map/finish_sum/pallas_call | solution.py:173
  163.3 2.5 collective-permute-done.30
  165.8 2.5 %fusion.30 = (bf16[768,1536]{1,0:T(8,128)(2,1)S(1)}, f32[768,1536]{1,0:T(8,128)S(1)}) fusion(bf16[256,1536]{1,0:T(8,128)(2,1)S(1)} %collective-permute-done.30, bf16[256,1536]{1,0:T(8,128)(2,1)} %finish_sum.2.dmixed_ref, bf16[768,256]{1,0:T(8,128)(2,1)S(1)} %bitcast.63, bf16[768,256]{1,0:T(8,128)(2,1)S(1)} %bitcast.62), kind=kOutput, calls=%fused_computation.64 | convolution fusion | flops 1213857792 | bytes 9437184 | tf_op jit(solution)/shard_map/dot_general | solution.py:688
  170.9 10.6 %gate_back.1 = (bf16[256,1536]{1,0:T(8,128)(2,1)}, f32[32,1536]{1,0:T(8,128)}) custom-call(bf16[256,1536]{1,0:T(8,128)(2,1)} %finish_sum.2.dmixed_ref, bf16[1536,1536]{1,0:T(8,128)(2,1)} %get-tuple-element.47.pw_ref, f32[256,1536]{1,0:T(8,128)} %get-tuple-element.48.conv_ref, bf16[16,1536]{1,0:T(8,128)(2,1)} %copy-done.27, bf16[256,1536]{1,0:T(8,128)(2,1)} %bitcast.60, ...), custom_call_target="tpu_custom_call" | custom-call | flops 6000000000 | bytes 44000000 | tf_op jit(solution)/shard_map/gate_back/pallas_call | solution.py:421
  182.3 3.0 %join_halves.3 = (bf16[192,1536]{1,0:T(8,128)(2,1)}, bf16[192,1536]{1,0:T(8,128)(2,1)}, bf16[16,1536]{1,0:T(8,128)(2,1)}, bf16[16,1536]{1,0:T(8,128)(2,1)}, f32[32,1536]{1,0:T(8,128)}) custom-call(f32[768,1536]{1,0:T(8,128)} %copy-done, f32[768,1536]{1,0:T(8,128)} %copy-done, bf16[96,1536]{1,0:T(8,128)(2,1)} %copy-done.25, bf16[96,1536]{1,0:T(8,128)(2,1)} %copy-done.26, ...), custom_call_target="tpu_custom_call" | custom-call | tf_op jit(solution)/shard_map/join_halves/pallas_call | solution.py:127
  186.4 3.7 %collective-permute-start.33 = (bf16[16,1536]{1,0:T(8,128)(2,1)}, bf16[16,1536]{1,0:T(8,128)(2,1)S(1)}, u32[]{:S(2)}, u32[]{:S(2)}) collective-permute-start(bf16[16,1536]{1,0:T(8,128)(2,1)} %get-tuple-element.51), channel_id=1, source_target_pairs={{0,8},{8,16},{16,24},{1,9},{9,17},{17,25},{2,10},{10,18},{18,26},{... | collective-permute-start | bytes 147464 | tf_op jit(solution)/shard_map/ppermute | solution.py:283
  195.0 2.7 %collective-permute-start.38 = (f32[16,1536]{1,0:T(8,128)S(1)}, f32[16,1536]{1,0:T(8,128)S(1)}, u32[]{:S(2)}, u32[]{:S(2)}) collective-permute-start(f32[16,1536]{1,0:T(8,128)S(1)} %select_add_fusion), channel_id=1, source_target_pairs={{0,8},{8,0},{16,24},{24,16},{1,9},{9,1},{17,25},{25,17},{2,10},{10... | collective-permute-start | bytes 294920 | tf_op jit(solution)/shard_map/ppermute | solution.py:705
  200.4 7.4 %convolve_back.1.refs_1_ = bf16[256,1536]{1,0:T(8,128)(2,1)} custom-call(bf16[16,1536]{1,0:T(8,128)(2,1)} %copy-done.29, bf16[256,1536]{1,0:T(8,128)(2,1)} %get-tuple-element.49.refs_0_.refs_1_.mid_ref, bf16[16,1536]{1,0:T(8,128)(2,1)} %copy-done.30, f32[31,1536]{1,0:T(8,128)} %taps_ref.3, bf16[256,1536]{1,0:T(8,128)(2,1)} %finish_sum.2.dmixed_ref), custom_call_target="tpu_custom_call" | custom-call | tf_op jit(solution)/shard_map/convolve_back/pallas_call | solution.py:382
  207.9 7.1 %collective-permute-done.39 = f32[16,1536]{1,0:T(8,128)S(1)} collective-permute-done((f32[16,1536]{1,0:T(8,128)S(1)}, f32[16,1536]{1,0:T(8,128)S(1)}, u32[]{:S(2)}, u32[]{:S(2)}) %collective-permute-start.39) | collective-permute-done | bytes 98336 | tf_op jit(solution)/shard_map/ppermute | solution.py:705
  217.3 2.8 %finish_sum.3 = (f32[192,1536]{1,0:T(8,128)}, f32[16,1536]{1,0:T(8,128)}) custom-call(f32[768,1536]{1,0:T(8,128)} %copy-done, bf16[192,1536]{1,0:T(8,128)(2,1)} %copy-done.18, bf16[192,1536]{1,0:T(8,128)(2,1)} %copy-done.19, f32[16,1536]{1,0:T(8,128)} %add_add_fusion.refs_0_, bf16[256,1536]{1,0:T(8,128)(2,1)} %convolve_back.1.refs_1_), custom_call_target="tpu_custom_call" | custom-call | tf_op jit(solution)/shard_map/finish_sum/pallas_call | solution.py:173
  222.4 6.3 %collective-permute-start.44 = (bf16[48,1536]{1,0:T(8,128)(2,1)S(1)}, bf16[48,1536]{1,0:T(8,128)(2,1)S(1)}, u32[]{:S(2)}, u32[]{:S(2)}) collective-permute-start(bf16[48,1536]{1,0:T(8,128)(2,1)S(1)} %get-tuple-element.64), channel_id=1, source_target_pairs={{0,8},{8,0},{16,24},{24,16},{1,9},{9,1},{17,25},{25,17},{2,10},{10... | collective-permute-start | bytes 442376 | tf_op jit(solution)/shard_map/ppermute | solution.py:735
  233.0 3.8 %collective-permute-done.42 = f32[16,1536]{1,0:T(8,128)S(1)} collective-permute-done((f32[16,1536]{1,0:T(8,128)S(1)}, f32[16,1536]{1,0:T(8,128)S(1)}, u32[]{:S(2)}, u32[]{:S(2)}) %collective-permute-start.42) | collective-permute-done | bytes 98336 | tf_op jit(solution)/shard_map/ppermute | solution.py:14
  236.9 3.4 %collective-permute-done.45 = bf16[48,1536]{1,0:T(8,128)(2,1)S(1)} collective-permute-done((bf16[48,1536]{1,0:T(8,128)(2,1)S(1)}, bf16[48,1536]{1,0:T(8,128)(2,1)S(1)}, u32[]{:S(2)}, u32[]{:S(2)}) %collective-permute-start.45) | collective-permute-done | bytes 147488 | tf_op jit(solution)/shard_map/ppermute | solution.py:735
  242.7 2.5 convert_element_type.54
  (200 shorter events, 74.6 us)
Async XLA Ops:
  7.2 235.6 %reduce-scatter.2.cloned.1.call-start = ((), (), s32[]{:S(2)}) async-start(), calls=%async_computation.1 | async-start | bytes 3932160 | tf_op jit(solution)/shard_map/reduce_scatter | solution.py:685
  7.2 75.3 %collective-permute-start.14 = (bf16[1536,1024]{1,0:T(8,128)(2,1)}, bf16[1536,1024]{1,0:T(8,128)(2,1)S(1)}, u32[]{:S(2)}, u32[]{:S(2)}) collective-permute-start(bf16[1536,1024]{1,0:T(8,128)(2,1)} %a_ref.1), channel_id=1, source_target_pairs={{0,1},{1,0},{2,3},{3,2},{4,5},{5,4},{6,7},{7,6},{8,9},{9,8},{10,11... | collective-permute-start | bytes 9437192 | tf_op jit(solution)/shard_map/ppermute | solution.py:14
  7.7 24.4 %collective-permute-start.4 = (bf16[192,1536]{1,0:T(8,128)(2,1)}, bf16[192,1536]{1,0:T(8,128)(2,1)S(1)}, u32[]{:S(2)}, u32[]{:S(2)}) collective-permute-start(bf16[192,1536]{1,0:T(8,128)(2,1)} %refs_3_.1), channel_id=1, source_target_pairs={{0,2},{1,3},{2,0},{3,1},{4,6},{5,7},{6,4},{7,5},{8,10},{9,11},{10,... | collective-permute-start | bytes 1769480 | tf_op jit(solution)/shard_map/ppermute | solution.py:14
  10.3 21.9 %collective-permute-start.6 = (bf16[192,1536]{1,0:T(8,128)(2,1)}, bf16[192,1536]{1,0:T(8,128)(2,1)S(1)}, u32[]{:S(2)}, u32[]{:S(2)}) collective-permute-start(bf16[192,1536]{1,0:T(8,128)(2,1)} %refs_3_.1), channel_id=1, source_target_pairs={{0,4},{1,5},{2,6},{3,7},{4,0},{5,1},{6,2},{7,3},{8,12},{9,13},{10,... | collective-permute-start | bytes 1769480 | tf_op jit(solution)/shard_map/ppermute | solution.py:14
  11.8 24.3 %collective-permute-start.3 = (bf16[192,1536]{1,0:T(8,128)(2,1)}, bf16[192,1536]{1,0:T(8,128)(2,1)}, u32[]{:S(2)}, u32[]{:S(2)}) collective-permute-start(bf16[192,1536]{1,0:T(8,128)(2,1)} %refs_3_.1), channel_id=1, source_target_pairs={{0,1},{1,0},{2,3},{3,2},{4,5},{5,4},{6,7},{7,6},{8,9},{9,8},{10,11... | collective-permute-start | bytes 1769480 | tf_op jit(solution)/shard_map/ppermute | solution.py:14
  53.1 19.9 %collective-permute-start.12 = (bf16[256,1536]{1,0:T(8,128)(2,1)}, bf16[256,1536]{1,0:T(8,128)(2,1)S(1)}, u32[]{:S(2)}, u32[]{:S(2)}) collective-permute-start(bf16[256,1536]{1,0:T(8,128)(2,1)} %get-tuple-element.36.own_ref), channel_id=1, source_target_pairs={{0,2},{1,3},{2,0},{3,1},{4,6},{5,7},{6,4},{7,5},{8,10},{9,11},{10,... | collective-permute-start | bytes 2359304 | tf_op jit(solution)/shard_map/ppermute | solution.py:14
  54.6 19.5 %collective-permute-start.13 = (bf16[256,1536]{1,0:T(8,128)(2,1)}, bf16[256,1536]{1,0:T(8,128)(2,1)S(1)}, u32[]{:S(2)}, u32[]{:S(2)}) collective-permute-start(bf16[256,1536]{1,0:T(8,128)(2,1)} %get-tuple-element.36.own_ref), channel_id=1, source_target_pairs={{0,4},{1,5},{2,6},{3,7},{4,0},{5,1},{6,2},{7,3},{8,12},{9,13},{10,... | collective-permute-start | bytes 2359304 | tf_op jit(solution)/shard_map/ppermute | solution.py:14
  78.4 17.5 %collective-permute-start.15 = (bf16[128,1536]{1,0:T(8,128)(2,1)}, bf16[128,1536]{1,0:T(8,128)(2,1)}, u32[]{:S(2)}, u32[]{:S(2)}) collective-permute-start(bf16[128,1536]{1,0:T(8,128)(2,1)} %get-tuple-element.40), channel_id=1, source_target_pairs={{0,4},{1,5},{2,6},{3,7},{4,0},{5,1},{6,2},{7,3},{8,12},{9,13},{10,... | collective-permute-start | bytes 1179656 | tf_op jit(solution)/shard_map/ppermute | solution.py:14
  78.9 17.0 %collective-permute-start.16 = (bf16[128,1536]{1,0:T(8,128)(2,1)}, bf16[128,1536]{1,0:T(8,128)(2,1)}, u32[]{:S(2)}, u32[]{:S(2)}) collective-permute-start(bf16[128,1536]{1,0:T(8,128)(2,1)} %get-tuple-element.41), channel_id=1, source_target_pairs={{0,2},{1,3},{2,0},{3,1},{4,6},{5,7},{6,4},{7,5},{8,10},{9,11},{10,... | collective-permute-start | bytes 1179656 | tf_op jit(solution)/shard_map/ppermute | solution.py:14
  80.1 26.4 %collective-permute-start.20 = (f32[2,256]{1,0:T(2,128)S(1)}, f32[2,256]{1,0:T(2,128)}, u32[]{:S(2)}, u32[]{:S(2)}) collective-permute-start(f32[2,256]{1,0:T(2,128)S(1)} %pad_maximum_fusion.3.refs_13_), channel_id=1, source_target_pairs={{0,2},{1,3},{2,0},{3,1},{4,6},{5,7},{6,4},{7,5},{8,10},{9,11},{10,... | collective-permute-start | bytes 6152 | tf_op jit(solution)/shard_map/ppermute | solution.py:14
  81.0 27.8 %collective-permute-start.21 = (f32[2,256]{1,0:T(2,128)S(1)}, f32[2,256]{1,0:T(2,128)}, u32[]{:S(2)}, u32[]{:S(2)}) collective-permute-start(f32[2,256]{1,0:T(2,128)S(1)} %pad_maximum_fusion.3.refs_13_), channel_id=1, source_target_pairs={{0,4},{1,5},{2,6},{3,7},{4,0},{5,1},{6,2},{7,3},{8,12},{9,13},{10,... | collective-permute-start | bytes 6152 | tf_op jit(solution)/shard_map/ppermute | solution.py:14
  82.5 26.3 %collective-permute-start.22 = (f32[2,256]{1,0:T(2,128)S(1)}, f32[2,256]{1,0:T(2,128)}, u32[]{:S(2)}, u32[]{:S(2)}) collective-permute-start(f32[2,256]{1,0:T(2,128)S(1)} %pad_maximum_fusion.3.refs_13_), channel_id=1, source_target_pairs={{0,6},{1,7},{2,4},{3,5},{4,2},{5,3},{6,0},{7,1},{8,14},{9,15},{10,... | collective-permute-start | bytes 6152 | tf_op jit(solution)/shard_map/ppermute | solution.py:14
  108.8 32.4 %collective-permute-start.27 = (bf16[768,1536]{1,0:T(8,128)(2,1)S(1)}, bf16[768,1536]{1,0:T(8,128)(2,1)}, u32[]{:S(2)}, u32[]{:S(2)}) collective-permute-start(bf16[768,1536]{1,0:T(8,128)(2,1)S(1)} %copy-done.9), channel_id=1, source_target_pairs={{0,1},{1,0},{2,3},{3,2},{4,5},{5,4},{6,7},{7,6},{8,9},{9,8},{10,11... | collective-permute-start | bytes 7077896 | tf_op jit(solution)/shard_map/ppermute | solution.py:14
  108.9 32.3 %collective-permute-start.28 = (bf16[256,1536]{1,0:T(8,128)(2,1)}, bf16[256,1536]{1,0:T(8,128)(2,1)}, u32[]{:S(2)}, u32[]{:S(2)}) collective-permute-start(bf16[256,1536]{1,0:T(8,128)(2,1)} %stack_halves.1.far_a), channel_id=1, source_target_pairs={{0,1},{1,0},{2,3},{3,2},{4,5},{5,4},{6,7},{7,6},{8,9},{9,8},{10,11... | collective-permute-start | bytes 2359304 | tf_op jit(solution)/shard_map/ppermute | solution.py:14
  118.5 22.7 %collective-permute-start.29 = (bf16[1024,1024]{1,0:T(8,128)(2,1)}, bf16[1024,1024]{1,0:T(8,128)(2,1)}, u32[]{:S(2)}, u32[]{:S(2)}) collective-permute-start(bf16[1024,1024]{1,0:T(8,128)(2,1)} %get-tuple-element.44), channel_id=1, source_target_pairs={{0,1},{1,0},{2,3},{3,2},{4,5},{5,4},{6,7},{7,6},{8,9},{9,8},{10,11... | collective-permute-start | bytes 6291464 | tf_op jit(solution)/shard_map/ppermute | solution.py:14
  122.3 12.3 %collective-permute-start.23 = (bf16[128,1536]{1,0:T(8,128)(2,1)S(1)}, bf16[128,1536]{1,0:T(8,128)(2,1)S(1)}, u32[]{:S(2)}, u32[]{:S(2)}) collective-permute-start(bf16[128,1536]{1,0:T(8,128)(2,1)S(1)} %get-tuple-element.70), channel_id=1, source_target_pairs={{0,2},{1,3},{2,0},{3,1},{4,6},{5,7},{6,4},{7,5},{8,10},{9,11},{10,... | collective-permute-start | bytes 1179656 | tf_op jit(solution)/shard_map/ppermute | solution.py:14
  123.6 11.1 %collective-permute-start.24 = (bf16[128,1536]{1,0:T(8,128)(2,1)S(1)}, bf16[128,1536]{1,0:T(8,128)(2,1)S(1)}, u32[]{:S(2)}, u32[]{:S(2)}) collective-permute-start(bf16[128,1536]{1,0:T(8,128)(2,1)S(1)} %get-tuple-element.69), channel_id=1, source_target_pairs={{0,4},{1,5},{2,6},{3,7},{4,0},{5,1},{6,2},{7,3},{8,12},{9,13},{10,... | collective-permute-start | bytes 1179656 | tf_op jit(solution)/shard_map/ppermute | solution.py:14
  139.4 19.1 %collective-permute-start.25 = (bf16[256,1536]{1,0:T(8,128)(2,1)}, bf16[256,1536]{1,0:T(8,128)(2,1)S(1)}, u32[]{:S(2)}, u32[]{:S(2)}) collective-permute-start(bf16[256,1536]{1,0:T(8,128)(2,1)} %get-tuple-element.45._), channel_id=1, source_target_pairs={{0,2},{1,3},{2,0},{3,1},{4,6},{5,7},{6,4},{7,5},{8,10},{9,11},{10,... | collective-permute-start | bytes 2359304 | tf_op jit(solution)/shard_map/ppermute | solution.py:14
  140.6 18.8 %collective-permute-start.26 = (bf16[256,1536]{1,0:T(8,128)(2,1)}, bf16[256,1536]{1,0:T(8,128)(2,1)S(1)}, u32[]{:S(2)}, u32[]{:S(2)}) collective-permute-start(bf16[256,1536]{1,0:T(8,128)(2,1)} %get-tuple-element.46), channel_id=1, source_target_pairs={{0,4},{1,5},{2,6},{3,7},{4,0},{5,1},{6,2},{7,3},{8,12},{9,13},{10,... | collective-permute-start | bytes 2359304 | tf_op jit(solution)/shard_map/ppermute | solution.py:14
  169.0 12.5 %collective-permute-start.31 = (bf16[96,1536]{1,0:T(8,128)(2,1)S(1)}, bf16[96,1536]{1,0:T(8,128)(2,1)S(1)}, u32[]{:S(2)}, u32[]{:S(2)}) collective-permute-start(bf16[96,1536]{1,0:T(8,128)(2,1)S(1)} %get-tuple-element.63), channel_id=1, source_target_pairs={{0,2},{1,3},{2,0},{3,1},{4,6},{5,7},{6,4},{7,5},{8,10},{9,11},{10,... | collective-permute-start | bytes 884744 | tf_op jit(solution)/shard_map/ppermute | solution.py:14
  170.2 11.3 %collective-permute-start.32 = (bf16[96,1536]{1,0:T(8,128)(2,1)S(1)}, bf16[96,1536]{1,0:T(8,128)(2,1)S(1)}, u32[]{:S(2)}, u32[]{:S(2)}) collective-permute-start(bf16[96,1536]{1,0:T(8,128)(2,1)S(1)} %get-tuple-element.62), channel_id=1, source_target_pairs={{0,4},{1,5},{2,6},{3,7},{4,0},{5,1},{6,2},{7,3},{8,12},{9,13},{10,... | collective-permute-start | bytes 884744 | tf_op jit(solution)/shard_map/ppermute | solution.py:14
  186.4 11.3 %collective-permute-start.33 = (bf16[16,1536]{1,0:T(8,128)(2,1)}, bf16[16,1536]{1,0:T(8,128)(2,1)S(1)}, u32[]{:S(2)}, u32[]{:S(2)}) collective-permute-start(bf16[16,1536]{1,0:T(8,128)(2,1)} %get-tuple-element.51), channel_id=1, source_target_pairs={{0,8},{8,16},{16,24},{1,9},{9,17},{17,25},{2,10},{10,18},{18,26},{... | collective-permute-start | bytes 147464 | tf_op jit(solution)/shard_map/ppermute | solution.py:283
  190.1 9.7 %collective-permute-start.34 = (bf16[16,1536]{1,0:T(8,128)(2,1)}, bf16[16,1536]{1,0:T(8,128)(2,1)S(1)}, u32[]{:S(2)}, u32[]{:S(2)}) collective-permute-start(bf16[16,1536]{1,0:T(8,128)(2,1)} %get-tuple-element.52), channel_id=1, source_target_pairs={{8,0},{16,8},{24,16},{9,1},{17,9},{25,17},{10,2},{18,10},{26,18},{... | collective-permute-start | bytes 147464 | tf_op jit(solution)/shard_map/ppermute | solution.py:283
  191.6 24.0 %collective-permute-start.35 = (bf16[192,1536]{1,0:T(8,128)(2,1)}, bf16[192,1536]{1,0:T(8,128)(2,1)S(1)}, u32[]{:S(2)}, u32[]{:S(2)}) collective-permute-start(bf16[192,1536]{1,0:T(8,128)(2,1)} %get-tuple-element.53), channel_id=1, source_target_pairs={{0,2},{1,3},{2,0},{3,1},{4,6},{5,7},{6,4},{7,5},{8,10},{9,11},{10,... | collective-permute-start | bytes 1769480 | tf_op jit(solution)/shard_map/ppermute | solution.py:14
  192.8 22.8 %collective-permute-start.36 = (bf16[192,1536]{1,0:T(8,128)(2,1)}, bf16[192,1536]{1,0:T(8,128)(2,1)S(1)}, u32[]{:S(2)}, u32[]{:S(2)}) collective-permute-start(bf16[192,1536]{1,0:T(8,128)(2,1)} %get-tuple-element.54), channel_id=1, source_target_pairs={{0,4},{1,5},{2,6},{3,7},{4,0},{5,1},{6,2},{7,3},{8,12},{9,13},{10,... | collective-permute-start | bytes 1769480 | tf_op jit(solution)/shard_map/ppermute | solution.py:14
  195.0 12.9 %collective-permute-start.38 = (f32[16,1536]{1,0:T(8,128)S(1)}, f32[16,1536]{1,0:T(8,128)S(1)}, u32[]{:S(2)}, u32[]{:S(2)}) collective-permute-start(f32[16,1536]{1,0:T(8,128)S(1)} %select_add_fusion), channel_id=1, source_target_pairs={{0,8},{8,0},{16,24},{24,16},{1,9},{9,1},{17,25},{25,17},{2,10},{10... | collective-permute-start | bytes 294920 | tf_op jit(solution)/shard_map/ppermute | solution.py:705
  197.7 17.3 %collective-permute-start.39 = (f32[16,1536]{1,0:T(8,128)S(1)}, f32[16,1536]{1,0:T(8,128)S(1)}, u32[]{:S(2)}, u32[]{:S(2)}) collective-permute-start(f32[16,1536]{1,0:T(8,128)S(1)} %select_add_fusion), channel_id=1, source_target_pairs={{0,16},{8,24},{16,0},{24,8},{1,17},{9,25},{17,1},{25,9},{2,18},{10... | collective-permute-start | bytes 294920 | tf_op jit(solution)/shard_map/ppermute | solution.py:705
  199.8 15.1 %collective-permute-start.40 = (f32[16,1536]{1,0:T(8,128)S(1)}, f32[16,1536]{1,0:T(8,128)S(1)}, u32[]{:S(2)}, u32[]{:S(2)}) collective-permute-start(f32[16,1536]{1,0:T(8,128)S(1)} %select_add_fusion), channel_id=1, source_target_pairs={{0,24},{8,16},{16,8},{24,0},{1,25},{9,17},{17,9},{25,1},{2,26},{10... | collective-permute-start | bytes 294920 | tf_op jit(solution)/shard_map/ppermute | solution.py:705
  220.1 11.1 %collective-permute-start.41 = (f32[16,1536]{1,0:T(8,128)}, f32[16,1536]{1,0:T(8,128)S(1)}, u32[]{:S(2)}, u32[]{:S(2)}) collective-permute-start(f32[16,1536]{1,0:T(8,128)} %get-tuple-element.56), channel_id=1, source_target_pairs={{0,2},{1,3},{2,0},{3,1},{4,6},{5,7},{6,4},{7,5},{8,10},{9,11},{10,... | collective-permute-start | bytes 294920 | tf_op jit(solution)/shard_map/ppermute | solution.py:14
  222.4 14.5 %collective-permute-start.44 = (bf16[48,1536]{1,0:T(8,128)(2,1)S(1)}, bf16[48,1536]{1,0:T(8,128)(2,1)S(1)}, u32[]{:S(2)}, u32[]{:S(2)}) collective-permute-start(bf16[48,1536]{1,0:T(8,128)(2,1)S(1)} %get-tuple-element.64), channel_id=1, source_target_pairs={{0,8},{8,0},{16,24},{24,16},{1,9},{9,1},{17,25},{25,17},{2,10},{10... | collective-permute-start | bytes 442376 | tf_op jit(solution)/shard_map/ppermute | solution.py:735
  228.8 11.5 %collective-permute-start.45 = (bf16[48,1536]{1,0:T(8,128)(2,1)S(1)}, bf16[48,1536]{1,0:T(8,128)(2,1)S(1)}, u32[]{:S(2)}, u32[]{:S(2)}) collective-permute-start(bf16[48,1536]{1,0:T(8,128)(2,1)S(1)} %get-tuple-element.66), channel_id=1, source_target_pairs={{0,16},{8,24},{16,0},{24,8},{1,17},{9,25},{17,1},{25,9},{2,18},{10... | collective-permute-start | bytes 442376 | tf_op jit(solution)/shard_map/ppermute | solution.py:735
  229.7 10.5 %collective-permute-start.46 = (bf16[48,1536]{1,0:T(8,128)(2,1)S(1)}, bf16[48,1536]{1,0:T(8,128)(2,1)S(1)}, u32[]{:S(2)}, u32[]{:S(2)}) collective-permute-start(bf16[48,1536]{1,0:T(8,128)(2,1)S(1)} %get-tuple-element.65), channel_id=1, source_target_pairs={{0,24},{8,16},{16,8},{24,0},{1,25},{9,17},{17,9},{25,1},{2,26},{10... | collective-permute-start | bytes 442376 | tf_op jit(solution)/shard_map/ppermute | solution.py:735
  (55 other events, 274.0 us)
Sparse Core Ops, SparseCore 0:
  152.8 67.1 reduce-scatter.1

commit v5 on v4

--- a/solution.py
+++ b/solution.py
@@ -289,7 +289,7 @@
 
 
 def channel_tile(width):
-    return 256 if width % 256 == 0 else width
+    return 384 if width % 384 == 0 else width
 
 
 def fill(pad_ref, shifted_ref, low_ref, mid_ref, high_ref):

time: 253 us -> 252 us (level)
  transfers between devices with their start and end apart: 48 -> 48, of which waited for: 17 -> 18; matrix products, arithmetic and copies ran while one was open for 14% -> 14% of each run, Pallas kernels for 32% -> 32%
where the time goes in v5:
time: 252 us; the launch traced here: 251 us
  Pallas kernels  79.4 us (32%)
  waiting for transfers between devices  59.4 us (24%)
  starting transfers between devices  50.5 us (20%)
  matrix products  21.8 us (9%)
  local copies, waits for them, and re-layouts  16.1 us (6%)
  between operations  14.6 us (6%)
  other arithmetic  9.6 us (4%)
    ppermute x37, waiting for transfers between devices, swap(): return lax.ppermute(value, 'fsdp', [(i, i ^ mask) for i in range(count)])  40.5 us
    ppermute x37, starting transfers between devices, swap(): return lax.ppermute(value, 'fsdp', [(i, i ^ mask) for i in range(count)])  28.2 us
    pallas_call x1, Pallas kernels, head_terms(): pl.pallas_call(kernel, grid=(width // tile,), out_shape=jax.ShapeDtypeStr...  11.1 us
    pallas_call x1, Pallas kernels, logits_and_stats(): pl.pallas_call(kernel, grid=(steps,), out_shape=(jax.ShapeDtypeStruct((ro...  10.8 us
    pallas_call x1, Pallas kernels, gate_back(): pl.pallas_call(kernel, grid=(width // tile,), out_shape=(jax.ShapeDtypeSt...  10.6 us
    unnamed x78, local copies, waits for them, and re-layouts  10.4 us
    ppermute x3, starting transfers between devices, body(): lax.ppermute(shard_of(m).astype(BF), 'seq', [(i, i ^ m) for i in range(se...  8.82 us
    dot_general x4, matrix products, back_head(): lax.dot_general(right_own[at], head_weight, rhs, preferred_element_type=F32)  7.73 us
  transfers between devices with their start and end apart: 48, of which 18 were waited for; matrix products, arithmetic and copies ran while one was open for 14% of the time, Pallas kernels for 32%

profile of v5, /device:TPU:0, one launch (start us, length us, event | category | flops | bytes accessed | tf_op | source)
XLA Modules:
  0.0 251.4 jit_solution(14195849676568957017)
XLA Ops:
  7.7 2.6 %collective-permute-start.4 = (bf16[192,1536]{1,0:T(8,128)(2,1)}, bf16[192,1536]{1,0:T(8,128)(2,1)S(1)}, u32[]{:S(2)}, u32[]{:S(2)}) collective-permute-start(bf16[192,1536]{1,0:T(8,128)(2,1)} %refs_3_.1), channel_id=1, source_target_pairs={{0,2},{1,3},{2,0},{3,1},{4,6},{5,7},{6,4},{7,5},{8,10},{9,11},{10,... | collective-permute-start | bytes 1769480 | tf_op jit(solution)/shard_map/ppermute | solution.py:14
  12.6 3.5 %collective-permute-start = (bf16[16,1536]{1,0:T(8,128)(2,1)S(1)}, bf16[16,1536]{1,0:T(8,128)(2,1)S(1)}, u32[]{:S(2)}, u32[]{:S(2)}) collective-permute-start(bf16[16,1536]{1,0:T(8,128)(2,1)S(1)} %get-tuple-element.76), channel_id=1, source_target_pairs={{0,8},{8,16},{16,24},{1,9},{9,17},{17,25},{2,10},{10,18},{18,26},{... | collective-permute-start | bytes 147464 | tf_op jit(solution)/shard_map/ppermute | solution.py:283
  19.1 5.1 %collective-permute-done.1.high_ref = bf16[16,1536]{1,0:T(8,128)(2,1)S(1)} collective-permute-done((bf16[16,1536]{1,0:T(8,128)(2,1)S(1)}, bf16[16,1536]{1,0:T(8,128)(2,1)S(1)}, u32[]{:S(2)}, u32[]{:S(2)}) %collective-permute-start.1) | collective-permute-done | bytes 49184 | tf_op jit(solution)/shard_map/ppermute | solution.py:283
  24.8 7.0 %convolve.1 = (f32[256,1536]{1,0:T(8,128)}, bf16[256,1536]{1,0:T(8,128)(2,1)}, bf16[1536,256]{1,0:T(8,128)(2,1)}, f32[8,128]{1,0:T(8,128)}) custom-call(bf16[16,1536]{1,0:T(8,128)(2,1)} %copy-done.27, bf16[256,1536]{1,0:T(8,128)(2,1)} %bitcast.58, bf16[16,1536]{1,0:T(8,128)(2,1)} %copy-done.28, f32[31,1536]{1,0:T(8,128)} %taps_ref.3), custom_call_target="tpu_custom_call" | custom-call | tf_op jit(solution)/shard_map/convolve/pallas_call | solution.py:343
  37.0 6.0 %collective-permute-done.10.refs_11_ = bf16[96,1536]{1,0:T(8,128)(2,1)S(1)} collective-permute-done((bf16[96,1536]{1,0:T(8,128)(2,1)}, bf16[96,1536]{1,0:T(8,128)(2,1)S(1)}, u32[]{:S(2)}, u32[]{:S(2)}) %collective-permute-start.10) | collective-permute-done | bytes 294944 | tf_op jit(solution)/shard_map/ppermute | solution.py:14
  46.0 6.8 %project.1 = (bf16[256,1536]{1,0:T(8,128)(2,1)}, bf16[1536,1536]{1,0:T(8,128)(2,1)}) custom-call(s32[10]{0:T(128)} %stack.80.refs_0_, bf16[256,1536]{1,0:T(8,128)(2,1)} %get-tuple-element.32.refs_1_, bf16[256,1536]{1,0:T(8,128)(2,1)} %bitcast.59, bf16[192,1536]{1,0:T(8,128)(2,1)} %refs_3_.1, bf16[192,1536]{1,0:T(8,128)(2,1)} %collective-permute-done.3.refs_4_, ...), custom_call_target="tpu_custom_call" | custom-call | flops 1207959552 | bytes 9437184 | tf_op jit(solution)/shard_map/project/pallas_call | solution.py:236
  56.9 15.8 %collective-permute-done.12.x_ref = bf16[256,1536]{1,0:T(8,128)(2,1)S(1)} collective-permute-done((bf16[256,1536]{1,0:T(8,128)(2,1)}, bf16[256,1536]{1,0:T(8,128)(2,1)S(1)}, u32[]{:S(2)}, u32[]{:S(2)}) %collective-permute-start.12) | collective-permute-done | bytes 786464 | tf_op jit(solution)/shard_map/ppermute | solution.py:14
  74.7 3.4 %near_and_forward.1 = (bf16[768,1536]{1,0:T(8,128)(2,1)}, bf16[128,1536]{1,0:T(8,128)(2,1)}, bf16[128,1536]{1,0:T(8,128)(2,1)}) custom-call(bf16[256,1536]{1,0:T(8,128)(2,1)} %get-tuple-element.36.own_ref, bf16[256,1536]{1,0:T(8,128)(2,1)} %copy-done.16, bf16[256,1536]{1,0:T(8,128)(2,1)} %copy-done.17, bf16[4,4,48,256]{3,2,1,0:T(8,128)(2,1)} %copy-done.12), custom_call_target="tpu_custom_call" | custom-call | tf_op jit(solution)/shard_map/near_and_forward/pallas_call | solution.py:64
  84.0 10.8 %logits.1 = (f32[768,1024]{1,0:T(8,128)}, f32[768,1024]{1,0:T(8,128)}, f32[8,768]{1,0:T(8,128)}) custom-call(bf16[768,1536]{1,0:T(8,128)(2,1)} %get-tuple-element.37.x_ref.near_a, bf16[1536,1024]{1,0:T(8,128)(2,1)} %a_ref.1, bf16[1536,1024]{1,0:T(8,128)(2,1)} %copy-done.1), custom_call_target="tpu_custom_call" | custom-call | tf_op jit(solution)/shard_map/logits/pallas_call | solution.py:517
  97.7 3.8 %fusion.28 = (f32[256]{0:T(256)}, f32[256,1024]{1,0:T(8,128)}) fusion(bf16[256,1536]{1,0:T(8,128)(2,1)} %stack_halves.1.far_a, bf16[1536,1024]{1,0:T(8,128)(2,1)S(1)} %copy-done.3), kind=kOutput, calls=%fused_computation.62 | convolution fusion | flops 805568256 | bytes 4981760 | tf_op jit(solution)/shard_map/dot_general | solution.py:653
  101.5 2.3 fusion.29
  111.4 6.9 %dlogits.1 = (bf16[1024,1024]{1,0:T(8,128)(2,1)}, bf16[1024,1024]{1,0:T(8,128)(2,1)}) custom-call(s32[2]{0:T(128)} %pad_add_fusion.refs_0_, f32[768,1024]{1,0:T(8,128)} %get-tuple-element.38.refs_1_.refs_3_.refs_5_, f32[768,1024]{1,0:T(8,128)} %get-tuple-element.39.refs_2_.refs_4_.refs_6_, f32[768,1024]{1,0:T(8,128)} %get-tuple-element.38.refs_1_.refs_3_.refs_5_, ...), custom_call_target="tpu_custom_call" | custom-call | tf_op jit(solution)/shard_map/dlogits/pallas_call | solution.py:586
  118.3 2.2 fusion.8
  127.6 2.3 convolution_add_fusion.1.x_ref
  132.1 2.2 convolution_add_fusion.3.refs_0_.own_ref
  135.8 3.3 %join_halves.2 = (bf16[256,1536]{1,0:T(8,128)(2,1)}, bf16[256,1536]{1,0:T(8,128)(2,1)}) custom-call(f32[256,1536]{1,0:T(8,128)} %convolution_add_fusion.2.y_ref, f32[256,1536]{1,0:T(8,128)} %convolution_add_fusion.1.x_ref, bf16[128,1536]{1,0:T(8,128)(2,1)} %copy-done.20, bf16[128,1536]{1,0:T(8,128)(2,1)} %copy-done.21, ...), custom_call_target="tpu_custom_call" | custom-call | tf_op jit(solution)/shard_map/join_halves/pallas_call | solution.py:127
  140.9 11.1 %head_terms.1.refs_0_ = bf16[1536,1024]{1,0:T(8,128)(2,1)} custom-call(bf16[768,1536]{1,0:T(8,128)(2,1)} %get-tuple-element.37.x_ref.near_a, bf16[256,1536]{1,0:T(8,128)(2,1)} %stack_halves.1.far_a, bf16[768,1536]{1,0:T(8,128)(2,1)} %collective-permute-done.27.near_b, bf16[256,1536]{1,0:T(8,128)(2,1)} %collective-permute-done.28.far_b, ...), custom_call_target="tpu_custom_call" | custom-call | flops 12999999488 | bytes 40000000 | tf_op jit(solution)/shard_map/head_terms/pallas_call | solution.py:464
  152.0 6.2 %collective-permute-done.25.x_ref = bf16[256,1536]{1,0:T(8,128)(2,1)S(1)} collective-permute-done((bf16[256,1536]{1,0:T(8,128)(2,1)}, bf16[256,1536]{1,0:T(8,128)(2,1)S(1)}, u32[]{:S(2)}, u32[]{:S(2)}) %collective-permute-start.25) | collective-permute-done | bytes 786464 | tf_op jit(solution)/shard_map/ppermute | solution.py:14
  160.1 3.0 %finish_sum.2.dmixed_ref = bf16[256,1536]{1,0:T(8,128)(2,1)} custom-call(f32[256,1536]{1,0:T(8,128)} %convolution_add_fusion.3.refs_0_.own_ref, bf16[256,1536]{1,0:T(8,128)(2,1)} %copy-done.14, bf16[256,1536]{1,0:T(8,128)(2,1)} %copy-done.15, bf16[1536,1024]{1,0:T(8,128)(2,1)} %head_terms.1.refs_0_), custom_call_target="tpu_custom_call" | custom-call | tf_op jit(solution)/shard_map/finish_sum/pallas_call | solution.py:173
  163.0 2.5 collective-permute-done.30
  165.5 2.5 %fusion.30 = (bf16[768,1536]{1,0:T(8,128)(2,1)S(1)}, f32[768,1536]{1,0:T(8,128)S(1)}) fusion(bf16[256,1536]{1,0:T(8,128)(2,1)S(1)} %collective-permute-done.30, bf16[256,1536]{1,0:T(8,128)(2,1)} %finish_sum.2.dmixed_ref, bf16[768,256]{1,0:T(8,128)(2,1)S(1)} %bitcast.63, bf16[768,256]{1,0:T(8,128)(2,1)S(1)} %bitcast.62), kind=kOutput, calls=%fused_computation.64 | convolution fusion | flops 1213857792 | bytes 9437184 | tf_op jit(solution)/shard_map/dot_general | solution.py:688
  170.6 10.6 %gate_back.1 = (bf16[256,1536]{1,0:T(8,128)(2,1)}, f32[32,1536]{1,0:T(8,128)}) custom-call(bf16[256,1536]{1,0:T(8,128)(2,1)} %finish_sum.2.dmixed_ref, bf16[1536,1536]{1,0:T(8,128)(2,1)} %get-tuple-element.47.pw_ref, f32[256,1536]{1,0:T(8,128)} %get-tuple-element.48.conv_ref, bf16[16,1536]{1,0:T(8,128)(2,1)} %copy-done.27, bf16[256,1536]{1,0:T(8,128)(2,1)} %bitcast.60, ...), custom_call_target="tpu_custom_call" | custom-call | flops 6000000000 | bytes 44000000 | tf_op jit(solution)/shard_map/gate_back/pallas_call | solution.py:421
  181.9 3.0 %join_halves.3 = (bf16[192,1536]{1,0:T(8,128)(2,1)}, bf16[192,1536]{1,0:T(8,128)(2,1)}, bf16[16,1536]{1,0:T(8,128)(2,1)}, bf16[16,1536]{1,0:T(8,128)(2,1)}, f32[32,1536]{1,0:T(8,128)}) custom-call(f32[768,1536]{1,0:T(8,128)} %copy-done, f32[768,1536]{1,0:T(8,128)} %copy-done, bf16[96,1536]{1,0:T(8,128)(2,1)} %copy-done.25, bf16[96,1536]{1,0:T(8,128)(2,1)} %copy-done.26, ...), custom_call_target="tpu_custom_call" | custom-call | tf_op jit(solution)/shard_map/join_halves/pallas_call | solution.py:127
  186.0 3.7 %collective-permute-start.33 = (bf16[16,1536]{1,0:T(8,128)(2,1)}, bf16[16,1536]{1,0:T(8,128)(2,1)S(1)}, u32[]{:S(2)}, u32[]{:S(2)}) collective-permute-start(bf16[16,1536]{1,0:T(8,128)(2,1)} %get-tuple-element.51), channel_id=1, source_target_pairs={{0,8},{8,16},{16,24},{1,9},{9,17},{17,25},{2,10},{10,18},{18,26},{... | collective-permute-start | bytes 147464 | tf_op jit(solution)/shard_map/ppermute | solution.py:283
  194.4 2.7 %collective-permute-start.38 = (f32[16,1536]{1,0:T(8,128)S(1)}, f32[16,1536]{1,0:T(8,128)S(1)}, u32[]{:S(2)}, u32[]{:S(2)}) collective-permute-start(f32[16,1536]{1,0:T(8,128)S(1)} %select_add_fusion), channel_id=1, source_target_pairs={{0,8},{8,0},{16,24},{24,16},{1,9},{9,1},{17,25},{25,17},{2,10},{10... | collective-permute-start | bytes 294920 | tf_op jit(solution)/shard_map/ppermute | solution.py:705
  200.2 6.9 %convolve_back.1.refs_1_ = bf16[256,1536]{1,0:T(8,128)(2,1)} custom-call(bf16[16,1536]{1,0:T(8,128)(2,1)} %copy-done.29, bf16[256,1536]{1,0:T(8,128)(2,1)} %get-tuple-element.49.refs_0_.refs_1_.mid_ref, bf16[16,1536]{1,0:T(8,128)(2,1)} %copy-done.30, f32[31,1536]{1,0:T(8,128)} %taps_ref.3, bf16[256,1536]{1,0:T(8,128)(2,1)} %finish_sum.2.dmixed_ref), custom_call_target="tpu_custom_call" | custom-call | tf_op jit(solution)/shard_map/convolve_back/pallas_call | solution.py:382
  207.2 7.1 %collective-permute-done.39 = f32[16,1536]{1,0:T(8,128)S(1)} collective-permute-done((f32[16,1536]{1,0:T(8,128)S(1)}, f32[16,1536]{1,0:T(8,128)S(1)}, u32[]{:S(2)}, u32[]{:S(2)}) %collective-permute-start.39) | collective-permute-done | bytes 98336 | tf_op jit(solution)/shard_map/ppermute | solution.py:705
  216.7 2.8 %finish_sum.3 = (f32[192,1536]{1,0:T(8,128)}, f32[16,1536]{1,0:T(8,128)}) custom-call(f32[768,1536]{1,0:T(8,128)} %copy-done, bf16[192,1536]{1,0:T(8,128)(2,1)} %copy-done.18, bf16[192,1536]{1,0:T(8,128)(2,1)} %copy-done.19, f32[16,1536]{1,0:T(8,128)} %add_add_fusion.refs_0_, bf16[256,1536]{1,0:T(8,128)(2,1)} %convolve_back.1.refs_1_), custom_call_target="tpu_custom_call" | custom-call | tf_op jit(solution)/shard_map/finish_sum/pallas_call | solution.py:173
  221.8 6.4 %collective-permute-start.44 = (bf16[48,1536]{1,0:T(8,128)(2,1)S(1)}, bf16[48,1536]{1,0:T(8,128)(2,1)S(1)}, u32[]{:S(2)}, u32[]{:S(2)}) collective-permute-start(bf16[48,1536]{1,0:T(8,128)(2,1)S(1)} %get-tuple-element.64), channel_id=1, source_target_pairs={{0,8},{8,0},{16,24},{24,16},{1,9},{9,1},{17,25},{25,17},{2,10},{10... | collective-permute-start | bytes 442376 | tf_op jit(solution)/shard_map/ppermute | solution.py:735
  232.4 3.8 %collective-permute-done.42 = f32[16,1536]{1,0:T(8,128)S(1)} collective-permute-done((f32[16,1536]{1,0:T(8,128)S(1)}, f32[16,1536]{1,0:T(8,128)S(1)}, u32[]{:S(2)}, u32[]{:S(2)}) %collective-permute-start.42) | collective-permute-done | bytes 98336 | tf_op jit(solution)/shard_map/ppermute | solution.py:14
  236.3 3.4 %collective-permute-done.45 = bf16[48,1536]{1,0:T(8,128)(2,1)S(1)} collective-permute-done((bf16[48,1536]{1,0:T(8,128)(2,1)S(1)}, bf16[48,1536]{1,0:T(8,128)(2,1)S(1)}, u32[]{:S(2)}, u32[]{:S(2)}) %collective-permute-start.45) | collective-permute-done | bytes 147488 | tf_op jit(solution)/shard_map/ppermute | solution.py:735
  242.1 2.5 convert_element_type.54
  (200 shorter events, 74.8 us)
Async XLA Ops:
  7.2 235.0 %reduce-scatter.2.cloned.1.call-start = ((), (), s32[]{:S(2)}) async-start(), calls=%async_computation.1 | async-start | bytes 3932160 | tf_op jit(solution)/shard_map/reduce_scatter | solution.py:685
  7.2 75.0 %collective-permute-start.14 = (bf16[1536,1024]{1,0:T(8,128)(2,1)}, bf16[1536,1024]{1,0:T(8,128)(2,1)S(1)}, u32[]{:S(2)}, u32[]{:S(2)}) collective-permute-start(bf16[1536,1024]{1,0:T(8,128)(2,1)} %a_ref.1), channel_id=1, source_target_pairs={{0,1},{1,0},{2,3},{3,2},{4,5},{5,4},{6,7},{7,6},{8,9},{9,8},{10,11... | collective-permute-start | bytes 9437192 | tf_op jit(solution)/shard_map/ppermute | solution.py:14
  7.7 24.1 %collective-permute-start.4 = (bf16[192,1536]{1,0:T(8,128)(2,1)}, bf16[192,1536]{1,0:T(8,128)(2,1)S(1)}, u32[]{:S(2)}, u32[]{:S(2)}) collective-permute-start(bf16[192,1536]{1,0:T(8,128)(2,1)} %refs_3_.1), channel_id=1, source_target_pairs={{0,2},{1,3},{2,0},{3,1},{4,6},{5,7},{6,4},{7,5},{8,10},{9,11},{10,... | collective-permute-start | bytes 1769480 | tf_op jit(solution)/shard_map/ppermute | solution.py:14
  10.3 21.6 %collective-permute-start.6 = (bf16[192,1536]{1,0:T(8,128)(2,1)}, bf16[192,1536]{1,0:T(8,128)(2,1)S(1)}, u32[]{:S(2)}, u32[]{:S(2)}) collective-permute-start(bf16[192,1536]{1,0:T(8,128)(2,1)} %refs_3_.1), channel_id=1, source_target_pairs={{0,4},{1,5},{2,6},{3,7},{4,0},{5,1},{6,2},{7,3},{8,12},{9,13},{10,... | collective-permute-start | bytes 1769480 | tf_op jit(solution)/shard_map/ppermute | solution.py:14
  11.8 24.0 %collective-permute-start.3 = (bf16[192,1536]{1,0:T(8,128)(2,1)}, bf16[192,1536]{1,0:T(8,128)(2,1)}, u32[]{:S(2)}, u32[]{:S(2)}) collective-permute-start(bf16[192,1536]{1,0:T(8,128)(2,1)} %refs_3_.1), channel_id=1, source_target_pairs={{0,1},{1,0},{2,3},{3,2},{4,5},{5,4},{6,7},{7,6},{8,9},{9,8},{10,11... | collective-permute-start | bytes 1769480 | tf_op jit(solution)/shard_map/ppermute | solution.py:14
  52.8 19.9 %collective-permute-start.12 = (bf16[256,1536]{1,0:T(8,128)(2,1)}, bf16[256,1536]{1,0:T(8,128)(2,1)S(1)}, u32[]{:S(2)}, u32[]{:S(2)}) collective-permute-start(bf16[256,1536]{1,0:T(8,128)(2,1)} %get-tuple-element.36.own_ref), channel_id=1, source_target_pairs={{0,2},{1,3},{2,0},{3,1},{4,6},{5,7},{6,4},{7,5},{8,10},{9,11},{10,... | collective-permute-start | bytes 2359304 | tf_op jit(solution)/shard_map/ppermute | solution.py:14
  54.3 19.5 %collective-permute-start.13 = (bf16[256,1536]{1,0:T(8,128)(2,1)}, bf16[256,1536]{1,0:T(8,128)(2,1)S(1)}, u32[]{:S(2)}, u32[]{:S(2)}) collective-permute-start(bf16[256,1536]{1,0:T(8,128)(2,1)} %get-tuple-element.36.own_ref), channel_id=1, source_target_pairs={{0,4},{1,5},{2,6},{3,7},{4,0},{5,1},{6,2},{7,3},{8,12},{9,13},{10,... | collective-permute-start | bytes 2359304 | tf_op jit(solution)/shard_map/ppermute | solution.py:14
  78.1 17.5 %collective-permute-start.15 = (bf16[128,1536]{1,0:T(8,128)(2,1)}, bf16[128,1536]{1,0:T(8,128)(2,1)}, u32[]{:S(2)}, u32[]{:S(2)}) collective-permute-start(bf16[128,1536]{1,0:T(8,128)(2,1)} %get-tuple-element.40), channel_id=1, source_target_pairs={{0,4},{1,5},{2,6},{3,7},{4,0},{5,1},{6,2},{7,3},{8,12},{9,13},{10,... | collective-permute-start | bytes 1179656 | tf_op jit(solution)/shard_map/ppermute | solution.py:14
  78.6 17.0 %collective-permute-start.16 = (bf16[128,1536]{1,0:T(8,128)(2,1)}, bf16[128,1536]{1,0:T(8,128)(2,1)}, u32[]{:S(2)}, u32[]{:S(2)}) collective-permute-start(bf16[128,1536]{1,0:T(8,128)(2,1)} %get-tuple-element.41), channel_id=1, source_target_pairs={{0,2},{1,3},{2,0},{3,1},{4,6},{5,7},{6,4},{7,5},{8,10},{9,11},{10,... | collective-permute-start | bytes 1179656 | tf_op jit(solution)/shard_map/ppermute | solution.py:14
  79.8 26.4 %collective-permute-start.20 = (f32[2,256]{1,0:T(2,128)S(1)}, f32[2,256]{1,0:T(2,128)}, u32[]{:S(2)}, u32[]{:S(2)}) collective-permute-start(f32[2,256]{1,0:T(2,128)S(1)} %pad_maximum_fusion.3.refs_13_), channel_id=1, source_target_pairs={{0,2},{1,3},{2,0},{3,1},{4,6},{5,7},{6,4},{7,5},{8,10},{9,11},{10,... | collective-permute-start | bytes 6152 | tf_op jit(solution)/shard_map/ppermute | solution.py:14
  80.7 27.8 %collective-permute-start.21 = (f32[2,256]{1,0:T(2,128)S(1)}, f32[2,256]{1,0:T(2,128)}, u32[]{:S(2)}, u32[]{:S(2)}) collective-permute-start(f32[2,256]{1,0:T(2,128)S(1)} %pad_maximum_fusion.3.refs_13_), channel_id=1, source_target_pairs={{0,4},{1,5},{2,6},{3,7},{4,0},{5,1},{6,2},{7,3},{8,12},{9,13},{10,... | collective-permute-start | bytes 6152 | tf_op jit(solution)/shard_map/ppermute | solution.py:14
  82.3 26.3 %collective-permute-start.22 = (f32[2,256]{1,0:T(2,128)S(1)}, f32[2,256]{1,0:T(2,128)}, u32[]{:S(2)}, u32[]{:S(2)}) collective-permute-start(f32[2,256]{1,0:T(2,128)S(1)} %pad_maximum_fusion.3.refs_13_), channel_id=1, source_target_pairs={{0,6},{1,7},{2,4},{3,5},{4,2},{5,3},{6,0},{7,1},{8,14},{9,15},{10,... | collective-permute-start | bytes 6152 | tf_op jit(solution)/shard_map/ppermute | solution.py:14
  108.6 32.4 %collective-permute-start.27 = (bf16[768,1536]{1,0:T(8,128)(2,1)S(1)}, bf16[768,1536]{1,0:T(8,128)(2,1)}, u32[]{:S(2)}, u32[]{:S(2)}) collective-permute-start(bf16[768,1536]{1,0:T(8,128)(2,1)S(1)} %copy-done.9), channel_id=1, source_target_pairs={{0,1},{1,0},{2,3},{3,2},{4,5},{5,4},{6,7},{7,6},{8,9},{9,8},{10,11... | collective-permute-start | bytes 7077896 | tf_op jit(solution)/shard_map/ppermute | solution.py:14
  108.6 32.3 %collective-permute-start.28 = (bf16[256,1536]{1,0:T(8,128)(2,1)}, bf16[256,1536]{1,0:T(8,128)(2,1)}, u32[]{:S(2)}, u32[]{:S(2)}) collective-permute-start(bf16[256,1536]{1,0:T(8,128)(2,1)} %stack_halves.1.far_a), channel_id=1, source_target_pairs={{0,1},{1,0},{2,3},{3,2},{4,5},{5,4},{6,7},{7,6},{8,9},{9,8},{10,11... | collective-permute-start | bytes 2359304 | tf_op jit(solution)/shard_map/ppermute | solution.py:14
  118.3 22.7 %collective-permute-start.29 = (bf16[1024,1024]{1,0:T(8,128)(2,1)}, bf16[1024,1024]{1,0:T(8,128)(2,1)}, u32[]{:S(2)}, u32[]{:S(2)}) collective-permute-start(bf16[1024,1024]{1,0:T(8,128)(2,1)} %get-tuple-element.44), channel_id=1, source_target_pairs={{0,1},{1,0},{2,3},{3,2},{4,5},{5,4},{6,7},{7,6},{8,9},{9,8},{10,11... | collective-permute-start | bytes 6291464 | tf_op jit(solution)/shard_map/ppermute | solution.py:14
  122.0 12.3 %collective-permute-start.23 = (bf16[128,1536]{1,0:T(8,128)(2,1)S(1)}, bf16[128,1536]{1,0:T(8,128)(2,1)S(1)}, u32[]{:S(2)}, u32[]{:S(2)}) collective-permute-start(bf16[128,1536]{1,0:T(8,128)(2,1)S(1)} %get-tuple-element.70), channel_id=1, source_target_pairs={{0,2},{1,3},{2,0},{3,1},{4,6},{5,7},{6,4},{7,5},{8,10},{9,11},{10,... | collective-permute-start | bytes 1179656 | tf_op jit(solution)/shard_map/ppermute | solution.py:14
  123.3 11.1 %collective-permute-start.24 = (bf16[128,1536]{1,0:T(8,128)(2,1)S(1)}, bf16[128,1536]{1,0:T(8,128)(2,1)S(1)}, u32[]{:S(2)}, u32[]{:S(2)}) collective-permute-start(bf16[128,1536]{1,0:T(8,128)(2,1)S(1)} %get-tuple-element.69), channel_id=1, source_target_pairs={{0,4},{1,5},{2,6},{3,7},{4,0},{5,1},{6,2},{7,3},{8,12},{9,13},{10,... | collective-permute-start | bytes 1179656 | tf_op jit(solution)/shard_map/ppermute | solution.py:14
  139.2 19.1 %collective-permute-start.25 = (bf16[256,1536]{1,0:T(8,128)(2,1)}, bf16[256,1536]{1,0:T(8,128)(2,1)S(1)}, u32[]{:S(2)}, u32[]{:S(2)}) collective-permute-start(bf16[256,1536]{1,0:T(8,128)(2,1)} %get-tuple-element.45._), channel_id=1, source_target_pairs={{0,2},{1,3},{2,0},{3,1},{4,6},{5,7},{6,4},{7,5},{8,10},{9,11},{10,... | collective-permute-start | bytes 2359304 | tf_op jit(solution)/shard_map/ppermute | solution.py:14
  140.3 18.8 %collective-permute-start.26 = (bf16[256,1536]{1,0:T(8,128)(2,1)}, bf16[256,1536]{1,0:T(8,128)(2,1)S(1)}, u32[]{:S(2)}, u32[]{:S(2)}) collective-permute-start(bf16[256,1536]{1,0:T(8,128)(2,1)} %get-tuple-element.46), channel_id=1, source_target_pairs={{0,4},{1,5},{2,6},{3,7},{4,0},{5,1},{6,2},{7,3},{8,12},{9,13},{10,... | collective-permute-start | bytes 2359304 | tf_op jit(solution)/shard_map/ppermute | solution.py:14
  168.8 12.4 %collective-permute-start.31 = (bf16[96,1536]{1,0:T(8,128)(2,1)S(1)}, bf16[96,1536]{1,0:T(8,128)(2,1)S(1)}, u32[]{:S(2)}, u32[]{:S(2)}) collective-permute-start(bf16[96,1536]{1,0:T(8,128)(2,1)S(1)} %get-tuple-element.63), channel_id=1, source_target_pairs={{0,2},{1,3},{2,0},{3,1},{4,6},{5,7},{6,4},{7,5},{8,10},{9,11},{10,... | collective-permute-start | bytes 884744 | tf_op jit(solution)/shard_map/ppermute | solution.py:14
  170.0 11.2 %collective-permute-start.32 = (bf16[96,1536]{1,0:T(8,128)(2,1)S(1)}, bf16[96,1536]{1,0:T(8,128)(2,1)S(1)}, u32[]{:S(2)}, u32[]{:S(2)}) collective-permute-start(bf16[96,1536]{1,0:T(8,128)(2,1)S(1)} %get-tuple-element.62), channel_id=1, source_target_pairs={{0,4},{1,5},{2,6},{3,7},{4,0},{5,1},{6,2},{7,3},{8,12},{9,13},{10,... | collective-permute-start | bytes 884744 | tf_op jit(solution)/shard_map/ppermute | solution.py:14
  186.0 11.0 %collective-permute-start.33 = (bf16[16,1536]{1,0:T(8,128)(2,1)}, bf16[16,1536]{1,0:T(8,128)(2,1)S(1)}, u32[]{:S(2)}, u32[]{:S(2)}) collective-permute-start(bf16[16,1536]{1,0:T(8,128)(2,1)} %get-tuple-element.51), channel_id=1, source_target_pairs={{0,8},{8,16},{16,24},{1,9},{9,17},{17,25},{2,10},{10,18},{18,26},{... | collective-permute-start | bytes 147464 | tf_op jit(solution)/shard_map/ppermute | solution.py:283
  189.7 9.9 %collective-permute-start.34 = (bf16[16,1536]{1,0:T(8,128)(2,1)}, bf16[16,1536]{1,0:T(8,128)(2,1)S(1)}, u32[]{:S(2)}, u32[]{:S(2)}) collective-permute-start(bf16[16,1536]{1,0:T(8,128)(2,1)} %get-tuple-element.52), channel_id=1, source_target_pairs={{8,0},{16,8},{24,16},{9,1},{17,9},{25,17},{10,2},{18,10},{26,18},{... | collective-permute-start | bytes 147464 | tf_op jit(solution)/shard_map/ppermute | solution.py:283
  191.0 24.0 %collective-permute-start.35 = (bf16[192,1536]{1,0:T(8,128)(2,1)}, bf16[192,1536]{1,0:T(8,128)(2,1)S(1)}, u32[]{:S(2)}, u32[]{:S(2)}) collective-permute-start(bf16[192,1536]{1,0:T(8,128)(2,1)} %get-tuple-element.53), channel_id=1, source_target_pairs={{0,2},{1,3},{2,0},{3,1},{4,6},{5,7},{6,4},{7,5},{8,10},{9,11},{10,... | collective-permute-start | bytes 1769480 | tf_op jit(solution)/shard_map/ppermute | solution.py:14
  192.2 22.8 %collective-permute-start.36 = (bf16[192,1536]{1,0:T(8,128)(2,1)}, bf16[192,1536]{1,0:T(8,128)(2,1)S(1)}, u32[]{:S(2)}, u32[]{:S(2)}) collective-permute-start(bf16[192,1536]{1,0:T(8,128)(2,1)} %get-tuple-element.54), channel_id=1, source_target_pairs={{0,4},{1,5},{2,6},{3,7},{4,0},{5,1},{6,2},{7,3},{8,12},{9,13},{10,... | collective-permute-start | bytes 1769480 | tf_op jit(solution)/shard_map/ppermute | solution.py:14
  194.4 12.9 %collective-permute-start.38 = (f32[16,1536]{1,0:T(8,128)S(1)}, f32[16,1536]{1,0:T(8,128)S(1)}, u32[]{:S(2)}, u32[]{:S(2)}) collective-permute-start(f32[16,1536]{1,0:T(8,128)S(1)} %select_add_fusion), channel_id=1, source_target_pairs={{0,8},{8,0},{16,24},{24,16},{1,9},{9,1},{17,25},{25,17},{2,10},{10... | collective-permute-start | bytes 294920 | tf_op jit(solution)/shard_map/ppermute | solution.py:705
  197.1 17.3 %collective-permute-start.39 = (f32[16,1536]{1,0:T(8,128)S(1)}, f32[16,1536]{1,0:T(8,128)S(1)}, u32[]{:S(2)}, u32[]{:S(2)}) collective-permute-start(f32[16,1536]{1,0:T(8,128)S(1)} %select_add_fusion), channel_id=1, source_target_pairs={{0,16},{8,24},{16,0},{24,8},{1,17},{9,25},{17,1},{25,9},{2,18},{10... | collective-permute-start | bytes 294920 | tf_op jit(solution)/shard_map/ppermute | solution.py:705
  199.6 14.8 %collective-permute-start.40 = (f32[16,1536]{1,0:T(8,128)S(1)}, f32[16,1536]{1,0:T(8,128)S(1)}, u32[]{:S(2)}, u32[]{:S(2)}) collective-permute-start(f32[16,1536]{1,0:T(8,128)S(1)} %select_add_fusion), channel_id=1, source_target_pairs={{0,24},{8,16},{16,8},{24,0},{1,25},{9,17},{17,9},{25,1},{2,26},{10... | collective-permute-start | bytes 294920 | tf_op jit(solution)/shard_map/ppermute | solution.py:705
  219.5 11.1 %collective-permute-start.41 = (f32[16,1536]{1,0:T(8,128)}, f32[16,1536]{1,0:T(8,128)S(1)}, u32[]{:S(2)}, u32[]{:S(2)}) collective-permute-start(f32[16,1536]{1,0:T(8,128)} %get-tuple-element.56), channel_id=1, source_target_pairs={{0,2},{1,3},{2,0},{3,1},{4,6},{5,7},{6,4},{7,5},{8,10},{9,11},{10,... | collective-permute-start | bytes 294920 | tf_op jit(solution)/shard_map/ppermute | solution.py:14
  221.8 14.5 %collective-permute-start.44 = (bf16[48,1536]{1,0:T(8,128)(2,1)S(1)}, bf16[48,1536]{1,0:T(8,128)(2,1)S(1)}, u32[]{:S(2)}, u32[]{:S(2)}) collective-permute-start(bf16[48,1536]{1,0:T(8,128)(2,1)S(1)} %get-tuple-element.64), channel_id=1, source_target_pairs={{0,8},{8,0},{16,24},{24,16},{1,9},{9,1},{17,25},{25,17},{2,10},{10... | collective-permute-start | bytes 442376 | tf_op jit(solution)/shard_map/ppermute | solution.py:735
  228.1 11.5 %collective-permute-start.45 = (bf16[48,1536]{1,0:T(8,128)(2,1)S(1)}, bf16[48,1536]{1,0:T(8,128)(2,1)S(1)}, u32[]{:S(2)}, u32[]{:S(2)}) collective-permute-start(bf16[48,1536]{1,0:T(8,128)(2,1)S(1)} %get-tuple-element.66), channel_id=1, source_target_pairs={{0,16},{8,24},{16,0},{24,8},{1,17},{9,25},{17,1},{25,9},{2,18},{10... | collective-permute-start | bytes 442376 | tf_op jit(solution)/shard_map/ppermute | solution.py:735
  229.1 10.6 %collective-permute-start.46 = (bf16[48,1536]{1,0:T(8,128)(2,1)S(1)}, bf16[48,1536]{1,0:T(8,128)(2,1)S(1)}, u32[]{:S(2)}, u32[]{:S(2)}) collective-permute-start(bf16[48,1536]{1,0:T(8,128)(2,1)S(1)} %get-tuple-element.65), channel_id=1, source_target_pairs={{0,24},{8,16},{16,8},{24,0},{1,25},{9,17},{17,9},{25,1},{2,26},{10... | collective-permute-start | bytes 442376 | tf_op jit(solution)/shard_map/ppermute | solution.py:735
  (55 other events, 274.0 us)
Sparse Core Ops, SparseCore 0:
  152.1 67.1 reduce-scatter.1
